TPU v7x, 256 devices: a whole 4x4x8 slice. The times are simulated.
256 devices in a mesh: grp: 16 (over z_hi, y, core), dev: 16 (over z_lo, x).
Axes of the slice: x: 4, y: 4, z: 8 (z_hi: 2, z_lo: 4; z = z_hi * 4 + z_lo), core: 2. Of those that a mesh axis runs over, the one named last changes fastest.
Arguments:
- tokens: bfloat16 [2048, 4096], P('grp', 'dev'), may hold values from -6 to 6
- norm_gain: float32 [4096], replicated, may hold values from 0.1 to 1.9
- gate_weight: bfloat16 [4096, 6144], P('grp', 'dev'), may hold values from -0.09375 to 0.09375
- up_weight: bfloat16 [4096, 6144], P('grp', 'dev'), may hold values from -0.09375 to 0.09375
- down_weight: bfloat16 [6144, 4096], P('dev', 'grp'), may hold values from -0.078125 to 0.078125
- out_cotangent: bfloat16 [2048, 4096], P('grp', 'dev'), may hold values from -6 to 6
Outputs:
- mixed_out: bfloat16 [2048, 4096], P('grp', 'dev')
- d_tokens: float32 [2048, 4096], P('grp', 'dev')
- grad_gate: float32 [4096, 6144], P('grp', 'dev')
- grad_up: float32 [4096, 6144], P('grp', 'dev')
- grad_down: float32 [6144, 4096], P('dev', 'grp')
All inputs are finite; a program needn't handle non-finite values.
Results may differ from a plain program's by a relative error of at most 0.022.
Values may be sent and summed in bfloat16 or wider, within the bound.
No kernel may reach another device: no remote copies, remote signals or barrier semaphores. Data moves between devices by JAX's collectives and lax.ppermute only.
A program may use at most 64 MiB of HBM per device.

v0:
```python
import functools

import jax
import jax.numpy as jnp
from jax import lax
from jax.experimental import pallas as pl
from jax.experimental.pallas import tpu as pltpu
from jax.sharding import Mesh
from jax.sharding import PartitionSpec as P

norm_epsilon = 1e-06
F32 = jnp.float32
BF16 = jnp.bfloat16
ANY = pl.BlockSpec(memory_space=pl.ANY)
SMEM = pl.BlockSpec(memory_space=pltpu.SMEM)
VMEM = pl.BlockSpec(memory_space=pltpu.VMEM)
MIB = 1 << 20


def dot(left, right, left_dim, right_dim):
    return lax.dot_general(
        left, right, (((left_dim,), (right_dim,)), ((), ())), preferred_element_type=F32
    )


def shift(array, axis, by):
    return lax.ppermute(array, axis, [(i, (i + by) % 4) for i in range(4)])


def swap(array, axis):
    return lax.ppermute(array, axis, [(0, 1), (1, 0)])


def z_pairs(k):
    k1, k2 = k // 2, k % 2
    return [
        (4 * zs + 2 * h + l, 4 * h + 2 * (zs ^ k1) + (l ^ k2))
        for zs in range(2)
        for h in range(2)
        for l in range(2)
    ]


def split_float(value):
    head = value.astype(BF16).astype(F32)
    return head, value - head


def call(body, ids, operands, specs, outs, scratch=(), limit=8):
    return pl.pallas_call(
        body,
        out_shape=[jax.ShapeDtypeStruct(s, d) for s, d in outs],
        in_specs=[SMEM] + specs,
        out_specs=[VMEM] * len(outs),
        scratch_shapes=list(scratch),
        compiler_params=pltpu.CompilerParams(vmem_limit_bytes=limit * MIB),
    )(ids, *operands)


def block_q(ids, t, cc):
    return lax.rem(ids[1] - t + 4, 4) * 2 + (ids[2] ^ cc)


def products_kernel(ids, *refs):
    pieces, weights, gain = refs[:4], refs[4:12], refs[12]
    send, keep, squares, mixed = refs[13:17]
    x_all, w_all, acc, sq, x_sem, w_sem = refs[17:]
    x_copies = [pltpu.make_async_copy(pieces[s], x_all.at[s], x_sem.at[s]) for s in range(4)]
    w_copies = [pltpu.make_async_copy(weights[i], w_all.at[:, i], w_sem.at[i]) for i in range(8)]
    for copy in x_copies + w_copies:
        copy.start()
    for copy in x_copies:
        copy.wait()
    low = ids[3] % 2
    own = (ids[3] // 2) ^ ids[0]
    total = [jnp.zeros((128, 1), F32) for _ in range(2)]
    for i in range(8):
        q = block_q(ids, i % 4, i // 4)
        s = lax.rem(ids[4] - lax.rem(q, 4) + 4, 4)
        k2 = low ^ (q // 4)
        row = gain[ids[0] * 8 + q]
        for k1 in range(2):
            value = x_all[s, 2 * k1 + k2, 0].astype(F32)
            total[k1] = total[k1] + jnp.sum(value * value, axis=1, keepdims=True)
            at = (slice(128 * k1, 128 * k1 + 128), slice(256 * i, 256 * i + 256))
            mixed[(0,) + at] = (value * row).astype(BF16)
            mixed[(1,) + at] = x_all[s, 2 * k1 + k2, 1]
    for copy in w_copies:
        copy.wait()
    for k1 in range(2):
        sq[k1] = jnp.broadcast_to(total[k1], (128, 128))
    for w in range(3):
        left = mixed[0 if w < 2 else 1]
        part = dot(left, w_all[w].reshape(2048, 384), 1, 0)
        acc[:, :, 384 * w : 384 * w + 384] = part.reshape(2, 128, 384)
    keep[...] = acc[own]
    squares[...] = sq[own]
    send[:, :1152] = acc[1 - own].astype(BF16)
    head, rest = split_float(sq[1 - own])
    lane = lax.broadcasted_iota(jnp.int32, (128, 128), 1)
    send[:, 1152:] = jnp.where(lane < 64, head, rest).astype(BF16)


def activation_kernel(ids, keep, squares, recv, mine, scale):
    total = squares[:, 0:1] + recv[:, 1152:1153].astype(F32) + recv[:, 1216:1217].astype(F32)
    inv_rms = lax.rsqrt(total / 4096 + norm_epsilon)
    scale[...] = jnp.broadcast_to(inv_rms, (128, 128))
    gate = (keep[:, :384] + recv[:, :384].astype(F32)) * inv_rms
    up = (keep[:, 384:768] + recv[:, 384:768].astype(F32)) * inv_rms
    d_inner = (keep[:, 768:] + recv[:, 768:1152].astype(F32)) * inv_rms
    root = 0.7978845608028654
    tanh = jnp.tanh(root * (gate + 0.044715 * (gate * gate * gate)))
    cdf = 0.5 * (1.0 + tanh)
    activated = gate * cdf
    slope = cdf + 0.5 * gate * (1.0 - tanh * tanh) * root * (1.0 + 3 * 0.044715 * (gate * gate))
    d_gate = (d_inner * up * slope).astype(BF16)
    d_up = (d_inner * activated).astype(BF16)
    mine[:128, :384] = (activated * up).astype(BF16)
    mine[:128, 384:768] = d_gate
    mine[:128, 768:] = d_up
    tau = jnp.sum(d_gate.astype(F32) * gate + d_up.astype(F32) * up, axis=1, keepdims=True)
    rows = jnp.broadcast_to(tau, (128, 128)).T[:16]
    head, rest = split_float(rows)
    mine[128:, :] = jnp.zeros((16, 1152), BF16)
    mine[128:, :128] = head.astype(BF16)
    mine[128:, 128:256] = rest.astype(BF16)


def load_rows(ids, mine, recv, d_all):
    own = (ids[3] // 2) ^ ids[0]
    d_all[own] = mine[...]
    d_all[1 - own] = recv[...]


def outputs_kernel(ids, mine, recv, *refs):
    weights, outs, (w_all, d_all, w_sem) = refs[:8], refs[8:12], refs[12:]
    copies = [pltpu.make_async_copy(weights[i], w_all.at[:, i], w_sem.at[i]) for i in range(8)]
    for copy in copies:
        copy.start()
    load_rows(ids, mine, recv, d_all)
    for copy in copies:
        copy.wait()
    low = ids[3] % 2
    acts = [d_all[:, :128, 384 * w : 384 * w + 384].reshape(256, 384) for w in range(3)]
    for s in range(4):
        for k2 in range(2):
            q = (low ^ k2) * 4 + lax.rem(ids[4] - s + 4, 4)
            t = lax.rem(ids[1] - q // 2 + 4, 4)
            i = (ids[2] ^ lax.rem(q, 2)) * 4 + t
            branch = dot(acts[0], w_all[2, i], 1, 1).astype(BF16)
            feat = dot(acts[1], w_all[0, i], 1, 1) + dot(acts[2], w_all[1, i], 1, 1)
            feat = feat.astype(BF16)
            for k1 in range(2):
                rows = slice(128 * k1, 128 * k1 + 128)
                outs[s][2 * k1 + k2, :128] = branch[rows]
                outs[s][2 * k1 + k2, 128:256] = feat[rows]
                outs[s][2 * k1 + k2, 256:] = d_all[k1, 128:, :256]


def gradients_kernel(ids, mine, recv, mixed, kept, sent, d_all):
    load_rows(ids, mine, recv, d_all)
    for w, a in ((0, 1), (1, 2), (2, 0)):
        right = d_all[:, :128, 384 * a : 384 * a + 384].reshape(256, 384)
        for cc, out in ((0, kept), (1, sent)):
            left = mixed[0 if w < 2 else 1, :, 1024 * cc : 1024 * cc + 1024]
            out[w] = dot(left, right, 0, 0).astype(BF16).reshape(4, 256, 384)


def core_sum_kernel(ids, kept, recv, *outs):
    for t in range(4):
        outs[t][...] = (kept[:, t].astype(F32) + recv[:, t].astype(F32)).astype(BF16)


def sum_refs(refs, at):
    total = refs[0][at].astype(F32)
    for ref in refs[1:]:
        total = total + ref[at].astype(F32)
    return total


def x_sum_kernel(ids, *refs):
    parts, outs = refs[:4], refs[4:]
    for k in range(4):
        outs[k][:256] = sum_refs(parts, (k, slice(0, 256))).astype(BF16)
        tail = sum_refs(parts, (k, slice(256, 272)))
        head, rest = split_float(tail[:, :128] + tail[:, 128:])
        outs[k][256:, :128] = head.astype(BF16)
        outs[k][256:, 128:] = rest.astype(BF16)


def finish_kernel(ids, p0, p1, p2, p3, tokens, cot, gain, scale, mixed_out, d_tokens):
    parts = (p0, p1, p2, p3)
    local = tokens[...].astype(F32)
    mixed_out[...] = (local + sum_refs(parts, slice(0, 128))).astype(BF16)
    tail = sum_refs(parts, slice(256, 272))
    tau = (tail[:, :128] + tail[:, 128:])[0:1]
    tau = jnp.broadcast_to(tau, (128, 128)).T
    coef = (scale[...] * tau * (1.0 / 4096))[:, 0:1]
    feat = sum_refs(parts, slice(128, 256)) * gain[ids[3] * 4 + ids[4]]
    d_tokens[...] = cot[...].astype(F32) + feat - local * coef


def grads_sum_kernel(ids, p0, p1, p2, p3, grad_gate, grad_up, grad_down):
    parts = (p0, p1, p2, p3)
    grad_gate[...] = sum_refs(parts, 0)
    grad_up[...] = sum_refs(parts, 1)
    grad_down[...] = sum_refs(parts, 2).T


def on_device(tokens, norm_gain, gate_weight, up_weight, down_weight, out_cotangent):
    ids = jnp.stack([lax.axis_index(n) for n in ("zh", "y", "c", "zl", "x")]).astype(jnp.int32)
    gain = norm_gain.reshape(16, 1, 256)

    pair = jnp.stack([tokens, out_cotangent])
    by_z = jnp.stack([lax.ppermute(pair, ("zh", "zl"), z_pairs(k)) for k in range(4)])
    pieces = [by_z] + [shift(by_z, "x", s) for s in (1, 2, 3)]
    weights = jnp.stack([gate_weight, up_weight, down_weight.T])
    by_y = [weights] + [shift(weights, "y", t) for t in (1, 2, 3)]
    w_blocks = by_y + [swap(piece, "c") for piece in by_y]

    send, keep, squares, mixed = call(
        products_kernel,
        ids,
        [*pieces, *w_blocks, gain],
        [ANY] * 12 + [VMEM],
        [((128, 1280), BF16), ((128, 1152), F32), ((128, 128), F32), ((2, 256, 2048), BF16)],
        [
            pltpu.VMEM((4, 4, 2, 128, 256), BF16),
            pltpu.VMEM((3, 8, 256, 384), BF16),
            pltpu.VMEM((2, 128, 1152), F32),
            pltpu.VMEM((2, 128, 128), F32),
            pltpu.SemaphoreType.DMA((4,)),
            pltpu.SemaphoreType.DMA((8,)),
        ],
        32,
    )
    mine, scale = call(
        activation_kernel,
        ids,
        [keep, squares, swap(send, "zh")],
        [VMEM] * 3,
        [((144, 1152), BF16), ((128, 128), F32)],
    )
    theirs = swap(mine, "zh")
    rows = pltpu.VMEM((2, 144, 1152), BF16)
    parts = call(
        outputs_kernel,
        ids,
        [mine, theirs, *w_blocks],
        [VMEM] * 2 + [ANY] * 8,
        [((4, 272, 256), BF16)] * 4,
        [pltpu.VMEM((3, 8, 256, 384), BF16), rows, pltpu.SemaphoreType.DMA((8,))],
        24,
    )
    kept, sent = call(
        gradients_kernel,
        ids,
        [mine, theirs, mixed],
        [VMEM] * 3,
        [((3, 4, 256, 384), BF16)] * 2,
        [rows],
        32,
    )
    parts = [parts[0]] + [shift(parts[s], "x", -s) for s in (1, 2, 3)]
    blocks = call(x_sum_kernel, ids, parts, [VMEM] * 4, [((272, 256), BF16)] * 4)
    blocks = [
        lax.ppermute(blocks[k], ("zh", "zl"), [(t, s) for s, t in z_pairs(k)]) for k in range(4)
    ]
    mixed_out, d_tokens = call(
        finish_kernel,
        ids,
        [*blocks, tokens, out_cotangent, gain, scale],
        [VMEM] * 8,
        [((128, 256), BF16), ((128, 256), F32)],
    )
    sums = call(
        core_sum_kernel, ids, [kept, swap(sent, "c")], [VMEM] * 2, [((3, 256, 384), BF16)] * 4, (), 16
    )
    sums = [sums[0]] + [shift(sums[t], "y", -t) for t in (1, 2, 3)]
    grad_gate, grad_up, grad_down = call(
        grads_sum_kernel,
        ids,
        sums,
        [VMEM] * 4,
        [((256, 384), F32), ((256, 384), F32), ((384, 256), F32)],
        (),
        16,
    )
    return (mixed_out, d_tokens, grad_gate, grad_up, grad_down)


def solution(mesh):
    split = Mesh(mesh.devices.reshape(2, 4, 2, 4, 4), ("zh", "y", "c", "zl", "x"))
    grp, dev = ("zh", "y", "c"), ("zl", "x")
    in_specs = (P(grp, dev), P(), P(grp, dev), P(grp, dev), P(dev, grp), P(grp, dev))
    out_specs = (P(grp, dev), P(grp, dev), P(grp, dev), P(grp, dev), P(dev, grp))
    return jax.shard_map(
        on_device, mesh=split, in_specs=in_specs, out_specs=out_specs, check_vma=False
    )
```

profile of v0, /device:TPU:97, one launch (start us, length us, event | category | flops | bytes accessed | tf_op | source)
XLA Modules:
  0.0 186.4 jit_solution(7416065043172824240)
XLA Ops:
  1.5 3.8 %collective-permute-start.3 = (bf16[2,128,256]{2,1,0:T(8,128)(2,1)S(1)}, bf16[2,128,256]{2,1,0:T(8,128)(2,1)S(1)}, u32[]{:S(2)}, u32[]{:S(2)}) collective-permute-start(bf16[2,128,256]{2,1,0:T(8,128)(2,1)S(1)} %pad_maximum_fusion.2), channel_id=1, source_target_pairs={{0,12},{4,8},{8,140},{12,136},{128,4},{132,0},{136,132},{140,128},... | collective-permute-start | bytes 393224 | tf_op jit(solution)/shard_map/ppermute | solution.py:215
  5.4 2.1 %collective-permute-start.2 = (bf16[2,128,256]{2,1,0:T(8,128)(2,1)S(1)}, bf16[2,128,256]{2,1,0:T(8,128)(2,1)S(1)}, u32[]{:S(2)}, u32[]{:S(2)}) collective-permute-start(bf16[2,128,256]{2,1,0:T(8,128)(2,1)S(1)} %pad_maximum_fusion.2), channel_id=1, source_target_pairs={{0,8},{4,12},{8,136},{12,140},{128,0},{132,4},{136,128},{140,132},... | collective-permute-start | bytes 393224 | tf_op jit(solution)/shard_map/ppermute | solution.py:215
  7.4 5.0 %collective-permute-start = (bf16[2,128,256]{2,1,0:T(8,128)(2,1)S(1)}, bf16[2,128,256]{2,1,0:T(8,128)(2,1)}, u32[]{:S(2)}, u32[]{:S(2)}) collective-permute-start(bf16[2,128,256]{2,1,0:T(8,128)(2,1)S(1)} %pad_maximum_fusion.2), channel_id=1, source_target_pairs={{0,0},{4,4},{8,128},{12,132},{128,8},{132,12},{136,136},{140,140},... | collective-permute-start | bytes 393224 | tf_op jit(solution)/shard_map/ppermute | solution.py:215
  13.6 1.1 pad_maximum_fusion.refs_4_.refs_0_
  14.7 2.8 %collective-permute-start.9 = (bf16[3,256,384]{2,1,0:T(8,128)(2,1)S(1)}, bf16[3,256,384]{2,1,0:T(8,128)(2,1)S(1)}, u32[]{:S(2)}, u32[]{:S(2)}) collective-permute-start(bf16[3,256,384]{2,1,0:T(8,128)(2,1)S(1)} %pad_maximum_fusion.refs_4_.refs_0_), channel_id=1, source_target_pairs={{0,96},{32,0},{64,32},{96,64},{1,97},{33,1},{65,33},{97,65},{2,98}... | collective-permute-start | bytes 1769480 | tf_op jit(solution)/shard_map/ppermute | solution.py:27
  18.5 3.3 %collective-permute-start.10 = (bf16[3,256,384]{2,1,0:T(8,128)(2,1)S(1)}, bf16[3,256,384]{2,1,0:T(8,128)(2,1)S(1)}, u32[]{:S(2)}, u32[]{:S(2)}) collective-permute-start(bf16[3,256,384]{2,1,0:T(8,128)(2,1)S(1)} %pad_maximum_fusion.refs_4_.refs_0_), channel_id=1, source_target_pairs={{0,16},{16,0},{1,17},{17,1},{2,18},{18,2},{3,19},{19,3},{4,20},{20... | collective-permute-start | bytes 1769480 | tf_op jit(solution)/shard_map/ppermute | solution.py:31
  21.9 1.8 pad_maximum_fusion.1.refs_0_
  23.7 2.5 %collective-permute-start.6 = (bf16[4,2,128,256]{3,2,1,0:T(8,128)(2,1)}, bf16[4,2,128,256]{3,2,1,0:T(8,128)(2,1)S(1)}, u32[]{:S(2)}, u32[]{:S(2)}) collective-permute-start(bf16[4,2,128,256]{3,2,1,0:T(8,128)(2,1)} %pad_maximum_fusion.1.refs_0_), channel_id=1, source_target_pairs={{0,3},{1,0},{2,1},{3,2},{4,7},{5,4},{6,5},{7,6},{8,11},{9,8},{10,9... | collective-permute-start | bytes 1572872 | tf_op jit(solution)/shard_map/ppermute | solution.py:27
  26.2 3.2 %collective-permute-done.9.refs_7_.refs_3_ = bf16[3,256,384]{2,1,0:T(8,128)(2,1)S(1)} collective-permute-done((bf16[3,256,384]{2,1,0:T(8,128)(2,1)S(1)}, bf16[3,256,384]{2,1,0:T(8,128)(2,1)S(1)}, u32[]{:S(2)}, u32[]{:S(2)}) %collective-permute-start.9) | collective-permute-done | bytes 589856 | tf_op jit(solution)/shard_map/ppermute | solution.py:27
  29.4 14.3 %collective-permute-start.13 = (bf16[3,256,384]{2,1,0:T(8,128)(2,1)S(1)}, bf16[3,256,384]{2,1,0:T(8,128)(2,1)S(1)}, u32[]{:S(2)}, u32[]{:S(2)}) collective-permute-start(bf16[3,256,384]{2,1,0:T(8,128)(2,1)S(1)} %collective-permute-done.9.refs_7_.refs_3_), channel_id=1, source_target_pairs={{0,16},{16,0},{1,17},{17,1},{2,18},{18,2},{3,19},{19,3},{4,20},{20... | collective-permute-start | bytes 1769480 | tf_op jit(solution)/shard_map/ppermute | solution.py:31
  43.7 3.2 %collective-permute-done.7.refs_5_.refs_1_ = bf16[3,256,384]{2,1,0:T(8,128)(2,1)S(1)} collective-permute-done((bf16[3,256,384]{2,1,0:T(8,128)(2,1)S(1)}, bf16[3,256,384]{2,1,0:T(8,128)(2,1)S(1)}, u32[]{:S(2)}, u32[]{:S(2)}) %collective-permute-start.7) | collective-permute-done | bytes 589856 | tf_op jit(solution)/shard_map/ppermute | solution.py:27
  47.4 2.7 %collective-permute-start.5 = (bf16[4,2,128,256]{3,2,1,0:T(8,128)(2,1)}, bf16[4,2,128,256]{3,2,1,0:T(8,128)(2,1)}, u32[]{:S(2)}, u32[]{:S(2)}) collective-permute-start(bf16[4,2,128,256]{3,2,1,0:T(8,128)(2,1)} %pad_maximum_fusion.1.refs_0_), channel_id=1, source_target_pairs={{0,2},{1,3},{2,0},{3,1},{4,6},{5,7},{6,4},{7,5},{8,10},{9,11},{10,... | collective-permute-start | bytes 1572872 | tf_op jit(solution)/shard_map/ppermute | solution.py:27
  51.9 10.9 %collective-permute-done.5.refs_2_ = bf16[4,2,128,256]{3,2,1,0:T(8,128)(2,1)} collective-permute-done((bf16[4,2,128,256]{3,2,1,0:T(8,128)(2,1)}, bf16[4,2,128,256]{3,2,1,0:T(8,128)(2,1)}, u32[]{:S(2)}, u32[]{:S(2)}) %collective-permute-start.5) | collective-permute-done | bytes 524320 | tf_op jit(solution)/shard_map/ppermute | solution.py:27
  62.8 11.5 %collective-permute-done.4.refs_1_ = bf16[4,2,128,256]{3,2,1,0:T(8,128)(2,1)} collective-permute-done((bf16[4,2,128,256]{3,2,1,0:T(8,128)(2,1)}, bf16[4,2,128,256]{3,2,1,0:T(8,128)(2,1)}, u32[]{:S(2)}, u32[]{:S(2)}) %collective-permute-start.4) | collective-permute-done | bytes 524320 | tf_op jit(solution)/shard_map/ppermute | solution.py:27
  76.0 4.4 %shard_map.101 = (bf16[128,1280]{1,0:T(8,128)(2,1)S(1)}, f32[128,1152]{1,0:T(8,128)S(1)}, f32[128,128]{1,0:T(8,128)S(1)}, bf16[2,256,2048]{2,1,0:T(8,128)(2,1)S(1)}) custom-call(s32[5]{0:T(128)S(1)} %copy-done.5, bf16[4,2,128,256]{3,2,1,0:T(8,128)(2,1)} %pad_maximum_fusion.1.refs_0_, bf16[4,2,128,256]{3,2,1,0:T(8,128)(2,1)} %collective-permute-done.4.refs_1_, ...), custom_call_target="tpu_custom_call" | custom-call | tf_op jit(solution)/shard_map/pallas_call | solution.py:50
  80.5 4.7 %collective-permute-start.14 = (bf16[128,1280]{1,0:T(8,128)(2,1)S(1)}, bf16[128,1280]{1,0:T(8,128)(2,1)S(1)}, u32[]{:S(2)}, u32[]{:S(2)}) collective-permute-start(bf16[128,1280]{1,0:T(8,128)(2,1)S(1)} %get-tuple-element.32), channel_id=1, source_target_pairs={{0,128},{128,0},{1,129},{129,1},{2,130},{130,2},{3,131},{131,3},{4... | collective-permute-start | bytes 983048 | tf_op jit(solution)/shard_map/ppermute | solution.py:31
  85.2 15.9 %collective-permute-done.14.recv = bf16[128,1280]{1,0:T(8,128)(2,1)S(1)} collective-permute-done((bf16[128,1280]{1,0:T(8,128)(2,1)S(1)}, bf16[128,1280]{1,0:T(8,128)(2,1)S(1)}, u32[]{:S(2)}, u32[]{:S(2)}) %collective-permute-start.14) | collective-permute-done | bytes 327712 | tf_op jit(solution)/shard_map/ppermute | solution.py:31
  102.6 15.3 %collective-permute-done.15.recv = bf16[144,1152]{1,0:T(8,128)(2,1)S(1)} collective-permute-done((bf16[144,1152]{1,0:T(8,128)(2,1)S(1)}, bf16[144,1152]{1,0:T(8,128)(2,1)S(1)}, u32[]{:S(2)}, u32[]{:S(2)}) %collective-permute-start.15) | collective-permute-done | bytes 331808 | tf_op jit(solution)/shard_map/ppermute | solution.py:31
  117.9 2.4 %shard_map.106 = (bf16[3,4,256,384]{3,2,1,0:T(8,128)(2,1)S(1)}, bf16[3,4,256,384]{3,2,1,0:T(8,128)(2,1)S(1)}) custom-call(s32[5]{0:T(128)S(1)} %copy-done.5, bf16[144,1152]{1,0:T(8,128)(2,1)S(1)} %get-tuple-element.33.mine, bf16[144,1152]{1,0:T(8,128)(2,1)S(1)} %collective-permute-done.15.recv, bf16[2,256,2048]{2,1,0:T(8,128)(2,1)S(1)} %get-tuple-element.45.mixed), custom_call_target="tpu_custom_call" | custom-call | tf_op jit(solution)/shard_map/pallas_call | solution.py:50
  120.4 1.7 collective-permute-start.23
  122.1 3.9 %shard_map.103 = (bf16[4,272,256]{2,1,0:T(8,128)(2,1)S(1)}, bf16[4,272,256]{2,1,0:T(8,128)(2,1)S(1)}, bf16[4,272,256]{2,1,0:T(8,128)(2,1)S(1)}, bf16[4,272,256]{2,1,0:T(8,128)(2,1)S(1)}) custom-call(s32[5]{0:T(128)S(1)} %copy-done.6, bf16[144,1152]{1,0:T(8,128)(2,1)S(1)} %get-tuple-element.33.mine, bf16[144,1152]{1,0:T(8,128)(2,1)S(1)} %collective-permute-done.15.recv, ...), custom_call_target="tpu_custom_call" | custom-call | tf_op jit(solution)/shard_map/pallas_call | solution.py:50
  126.1 2.7 %collective-permute-start.17 = (bf16[4,272,256]{2,1,0:T(8,128)(2,1)S(1)}, bf16[4,272,256]{2,1,0:T(8,128)(2,1)S(1)}, u32[]{:S(2)}, u32[]{:S(2)}) collective-permute-start(bf16[4,272,256]{2,1,0:T(8,128)(2,1)S(1)} %get-tuple-element.36), channel_id=1, source_target_pairs={{0,2},{1,3},{2,0},{3,1},{4,6},{5,7},{6,4},{7,5},{8,10},{9,11},{10,... | collective-permute-start | bytes 1671176 | tf_op jit(solution)/shard_map/ppermute | solution.py:27
  129.5 1.1 shard_map.107
  131.7 8.6 %collective-permute-done.16.refs_1_ = bf16[4,272,256]{2,1,0:T(8,128)(2,1)S(1)} collective-permute-done((bf16[4,272,256]{2,1,0:T(8,128)(2,1)S(1)}, bf16[4,272,256]{2,1,0:T(8,128)(2,1)S(1)}, u32[]{:S(2)}, u32[]{:S(2)}) %collective-permute-start.16) | collective-permute-done | bytes 557088 | tf_op jit(solution)/shard_map/ppermute | solution.py:27
  140.3 1.5 collective-permute-done.17.refs_2_
  141.8 12.4 %collective-permute-done.18.refs_3_ = bf16[4,272,256]{2,1,0:T(8,128)(2,1)S(1)} collective-permute-done((bf16[4,272,256]{2,1,0:T(8,128)(2,1)S(1)}, bf16[4,272,256]{2,1,0:T(8,128)(2,1)S(1)}, u32[]{:S(2)}, u32[]{:S(2)}) %collective-permute-start.18) | collective-permute-done | bytes 557088 | tf_op jit(solution)/shard_map/ppermute | solution.py:27
  155.0 3.8 %collective-permute-start.19 = (bf16[272,256]{1,0:T(8,128)(2,1)S(1)}, bf16[272,256]{1,0:T(8,128)(2,1)S(1)}, u32[]{:S(2)}, u32[]{:S(2)}) collective-permute-start(bf16[272,256]{1,0:T(8,128)(2,1)S(1)} %get-tuple-element.38), channel_id=1, source_target_pairs={{0,0},{4,4},{128,8},{132,12},{8,128},{12,132},{136,136},{140,140},... | collective-permute-start | bytes 417800 | tf_op jit(solution)/shard_map/ppermute | solution.py:267
  158.9 4.9 %collective-permute-done.19.p0 = bf16[272,256]{1,0:T(8,128)(2,1)S(1)} collective-permute-done((bf16[272,256]{1,0:T(8,128)(2,1)S(1)}, bf16[272,256]{1,0:T(8,128)(2,1)S(1)}, u32[]{:S(2)}, u32[]{:S(2)}) %collective-permute-start.19) | collective-permute-done | bytes 139296 | tf_op jit(solution)/shard_map/ppermute | solution.py:267
  163.8 8.3 %collective-permute-done.20.p1 = bf16[272,256]{1,0:T(8,128)(2,1)S(1)} collective-permute-done((bf16[272,256]{1,0:T(8,128)(2,1)S(1)}, bf16[272,256]{1,0:T(8,128)(2,1)S(1)}, u32[]{:S(2)}, u32[]{:S(2)}) %collective-permute-start.20) | collective-permute-done | bytes 139296 | tf_op jit(solution)/shard_map/ppermute | solution.py:267
  172.1 11.1 %collective-permute-done.22.p3 = bf16[272,256]{1,0:T(8,128)(2,1)S(1)} collective-permute-done((bf16[272,256]{1,0:T(8,128)(2,1)S(1)}, bf16[272,256]{1,0:T(8,128)(2,1)S(1)}, u32[]{:S(2)}, u32[]{:S(2)}) %collective-permute-start.22) | collective-permute-done | bytes 139296 | tf_op jit(solution)/shard_map/ppermute | solution.py:267
  183.2 1.4 shard_map.105
  184.6 1.8 shard_map.108
  (49 shorter events, 11.5 us)
Async XLA Ops:
  0.6 73.7 %copy-start.4 = (f32[4096]{0:T(1024)S(1)}, f32[4096]{0:T(1024)}, u32[]{:S(2)}) copy-start(f32[4096]{0:T(1024)} %param.7) | copy-start | bytes 49156
  1.5 16.0 %collective-permute-start.3 = (bf16[2,128,256]{2,1,0:T(8,128)(2,1)S(1)}, bf16[2,128,256]{2,1,0:T(8,128)(2,1)S(1)}, u32[]{:S(2)}, u32[]{:S(2)}) collective-permute-start(bf16[2,128,256]{2,1,0:T(8,128)(2,1)S(1)} %pad_maximum_fusion.2), channel_id=1, source_target_pairs={{0,12},{4,8},{8,140},{12,136},{128,4},{132,0},{136,132},{140,128},... | collective-permute-start | bytes 393224 | tf_op jit(solution)/shard_map/ppermute | solution.py:215
  5.4 12.5 %collective-permute-start.2 = (bf16[2,128,256]{2,1,0:T(8,128)(2,1)S(1)}, bf16[2,128,256]{2,1,0:T(8,128)(2,1)S(1)}, u32[]{:S(2)}, u32[]{:S(2)}) collective-permute-start(bf16[2,128,256]{2,1,0:T(8,128)(2,1)S(1)} %pad_maximum_fusion.2), channel_id=1, source_target_pairs={{0,8},{4,12},{8,136},{12,140},{128,0},{132,4},{136,128},{140,132},... | collective-permute-start | bytes 393224 | tf_op jit(solution)/shard_map/ppermute | solution.py:215
  7.4 11.1 %collective-permute-start.1 = (bf16[2,128,256]{2,1,0:T(8,128)(2,1)S(1)}, bf16[2,128,256]{2,1,0:T(8,128)(2,1)S(1)}, u32[]{:S(2)}, u32[]{:S(2)}) collective-permute-start(bf16[2,128,256]{2,1,0:T(8,128)(2,1)S(1)} %pad_maximum_fusion.2), channel_id=1, source_target_pairs={{0,4},{4,0},{8,132},{12,128},{128,12},{132,8},{136,140},{140,136},... | collective-permute-start | bytes 393224 | tf_op jit(solution)/shard_map/ppermute | solution.py:215
  7.4 14.5 %collective-permute-start = (bf16[2,128,256]{2,1,0:T(8,128)(2,1)S(1)}, bf16[2,128,256]{2,1,0:T(8,128)(2,1)}, u32[]{:S(2)}, u32[]{:S(2)}) collective-permute-start(bf16[2,128,256]{2,1,0:T(8,128)(2,1)S(1)} %pad_maximum_fusion.2), channel_id=1, source_target_pairs={{0,0},{4,4},{8,128},{12,132},{128,8},{132,12},{136,136},{140,140},... | collective-permute-start | bytes 393224 | tf_op jit(solution)/shard_map/ppermute | solution.py:215
  14.7 14.7 %collective-permute-start.9 = (bf16[3,256,384]{2,1,0:T(8,128)(2,1)S(1)}, bf16[3,256,384]{2,1,0:T(8,128)(2,1)S(1)}, u32[]{:S(2)}, u32[]{:S(2)}) collective-permute-start(bf16[3,256,384]{2,1,0:T(8,128)(2,1)S(1)} %pad_maximum_fusion.refs_4_.refs_0_), channel_id=1, source_target_pairs={{0,96},{32,0},{64,32},{96,64},{1,97},{33,1},{65,33},{97,65},{2,98}... | collective-permute-start | bytes 1769480 | tf_op jit(solution)/shard_map/ppermute | solution.py:27
  17.5 26.2 %collective-permute-start.8 = (bf16[3,256,384]{2,1,0:T(8,128)(2,1)S(1)}, bf16[3,256,384]{2,1,0:T(8,128)(2,1)S(1)}, u32[]{:S(2)}, u32[]{:S(2)}) collective-permute-start(bf16[3,256,384]{2,1,0:T(8,128)(2,1)S(1)} %pad_maximum_fusion.refs_4_.refs_0_), channel_id=1, source_target_pairs={{0,64},{32,96},{64,0},{96,32},{1,65},{33,97},{65,1},{97,33},{2,66}... | collective-permute-start | bytes 1769480 | tf_op jit(solution)/shard_map/ppermute | solution.py:27
  17.8 29.0 %collective-permute-start.7 = (bf16[3,256,384]{2,1,0:T(8,128)(2,1)S(1)}, bf16[3,256,384]{2,1,0:T(8,128)(2,1)S(1)}, u32[]{:S(2)}, u32[]{:S(2)}) collective-permute-start(bf16[3,256,384]{2,1,0:T(8,128)(2,1)S(1)} %pad_maximum_fusion.refs_4_.refs_0_), channel_id=1, source_target_pairs={{0,32},{32,64},{64,96},{96,0},{1,33},{33,65},{65,97},{97,1},{2,34}... | collective-permute-start | bytes 1769480 | tf_op jit(solution)/shard_map/ppermute | solution.py:27
  18.5 28.8 %collective-permute-start.10 = (bf16[3,256,384]{2,1,0:T(8,128)(2,1)S(1)}, bf16[3,256,384]{2,1,0:T(8,128)(2,1)S(1)}, u32[]{:S(2)}, u32[]{:S(2)}) collective-permute-start(bf16[3,256,384]{2,1,0:T(8,128)(2,1)S(1)} %pad_maximum_fusion.refs_4_.refs_0_), channel_id=1, source_target_pairs={{0,16},{16,0},{1,17},{17,1},{2,18},{18,2},{3,19},{19,3},{4,20},{20... | collective-permute-start | bytes 1769480 | tf_op jit(solution)/shard_map/ppermute | solution.py:31
  23.7 26.4 %collective-permute-start.6 = (bf16[4,2,128,256]{3,2,1,0:T(8,128)(2,1)}, bf16[4,2,128,256]{3,2,1,0:T(8,128)(2,1)S(1)}, u32[]{:S(2)}, u32[]{:S(2)}) collective-permute-start(bf16[4,2,128,256]{3,2,1,0:T(8,128)(2,1)} %pad_maximum_fusion.1.refs_0_), channel_id=1, source_target_pairs={{0,3},{1,0},{2,1},{3,2},{4,7},{5,4},{6,5},{7,6},{8,11},{9,8},{10,9... | collective-permute-start | bytes 1572872 | tf_op jit(solution)/shard_map/ppermute | solution.py:27
  29.4 45.0 %collective-permute-start.13 = (bf16[3,256,384]{2,1,0:T(8,128)(2,1)S(1)}, bf16[3,256,384]{2,1,0:T(8,128)(2,1)S(1)}, u32[]{:S(2)}, u32[]{:S(2)}) collective-permute-start(bf16[3,256,384]{2,1,0:T(8,128)(2,1)S(1)} %collective-permute-done.9.refs_7_.refs_3_), channel_id=1, source_target_pairs={{0,16},{16,0},{1,17},{17,1},{2,18},{18,2},{3,19},{19,3},{4,20},{20... | collective-permute-start | bytes 1769480 | tf_op jit(solution)/shard_map/ppermute | solution.py:31
  43.7 30.6 %collective-permute-start.12 = (bf16[3,256,384]{2,1,0:T(8,128)(2,1)S(1)}, bf16[3,256,384]{2,1,0:T(8,128)(2,1)}, u32[]{:S(2)}, u32[]{:S(2)}) collective-permute-start(bf16[3,256,384]{2,1,0:T(8,128)(2,1)S(1)} %collective-permute-done.8.refs_6_.refs_2_), channel_id=1, source_target_pairs={{0,16},{16,0},{1,17},{17,1},{2,18},{18,2},{3,19},{19,3},{4,20},{20... | collective-permute-start | bytes 1769480 | tf_op jit(solution)/shard_map/ppermute | solution.py:31
  46.9 27.4 %collective-permute-start.11 = (bf16[3,256,384]{2,1,0:T(8,128)(2,1)S(1)}, bf16[3,256,384]{2,1,0:T(8,128)(2,1)}, u32[]{:S(2)}, u32[]{:S(2)}) collective-permute-start(bf16[3,256,384]{2,1,0:T(8,128)(2,1)S(1)} %collective-permute-done.7.refs_5_.refs_1_), channel_id=1, source_target_pairs={{0,16},{16,0},{1,17},{17,1},{2,18},{18,2},{3,19},{19,3},{4,20},{20... | collective-permute-start | bytes 1769480 | tf_op jit(solution)/shard_map/ppermute | solution.py:31
  47.4 15.4 %collective-permute-start.5 = (bf16[4,2,128,256]{3,2,1,0:T(8,128)(2,1)}, bf16[4,2,128,256]{3,2,1,0:T(8,128)(2,1)}, u32[]{:S(2)}, u32[]{:S(2)}) collective-permute-start(bf16[4,2,128,256]{3,2,1,0:T(8,128)(2,1)} %pad_maximum_fusion.1.refs_0_), channel_id=1, source_target_pairs={{0,2},{1,3},{2,0},{3,1},{4,6},{5,7},{6,4},{7,5},{8,10},{9,11},{10,... | collective-permute-start | bytes 1572872 | tf_op jit(solution)/shard_map/ppermute | solution.py:27
  50.9 23.4 %collective-permute-start.4 = (bf16[4,2,128,256]{3,2,1,0:T(8,128)(2,1)}, bf16[4,2,128,256]{3,2,1,0:T(8,128)(2,1)}, u32[]{:S(2)}, u32[]{:S(2)}) collective-permute-start(bf16[4,2,128,256]{3,2,1,0:T(8,128)(2,1)} %pad_maximum_fusion.1.refs_0_), channel_id=1, source_target_pairs={{0,1},{1,2},{2,3},{3,0},{4,5},{5,6},{6,7},{7,4},{8,9},{9,10},{10,1... | collective-permute-start | bytes 1572872 | tf_op jit(solution)/shard_map/ppermute | solution.py:27
  74.3 1.0 copy-start.1
  80.4 41.7 %copy-start.6 = (s32[5]{0:T(128)S(1)}, s32[5]{0:T(128)}, u32[]{:S(2)}) copy-start(s32[5]{0:T(128)} %stack.59.ids) | copy-start | bytes 64
  80.5 20.6 %collective-permute-start.14 = (bf16[128,1280]{1,0:T(8,128)(2,1)S(1)}, bf16[128,1280]{1,0:T(8,128)(2,1)S(1)}, u32[]{:S(2)}, u32[]{:S(2)}) collective-permute-start(bf16[128,1280]{1,0:T(8,128)(2,1)S(1)} %get-tuple-element.32), channel_id=1, source_target_pairs={{0,128},{128,0},{1,129},{129,1},{2,130},{130,2},{3,131},{131,3},{4... | collective-permute-start | bytes 983048 | tf_op jit(solution)/shard_map/ppermute | solution.py:31
  102.1 15.9 %collective-permute-start.15 = (bf16[144,1152]{1,0:T(8,128)(2,1)S(1)}, bf16[144,1152]{1,0:T(8,128)(2,1)S(1)}, u32[]{:S(2)}, u32[]{:S(2)}) collective-permute-start(bf16[144,1152]{1,0:T(8,128)(2,1)S(1)} %get-tuple-element.33.mine), channel_id=1, source_target_pairs={{0,128},{128,0},{1,129},{129,1},{2,130},{130,2},{3,131},{131,3},{4... | collective-permute-start | bytes 995336 | tf_op jit(solution)/shard_map/ppermute | solution.py:31
  120.4 9.1 %collective-permute-start.23 = (bf16[3,4,256,384]{3,2,1,0:T(8,128)(2,1)S(1)}, bf16[3,4,256,384]{3,2,1,0:T(8,128)(2,1)S(1)}, u32[]{:S(2)}, u32[]{:S(2)}) collective-permute-start(bf16[3,4,256,384]{3,2,1,0:T(8,128)(2,1)S(1)} %get-tuple-element.47), channel_id=1, source_target_pairs={{0,16},{16,0},{1,17},{17,1},{2,18},{18,2},{3,19},{19,3},{4,20},{20... | collective-permute-start | bytes 7077896 | tf_op jit(solution)/shard_map/ppermute | solution.py:31
  126.0 14.3 %collective-permute-start.16 = (bf16[4,272,256]{2,1,0:T(8,128)(2,1)S(1)}, bf16[4,272,256]{2,1,0:T(8,128)(2,1)S(1)}, u32[]{:S(2)}, u32[]{:S(2)}) collective-permute-start(bf16[4,272,256]{2,1,0:T(8,128)(2,1)S(1)} %get-tuple-element.35), channel_id=1, source_target_pairs={{0,3},{1,0},{2,1},{3,2},{4,7},{5,4},{6,5},{7,6},{8,11},{9,8},{10,9... | collective-permute-start | bytes 1671176 | tf_op jit(solution)/shard_map/ppermute | solution.py:27
  126.1 15.7 %collective-permute-start.17 = (bf16[4,272,256]{2,1,0:T(8,128)(2,1)S(1)}, bf16[4,272,256]{2,1,0:T(8,128)(2,1)S(1)}, u32[]{:S(2)}, u32[]{:S(2)}) collective-permute-start(bf16[4,272,256]{2,1,0:T(8,128)(2,1)S(1)} %get-tuple-element.36), channel_id=1, source_target_pairs={{0,2},{1,3},{2,0},{3,1},{4,6},{5,7},{6,4},{7,5},{8,10},{9,11},{10,... | collective-permute-start | bytes 1671176 | tf_op jit(solution)/shard_map/ppermute | solution.py:27
  128.8 25.4 %collective-permute-start.18 = (bf16[4,272,256]{2,1,0:T(8,128)(2,1)S(1)}, bf16[4,272,256]{2,1,0:T(8,128)(2,1)S(1)}, u32[]{:S(2)}, u32[]{:S(2)}) collective-permute-start(bf16[4,272,256]{2,1,0:T(8,128)(2,1)S(1)} %get-tuple-element.37), channel_id=1, source_target_pairs={{0,1},{1,2},{2,3},{3,0},{4,5},{5,6},{6,7},{7,4},{8,9},{9,10},{10,1... | collective-permute-start | bytes 1671176 | tf_op jit(solution)/shard_map/ppermute | solution.py:27
  129.5 53.7 %copy-start.2 = (bf16[128,256]{1,0:T(8,128)(2,1)S(1)}, bf16[128,256]{1,0:T(8,128)(2,1)}, u32[]{:S(2)}) copy-start(bf16[128,256]{1,0:T(8,128)(2,1)} %cot.1) | copy-start | bytes 196612
  129.5 53.7 %copy-start.3 = (bf16[128,256]{1,0:T(8,128)(2,1)S(1)}, bf16[128,256]{1,0:T(8,128)(2,1)}, u32[]{:S(2)}) copy-start(bf16[128,256]{1,0:T(8,128)(2,1)} %tokens.1) | copy-start | bytes 196612
  130.6 54.0 %collective-permute-start.24 = (bf16[3,256,384]{2,1,0:T(8,128)(2,1)S(1)}, bf16[3,256,384]{2,1,0:T(8,128)(2,1)S(1)}, u32[]{:S(2)}, u32[]{:S(2)}) collective-permute-start(bf16[3,256,384]{2,1,0:T(8,128)(2,1)S(1)} %get-tuple-element.49), channel_id=1, source_target_pairs={{0,96},{32,0},{64,32},{96,64},{1,97},{33,1},{65,33},{97,65},{2,98}... | collective-permute-start | bytes 1769480 | tf_op jit(solution)/shard_map/ppermute | solution.py:27
  131.0 53.6 %collective-permute-start.25 = (bf16[3,256,384]{2,1,0:T(8,128)(2,1)S(1)}, bf16[3,256,384]{2,1,0:T(8,128)(2,1)S(1)}, u32[]{:S(2)}, u32[]{:S(2)}) collective-permute-start(bf16[3,256,384]{2,1,0:T(8,128)(2,1)S(1)} %get-tuple-element.50), channel_id=1, source_target_pairs={{0,64},{32,96},{64,0},{96,32},{1,65},{33,97},{65,1},{97,33},{2,66}... | collective-permute-start | bytes 1769480 | tf_op jit(solution)/shard_map/ppermute | solution.py:27
  140.3 44.3 %collective-permute-start.26 = (bf16[3,256,384]{2,1,0:T(8,128)(2,1)S(1)}, bf16[3,256,384]{2,1,0:T(8,128)(2,1)S(1)}, u32[]{:S(2)}, u32[]{:S(2)}) collective-permute-start(bf16[3,256,384]{2,1,0:T(8,128)(2,1)S(1)} %get-tuple-element.51), channel_id=1, source_target_pairs={{0,32},{32,64},{64,96},{96,0},{1,33},{33,65},{65,97},{97,1},{2,34}... | collective-permute-start | bytes 1769480 | tf_op jit(solution)/shard_map/ppermute | solution.py:27
  155.0 8.8 %collective-permute-start.19 = (bf16[272,256]{1,0:T(8,128)(2,1)S(1)}, bf16[272,256]{1,0:T(8,128)(2,1)S(1)}, u32[]{:S(2)}, u32[]{:S(2)}) collective-permute-start(bf16[272,256]{1,0:T(8,128)(2,1)S(1)} %get-tuple-element.38), channel_id=1, source_target_pairs={{0,0},{4,4},{128,8},{132,12},{8,128},{12,132},{136,136},{140,140},... | collective-permute-start | bytes 417800 | tf_op jit(solution)/shard_map/ppermute | solution.py:267
  158.8 13.3 %collective-permute-start.20 = (bf16[272,256]{1,0:T(8,128)(2,1)S(1)}, bf16[272,256]{1,0:T(8,128)(2,1)S(1)}, u32[]{:S(2)}, u32[]{:S(2)}) collective-permute-start(bf16[272,256]{1,0:T(8,128)(2,1)S(1)} %get-tuple-element.39), channel_id=1, source_target_pairs={{4,0},{0,4},{132,8},{128,12},{12,128},{8,132},{140,136},{136,140},... | collective-permute-start | bytes 417800 | tf_op jit(solution)/shard_map/ppermute | solution.py:267
  163.7 8.3 %collective-permute-start.21 = (bf16[272,256]{1,0:T(8,128)(2,1)S(1)}, bf16[272,256]{1,0:T(8,128)(2,1)S(1)}, u32[]{:S(2)}, u32[]{:S(2)}) collective-permute-start(bf16[272,256]{1,0:T(8,128)(2,1)S(1)} %get-tuple-element.40), channel_id=1, source_target_pairs={{8,0},{12,4},{136,8},{140,12},{0,128},{4,132},{128,136},{132,140},... | collective-permute-start | bytes 417800 | tf_op jit(solution)/shard_map/ppermute | solution.py:267
  172.1 11.1 %collective-permute-start.22 = (bf16[272,256]{1,0:T(8,128)(2,1)S(1)}, bf16[272,256]{1,0:T(8,128)(2,1)S(1)}, u32[]{:S(2)}, u32[]{:S(2)}) collective-permute-start(bf16[272,256]{1,0:T(8,128)(2,1)S(1)} %get-tuple-element.41), channel_id=1, source_target_pairs={{12,0},{8,4},{140,8},{136,12},{4,128},{0,132},{132,136},{128,140},... | collective-permute-start | bytes 417800 | tf_op jit(solution)/shard_map/ppermute | solution.py:267
  (2 other events, 1.4 us)
where the time goes:
time: 187 us; the launch traced here: 186 us
  waiting for transfers between devices  107 us (57%)
  starting transfers between devices  53.8 us (29%)
  Pallas kernels  16.9 us (9%)
  local copies, waits for them, and re-layouts  4.18 us (2%)
  other arithmetic  3.79 us (2%)
    ppermute x12, waiting for transfers between devices, shift(): return lax.ppermute(array, axis, [(i, (i + by) % 4) for i in range(4)])  51.3 us
    ppermute x7, waiting for transfers between devices, swap(): return lax.ppermute(array, axis, [(0, 1), (1, 0)])  31.3 us
    ppermute x7, starting transfers between devices, swap(): return lax.ppermute(array, axis, [(0, 1), (1, 0)])  25 us
    ppermute x4, waiting for transfers between devices, on_device(): lax.ppermute(blocks[k], ('zh', 'zl'), [(t, s) for s, t in z_pairs(k)])  24.3 us
    pallas_call x8, Pallas kernels, call(): pl.pallas_call(body, out_shape=[jax.ShapeDtypeStruct(s, d) for s, d in ou...  16.9 us
    ppermute x12, starting transfers between devices, shift(): return lax.ppermute(array, axis, [(i, (i + by) % 4) for i in range(4)])  14 us
    ppermute x4, starting transfers between devices, on_device(): lax.ppermute(pair, ('zh', 'zl'), z_pairs(k))  10.9 us
    ppermute x4, starting transfers between devices, on_device(): lax.ppermute(blocks[k], ('zh', 'zl'), [(t, s) for s, t in z_pairs(k)])  3.87 us
  transfers between devices with their start and end apart: 27, of which 13 were waited for; matrix products, arithmetic and copies ran while one was open for 2% of the time, Pallas kernels for 4%

commit v1 on v0

v1 whole, which is shorter than its diff:
```python
import math

import jax
import jax.numpy as jnp
from jax import lax
from jax.experimental import pallas as pl
from jax.experimental.pallas import tpu as pltpu
from jax.sharding import Mesh
from jax.sharding import PartitionSpec as P

norm_epsilon = 1e-06
F32 = jnp.float32
BF16 = jnp.bfloat16
ANY = pl.BlockSpec(memory_space=pl.ANY)
HBM = pl.BlockSpec(memory_space=pltpu.HBM)
SMEM = pl.BlockSpec(memory_space=pltpu.SMEM)
VMEM = pl.BlockSpec(memory_space=pltpu.VMEM)
MIB = 1 << 20


def dot(left, right, left_dim, right_dim):
    return lax.dot_general(
        left, right, (((left_dim,), (right_dim,)), ((), ())), preferred_element_type=F32
    )


def shift(array, axis, by):
    return lax.ppermute(array, axis, [(i, (i + by) % 4) for i in range(4)])


def swap(array, axis):
    return lax.ppermute(array, axis, [(0, 1), (1, 0)])


def z_pairs(k):
    k1, k2 = k // 2, k % 2
    return [
        (4 * zs + 2 * h + l, 4 * h + 2 * (zs ^ k1) + (l ^ k2))
        for zs in range(2)
        for h in range(2)
        for l in range(2)
    ]


def split_float(value):
    head = value.astype(BF16).astype(F32)
    return head, value - head


def call(body, ids, operands, specs, outs, scratch=(), limit=8, flops=0):
    size = sum(a.size * a.dtype.itemsize for a in operands)
    size += sum(2 * math.prod(shape) for shape, _ in outs)
    return pl.pallas_call(
        body,
        out_shape=[jax.ShapeDtypeStruct(s, d) for s, d in outs],
        in_specs=[SMEM] + specs,
        out_specs=[VMEM] * len(outs),
        scratch_shapes=list(scratch),
        compiler_params=pltpu.CompilerParams(vmem_limit_bytes=limit * MIB),
        cost_estimate=pl.CostEstimate(flops=flops, bytes_accessed=size, transcendentals=0),
    )(ids, *operands)


def block_q(ids, i):
    return lax.rem(ids[1] - i % 4 + 4, 4) * 2 + (ids[2] ^ (i // 4))


def block_i(ids, s, k2):
    q = ((ids[3] % 2) ^ k2) * 4 + lax.rem(ids[4] - s + 4, 4)
    return (ids[2] ^ lax.rem(q, 2)) * 4 + lax.rem(ids[1] - q // 2 + 4, 4)


def weight_copies(weights, rows, w_all, sem):
    first, count = rows
    return [
        pltpu.make_async_copy(view.at[pl.ds(first, count)], w_all.at[:, i], sem.at[i])
        for i, view in enumerate(weights)
    ]


def pack_kernel(ids, tokens, cot, gate, up, down, pair, own, down_in, sem):
    moves = [(down, down_in), (tokens, pair.at[0]), (cot, pair.at[1])]
    moves += [(gate, own.at[0]), (up, own.at[1])]
    copies = [pltpu.make_async_copy(*move, sem.at[i]) for i, move in enumerate(moves)]
    for copy in copies:
        copy.start()
    copies[0].wait()
    own[2] = down_in[...].T
    for copy in copies[1:]:
        copy.wait()


def stack_kernel(ids, p0, p1, p2, p3, tokens, cot):
    for k, piece in enumerate((p0, p1, p2, p3)):
        tokens[k] = piece[0]
        cot[k] = piece[1]


def load_pieces(ids, pieces, x_all, x_sem):
    copies = [pltpu.make_async_copy(pieces[s], x_all.at[s], x_sem.at[s]) for s in range(4)]
    for copy in copies:
        copy.start()
    for copy in copies:
        copy.wait()


def blocks_of(ids, x_all):
    for i in range(8):
        q = block_q(ids, i)
        s = lax.rem(ids[4] - lax.rem(q, 4) + 4, 4)
        k2 = (ids[3] % 2) ^ (q // 4)
        for k1 in range(2):
            at = (slice(128 * k1, 128 * k1 + 128), slice(256 * i, 256 * i + 256))
            yield i, q, k1, at, x_all[s, 2 * k1 + k2]


def forward_products_kernel(ids, *refs):
    pieces, weights, gain, send, mixed = refs[:4], refs[4:12], refs[12], refs[13], refs[14]
    x_all, w_all, x_sem, w_sem = refs[15:]
    copies = weight_copies(weights, (0, 2), w_all, w_sem)
    for copy in copies:
        copy.start()
    load_pieces(ids, pieces, x_all, x_sem)
    total = [jnp.zeros((128, 1), F32) for _ in range(2)]
    for i, q, k1, at, block in blocks_of(ids, x_all):
        value = block.astype(F32)
        total[k1] = total[k1] + jnp.sum(value * value, axis=1, keepdims=True)
        mixed[at] = (value * gain[ids[0] * 8 + q]).astype(BF16)
    for copy in copies:
        copy.wait()
    for w in range(2):
        part = dot(mixed[...], w_all[w].reshape(2048, 384), 1, 0)
        send[:256, 384 * w : 384 * w + 384] = part.astype(BF16)
    send[256:, :] = jnp.zeros((16, 768), BF16)
    for k1 in range(2):
        head, rest = split_float(jnp.broadcast_to(total[k1], (128, 128)).T[:16])
        send[256:, 128 * k1 : 128 * k1 + 128] = head.astype(BF16)
        send[256:, 256 + 128 * k1 : 384 + 128 * k1] = rest.astype(BF16)


def backward_products_kernel(ids, *refs):
    pieces, weights, send, mixed = refs[:4], refs[4:12], refs[12], refs[13]
    x_all, w_all, x_sem, w_sem = refs[14:]
    copies = weight_copies(weights, (2, 1), w_all, w_sem)
    for copy in copies:
        copy.start()
    load_pieces(ids, pieces, x_all, x_sem)
    for i, q, k1, at, block in blocks_of(ids, x_all):
        mixed[at] = block
    for copy in copies:
        copy.wait()
    part = dot(mixed[...], w_all[0].reshape(2048, 384), 1, 0)
    send[...] = part.astype(BF16)


def activations(mine, recv):
    tail = mine[256:257].astype(F32) + recv[256:257].astype(F32)
    total = jnp.concatenate([tail[:, :128] + tail[:, 256:384], tail[:, 128:256] + tail[:, 384:512]])
    cols = [jnp.broadcast_to(total[k : k + 1], (128, 128)).T[:, 0:1] for k in range(2)]
    inv_rms = lax.rsqrt(jnp.concatenate(cols) / 4096 + norm_epsilon)
    pre = (mine[:256].astype(F32) + recv[:256].astype(F32)) * inv_rms
    gate, up = pre[:, :384], pre[:, 384:]
    root = 0.7978845608028654
    tanh = jnp.tanh(root * (gate + 0.044715 * (gate * gate * gate)))
    cdf = 0.5 * (1.0 + tanh)
    slope = cdf + 0.5 * gate * (1.0 - tanh * tanh) * root * (1.0 + 3 * 0.044715 * (gate * gate))
    return inv_rms, gate, up, gate * cdf, slope


def gradients_kernel(
    ids, mine, recv, d_mine, d_recv, tokens, cot, kept, sent, acts, scale, tail
):
    inv_rms, gate, up, activated, slope = activations(mine, recv)
    d_inner = (d_mine[...].astype(F32) + d_recv[...].astype(F32)) * inv_rms
    d_gate = (d_inner * up * slope).astype(BF16)
    d_up = (d_inner * activated).astype(BF16)
    acts[:, :384] = d_gate
    acts[:, 384:768] = d_up
    acts[:, 768:] = (activated * up).astype(BF16)
    own = (ids[3] // 2) ^ ids[0]
    picked = jnp.where(own == 0, inv_rms[:128], inv_rms[128:])
    scale[...] = jnp.broadcast_to(picked, (128, 128))
    tau = jnp.sum(d_gate.astype(F32) * gate + d_up.astype(F32) * up, axis=1, keepdims=True)
    for k1 in range(2):
        rows = jnp.broadcast_to(tau[128 * k1 : 128 * k1 + 128], (128, 128)).T[:16]
        head, rest = split_float(rows)
        tail[k1, :, :128] = head.astype(BF16)
        tail[k1, :, 128:] = rest.astype(BF16)
    for cc, out in ((1, sent), (0, kept)):
        for w in range(3):
            right = acts[:, 384 * w : 384 * w + 384]
            source = cot if w == 2 else tokens
            left = source[:, 1024 * cc : 1024 * cc + 1024]
            out[w] = dot(left, right, 0, 0).astype(BF16).reshape(4, 256, 384)


def outputs_kernel(ids, acts, tail, *refs):
    weights, outs, (w_all, w_sem) = refs[:8], refs[8:12], refs[12:]
    copies = weight_copies(weights, (0, 3), w_all, w_sem)
    for copy in copies:
        copy.start()
    for copy in copies:
        copy.wait()
    left = [acts[:, 384 * w : 384 * w + 384] for w in range(3)]
    for s in range(4):
        for k2 in range(2):
            i = block_i(ids, s, k2)
            branch = dot(left[2], w_all[2, i], 1, 1).astype(BF16)
            feat = dot(left[0], w_all[0, i], 1, 1) + dot(left[1], w_all[1, i], 1, 1)
            feat = feat.astype(BF16)
            for k1 in range(2):
                rows = slice(128 * k1, 128 * k1 + 128)
                outs[s][2 * k1 + k2, :128] = branch[rows]
                outs[s][2 * k1 + k2, 128:256] = feat[rows]
                outs[s][2 * k1 + k2, 256:] = tail[k1]


def core_sum_kernel(ids, kept, recv, *outs):
    for t in range(4):
        outs[t][...] = (kept[:, t].astype(F32) + recv[:, t].astype(F32)).astype(BF16)


def sum_refs(refs, at):
    total = refs[0][at].astype(F32)
    for ref in refs[1:]:
        total = total + ref[at].astype(F32)
    return total


def x_sum_kernel(ids, *refs):
    parts, outs = refs[:4], refs[4:]
    for k in range(4):
        outs[k][:256] = sum_refs(parts, (k, slice(0, 256))).astype(BF16)
        tail = sum_refs(parts, (k, slice(256, 272)))
        head, rest = split_float(tail[:, :128] + tail[:, 128:])
        outs[k][256:, :128] = head.astype(BF16)
        outs[k][256:, 128:] = rest.astype(BF16)


def finish_kernel(ids, p0, p1, p2, p3, tokens, cot, gain, scale, mixed_out, d_tokens):
    parts = (p0, p1, p2, p3)
    local = tokens[...].astype(F32)
    mixed_out[...] = (local + sum_refs(parts, slice(0, 128))).astype(BF16)
    tail = sum_refs(parts, slice(256, 272))
    tau = (tail[:, :128] + tail[:, 128:])[0:1]
    tau = jnp.broadcast_to(tau, (128, 128)).T
    coef = (scale[...] * tau * (1.0 / 4096))[:, 0:1]
    feat = sum_refs(parts, slice(128, 256)) * gain[ids[3] * 4 + ids[4]]
    d_tokens[...] = cot[...].astype(F32) + feat - local * coef


def grads_sum_kernel(ids, p0, p1, p2, p3, grad_gate, grad_up, grad_down):
    parts = (p0, p1, p2, p3)
    grad_gate[...] = sum_refs(parts, 0)
    grad_up[...] = sum_refs(parts, 1)
    grad_down[...] = sum_refs(parts, 2).T


def after(value, *events):
    return lax.optimization_barrier((value, *events))[0]


def on_device(tokens, norm_gain, gate_weight, up_weight, down_weight, out_cotangent):
    ids = jnp.stack([lax.axis_index(n) for n in ("zh", "y", "c", "zl", "x")]).astype(jnp.int32)
    gain = norm_gain.reshape(16, 1, 256)
    dma = pltpu.SemaphoreType.DMA

    pair, own = call(
        pack_kernel,
        ids,
        [tokens, out_cotangent, gate_weight, up_weight, down_weight],
        [HBM] * 5,
        [((2, 128, 256), BF16), ((3, 256, 384), BF16)],
        [pltpu.VMEM((384, 256), BF16), dma((5,))],
    )
    by_z = [lax.ppermute(pair, ("zh", "zl"), z_pairs(k)) for k in range(4)]
    tok_z, cot_z = call(stack_kernel, ids, by_z, [VMEM] * 4, [((4, 128, 256), BF16)] * 2)
    y1, y3, _ = lax.optimization_barrier((shift(own, "y", 1), shift(own, "y", 3), tok_z))
    y2 = shift(after(own, y1, y3), "y", 2)
    tok_x = [shift(tok_z, "x", s) for s in (1, 2, 3)]
    y2 = after(y2, *tok_x)
    cot_z = after(cot_z, *tok_x)
    tok_x = [tok_z] + tok_x
    cot_x = [cot_z] + [shift(cot_z, "x", s) for s in (1, 2, 3)]
    by_y = [own, y1, y2, y3]
    weights = by_y + [swap(piece, "c") for piece in by_y]

    x_scratch = [pltpu.VMEM((4, 4, 128, 256), BF16)]
    send, tok_all = call(
        forward_products_kernel,
        ids,
        [*tok_x, *weights, gain],
        [ANY] * 12 + [VMEM],
        [((272, 768), BF16), ((256, 2048), BF16)],
        x_scratch + [pltpu.VMEM((2, 8, 256, 384), BF16), dma((4,)), dma((8,))],
        20,
    )
    d_send, cot_all = call(
        backward_products_kernel,
        ids,
        [*cot_x, *weights],
        [ANY] * 12,
        [((256, 384), BF16), ((256, 2048), BF16)],
        x_scratch + [pltpu.VMEM((1, 8, 256, 384), BF16), dma((4,)), dma((8,))],
        16,
    )
    kept, sent, acts, scale, tail = call(
        gradients_kernel,
        ids,
        [send, swap(send, "zh"), d_send, swap(d_send, "zh"), tok_all, cot_all],
        [VMEM] * 6,
        [((3, 4, 256, 384), BF16)] * 2
        + [((256, 1152), BF16), ((128, 128), F32), ((2, 16, 256), BF16)],
        (),
        24,
        1 << 31,
    )
    parts = call(
        outputs_kernel,
        ids,
        [acts, tail, *weights],
        [VMEM] * 2 + [ANY] * 8,
        [((4, 272, 256), BF16)] * 4,
        [pltpu.VMEM((3, 8, 256, 384), BF16), dma((8,))],
        24,
        1 << 30,
    )
    sums = call(
        core_sum_kernel, ids, [kept, swap(sent, "c")], [VMEM] * 2, [((3, 256, 384), BF16)] * 4, (), 16
    )
    near = [shift(sums[1], "y", -1), shift(sums[3], "y", 1)]
    far = shift(sums[2], "y", 2)
    parts = [parts[0]] + [shift(parts[s], "x", -s) for s in (1, 2, 3)]
    blocks = call(x_sum_kernel, ids, parts, [VMEM] * 4, [((272, 256), BF16)] * 4)
    blocks = [*blocks[:2]] + [after(block, *near) for block in blocks[2:]]
    blocks = [
        lax.ppermute(blocks[k], ("zh", "zl"), [(t, s) for s, t in z_pairs(k)]) for k in range(4)
    ]
    mixed_out, d_tokens = call(
        finish_kernel,
        ids,
        [*blocks, tokens, out_cotangent, gain, scale],
        [VMEM] * 8,
        [((128, 256), BF16), ((128, 256), F32)],
    )
    grad_gate, grad_up, grad_down = call(
        grads_sum_kernel,
        ids,
        [sums[0], near[0], far, near[1]],
        [VMEM] * 4,
        [((256, 384), F32), ((256, 384), F32), ((384, 256), F32)],
        (),
        16,
    )
    return (mixed_out, d_tokens, grad_gate, grad_up, grad_down)


def solution(mesh):
    split = Mesh(mesh.devices.reshape(2, 4, 2, 4, 4), ("zh", "y", "c", "zl", "x"))
    grp, dev = ("zh", "y", "c"), ("zl", "x")
    in_specs = (P(grp, dev), P(), P(grp, dev), P(grp, dev), P(dev, grp), P(grp, dev))
    out_specs = (P(grp, dev), P(grp, dev), P(grp, dev), P(grp, dev), P(dev, grp))
    return jax.shard_map(
        on_device, mesh=split, in_specs=in_specs, out_specs=out_specs, check_vma=False
    )
```

time: 187 us -> 155 us (0.83)
  waiting for transfers between devices: 107 us -> 66.1 us
  starting transfers between devices: 53.8 us -> 62.1 us
  other arithmetic: 3.79 us -> 0 us
  Pallas kernels: 16.9 us -> 19.9 us
    ppermute x12 -> x15, waiting for transfers between devices: 51.3 us -> 32.3 us  [shift(): return lax.ppermute(array, axis, [(i, (i + by) % 4) for i in range(4)])]
    ppermute x7, waiting for transfers between devices: 31.3 us -> 13.9 us  [swap(): return lax.ppermute(array, axis, [(0, 1), (1, 0)])]
    ppermute x4, waiting for transfers between devices: 24.3 us -> 12.7 us  [on_device(): lax.ppermute(blocks[k], ('zh', 'zl'), [(t, s) for s, t in z_pairs(k)])]
    ppermute x4, starting transfers between devices: 3.87 us -> 14.4 us  [on_device(): lax.ppermute(blocks[k], ('zh', 'zl'), [(t, s) for s, t in z_pairs(k)])]
    ppermute x4, waiting for transfers between devices: 0.14 us -> 7.21 us  [on_device(): by_z = [lax.ppermute(pair, ('zh', 'zl'), z_pairs(k)) for k in range(4)]]
    ppermute x7, starting transfers between devices: 25 us -> 21.2 us  [swap(): return lax.ppermute(array, axis, [(0, 1), (1, 0)])]
    another operation x3 -> x0, other arithmetic: 3.79 us -> none  [the longest x1 1.79 us: on_device(): jnp.stack([lax.ppermute(pair, ('zh', 'zl'), z_pairs(k)) for k in range(4)])]
    pallas_call x8 -> x10, Pallas kernels: 16.9 us -> 19.9 us  [call(): pl.pallas_call(body, out_shape=[jax.ShapeDtypeStruct(s, d) for s, d in ou...]
  transfers between devices with their start and end apart: 27 -> 30, of which waited for: 13 -> 13; matrix products, arithmetic and copies ran while one was open for 2% -> 0% of each run, Pallas kernels for 4% -> 9%
where the time goes in v1:
time: 155 us; the launch traced here: 154 us
  waiting for transfers between devices  66.1 us (43%)
  starting transfers between devices  62.1 us (40%)
  Pallas kernels  19.9 us (13%)
  local copies, waits for them, and re-layouts  5.28 us (3%)
    ppermute x15, waiting for transfers between devices, shift(): return lax.ppermute(array, axis, [(i, (i + by) % 4) for i in range(4)])  32.3 us
    ppermute x7, starting transfers between devices, swap(): return lax.ppermute(array, axis, [(0, 1), (1, 0)])  21.2 us
    pallas_call x10, Pallas kernels, call(): pl.pallas_call(body, out_shape=[jax.ShapeDtypeStruct(s, d) for s, d in ou...  19.9 us
    ppermute x15, starting transfers between devices, shift(): return lax.ppermute(array, axis, [(i, (i + by) % 4) for i in range(4)])  15.7 us
    ppermute x4, starting transfers between devices, on_device(): lax.ppermute(blocks[k], ('zh', 'zl'), [(t, s) for s, t in z_pairs(k)])  14.4 us
    ppermute x7, waiting for transfers between devices, swap(): return lax.ppermute(array, axis, [(0, 1), (1, 0)])  13.9 us
    ppermute x4, waiting for transfers between devices, on_device(): lax.ppermute(blocks[k], ('zh', 'zl'), [(t, s) for s, t in z_pairs(k)])  12.7 us
    ppermute x4, starting transfers between devices, on_device(): by_z = [lax.ppermute(pair, ('zh', 'zl'), z_pairs(k)) for k in range(4)]  10.9 us
  transfers between devices with their start and end apart: 30, of which 13 were waited for; matrix products, arithmetic and copies ran while one was open for 0% of the time, Pallas kernels for 9%

profile of v1, /device:TPU:97, one launch (start us, length us, event | category | flops | bytes accessed | tf_op | source)
XLA Modules:
  0.0 154.3 jit_solution(5171445745443221915)
XLA Ops:
  5.2 1.6 %shard_map.101 = (bf16[2,128,256]{2,1,0:T(8,128)(2,1)S(1)}, bf16[3,256,384]{2,1,0:T(8,128)(2,1)S(1)}) custom-call(s32[5]{0:T(128)S(1)} %stack.23.ids, bf16[128,256]{1,0:T(8,128)(2,1)S(1)} %copy-done, bf16[128,256]{1,0:T(8,128)(2,1)S(1)} %copy-done.2, bf16[256,384]{1,0:T(8,128)(2,1)S(1)} %copy-done.4, bf16[256,384]{1,0:T(8,128)(2,1)S(1)} %copy-done.5, ...), custom_call_target="tpu_custom_call" | custom-call | bytes 1441792 | tf_op jit(solution)/shard_map/pallas_call | solution.py:53
  6.8 2.8 %collective-permute-start.8 = (bf16[3,256,384]{2,1,0:T(8,128)(2,1)S(1)}, bf16[3,256,384]{2,1,0:T(8,128)(2,1)S(1)}, u32[]{:S(2)}, u32[]{:S(2)}) collective-permute-start(bf16[3,256,384]{2,1,0:T(8,128)(2,1)S(1)} %get-tuple-element.47.refs_4_.refs_0_), channel_id=1, source_target_pairs={{0,96},{32,0},{64,32},{96,64},{1,97},{33,1},{65,33},{97,65},{2,98}... | collective-permute-start | bytes 1769480 | tf_op jit(solution)/shard_map/ppermute | solution.py:28
  9.6 3.8 %collective-permute-start.3 = (bf16[2,128,256]{2,1,0:T(8,128)(2,1)S(1)}, bf16[2,128,256]{2,1,0:T(8,128)(2,1)S(1)}, u32[]{:S(2)}, u32[]{:S(2)}) collective-permute-start(bf16[2,128,256]{2,1,0:T(8,128)(2,1)S(1)} %get-tuple-element.42), channel_id=1, source_target_pairs={{0,12},{4,8},{8,140},{12,136},{128,4},{132,0},{136,132},{140,128},... | collective-permute-start | bytes 393224 | tf_op jit(solution)/shard_map/ppermute | solution.py:276
  13.4 2.1 %collective-permute-start.2 = (bf16[2,128,256]{2,1,0:T(8,128)(2,1)S(1)}, bf16[2,128,256]{2,1,0:T(8,128)(2,1)S(1)}, u32[]{:S(2)}, u32[]{:S(2)}) collective-permute-start(bf16[2,128,256]{2,1,0:T(8,128)(2,1)S(1)} %get-tuple-element.42), channel_id=1, source_target_pairs={{0,8},{4,12},{8,136},{12,140},{128,0},{132,4},{136,128},{140,132},... | collective-permute-start | bytes 393224 | tf_op jit(solution)/shard_map/ppermute | solution.py:276
  15.5 5.0 %collective-permute-start = (bf16[2,128,256]{2,1,0:T(8,128)(2,1)S(1)}, bf16[2,128,256]{2,1,0:T(8,128)(2,1)S(1)}, u32[]{:S(2)}, u32[]{:S(2)}) collective-permute-start(bf16[2,128,256]{2,1,0:T(8,128)(2,1)S(1)} %get-tuple-element.42), channel_id=1, source_target_pairs={{0,0},{4,4},{8,128},{12,132},{128,8},{132,12},{136,136},{140,140},... | collective-permute-start | bytes 393224 | tf_op jit(solution)/shard_map/ppermute | solution.py:276
  20.5 2.3 %collective-permute-done.2.p2 = bf16[2,128,256]{2,1,0:T(8,128)(2,1)S(1)} collective-permute-done((bf16[2,128,256]{2,1,0:T(8,128)(2,1)S(1)}, bf16[2,128,256]{2,1,0:T(8,128)(2,1)S(1)}, u32[]{:S(2)}, u32[]{:S(2)}) %collective-permute-start.2) | collective-permute-done | bytes 131104 | tf_op jit(solution)/shard_map/ppermute | solution.py:276
  22.8 1.6 %collective-permute-done.1.p1 = bf16[2,128,256]{2,1,0:T(8,128)(2,1)S(1)} collective-permute-done((bf16[2,128,256]{2,1,0:T(8,128)(2,1)S(1)}, bf16[2,128,256]{2,1,0:T(8,128)(2,1)S(1)}, u32[]{:S(2)}, u32[]{:S(2)}) %collective-permute-start.1) | collective-permute-done | bytes 131104 | tf_op jit(solution)/shard_map/ppermute | solution.py:276
  24.4 3.3 %collective-permute-done.p0 = bf16[2,128,256]{2,1,0:T(8,128)(2,1)S(1)} collective-permute-done((bf16[2,128,256]{2,1,0:T(8,128)(2,1)S(1)}, bf16[2,128,256]{2,1,0:T(8,128)(2,1)S(1)}, u32[]{:S(2)}, u32[]{:S(2)}) %collective-permute-start) | collective-permute-done | bytes 131104 | tf_op jit(solution)/shard_map/ppermute | solution.py:276
  28.3 1.7 %collective-permute-start.9 = (bf16[3,256,384]{2,1,0:T(8,128)(2,1)S(1)}, bf16[3,256,384]{2,1,0:T(8,128)(2,1)S(1)}, u32[]{:S(2)}, u32[]{:S(2)}) collective-permute-start(bf16[3,256,384]{2,1,0:T(8,128)(2,1)S(1)} %get-tuple-element.47.refs_4_.refs_0_), channel_id=1, source_target_pairs={{0,64},{32,96},{64,0},{96,32},{1,65},{33,97},{65,1},{97,33},{2,66}... | collective-permute-start | bytes 1769480 | tf_op jit(solution)/shard_map/ppermute | solution.py:28
  30.0 2.5 %collective-permute-start.6 = (bf16[4,128,256]{2,1,0:T(8,128)(2,1)S(1)}, bf16[4,128,256]{2,1,0:T(8,128)(2,1)S(1)}, u32[]{:S(2)}, u32[]{:S(2)}) collective-permute-start(bf16[4,128,256]{2,1,0:T(8,128)(2,1)S(1)} %get-tuple-element.43.refs_0_), channel_id=1, source_target_pairs={{0,3},{1,0},{2,1},{3,2},{4,7},{5,4},{6,5},{7,6},{8,11},{9,8},{10,9... | collective-permute-start | bytes 786440 | tf_op jit(solution)/shard_map/ppermute | solution.py:28
  33.6 5.0 %collective-permute-start.10 = (bf16[3,256,384]{2,1,0:T(8,128)(2,1)S(1)}, bf16[3,256,384]{2,1,0:T(8,128)(2,1)S(1)}, u32[]{:S(2)}, u32[]{:S(2)}) collective-permute-start(bf16[3,256,384]{2,1,0:T(8,128)(2,1)S(1)} %get-tuple-element.47.refs_4_.refs_0_), channel_id=1, source_target_pairs={{0,16},{16,0},{1,17},{17,1},{2,18},{18,2},{3,19},{19,3},{4,20},{20... | collective-permute-start | bytes 1769480 | tf_op jit(solution)/shard_map/ppermute | solution.py:32
  39.1 5.6 %collective-permute-start.11 = (bf16[3,256,384]{2,1,0:T(8,128)(2,1)S(1)}, bf16[3,256,384]{2,1,0:T(8,128)(2,1)S(1)}, u32[]{:S(2)}, u32[]{:S(2)}) collective-permute-start(bf16[3,256,384]{2,1,0:T(8,128)(2,1)S(1)} %collective-permute-done.7.refs_5_.refs_1_), channel_id=1, source_target_pairs={{0,16},{16,0},{1,17},{17,1},{2,18},{18,2},{3,19},{19,3},{4,20},{20... | collective-permute-start | bytes 1769480 | tf_op jit(solution)/shard_map/ppermute | solution.py:32
  45.7 2.7 %collective-permute-start.12 = (bf16[3,256,384]{2,1,0:T(8,128)(2,1)S(1)}, bf16[3,256,384]{2,1,0:T(8,128)(2,1)S(1)}, u32[]{:S(2)}, u32[]{:S(2)}) collective-permute-start(bf16[3,256,384]{2,1,0:T(8,128)(2,1)S(1)} %collective-permute-done.9.refs_6_.refs_2_), channel_id=1, source_target_pairs={{0,16},{16,0},{1,17},{17,1},{2,18},{18,2},{3,19},{19,3},{4,20},{20... | collective-permute-start | bytes 1769480 | tf_op jit(solution)/shard_map/ppermute | solution.py:32
  50.8 3.2 %shard_map.103 = (bf16[272,768]{1,0:T(8,128)(2,1)S(1)}, bf16[256,2048]{1,0:T(8,128)(2,1)S(1)}) custom-call(s32[5]{0:T(128)S(1)} %stack.23.ids, bf16[4,128,256]{2,1,0:T(8,128)(2,1)S(1)} %get-tuple-element.43.refs_0_, bf16[4,128,256]{2,1,0:T(8,128)(2,1)S(1)} %collective-permute-done.4.refs_1_, bf16[4,128,256]{2,1,0:T(8,128)(2,1)S(1)} %collective-permute-done.5.refs_2_, ...), custom_call_target="tpu_custom_call" | custom-call | bytes 7249920 | tf_op jit(solution)/shard_map/pallas_call | solution.py:53
  54.1 3.0 %collective-permute-start.14 = (bf16[272,768]{1,0:T(8,128)(2,1)S(1)}, bf16[272,768]{1,0:T(8,128)(2,1)S(1)}, u32[]{:S(2)}, u32[]{:S(2)}) collective-permute-start(bf16[272,768]{1,0:T(8,128)(2,1)S(1)} %get-tuple-element.49.mine), channel_id=1, source_target_pairs={{0,128},{128,0},{1,129},{129,1},{2,130},{130,2},{3,131},{131,3},{4... | collective-permute-start | bytes 1253384 | tf_op jit(solution)/shard_map/ppermute | solution.py:32
  57.9 6.2 %collective-permute-done.15.refs_1_ = bf16[4,128,256]{2,1,0:T(8,128)(2,1)S(1)} collective-permute-done((bf16[4,128,256]{2,1,0:T(8,128)(2,1)S(1)}, bf16[4,128,256]{2,1,0:T(8,128)(2,1)S(1)}, u32[]{:S(2)}, u32[]{:S(2)}) %collective-permute-start.15) | collective-permute-done | bytes 262176 | tf_op jit(solution)/shard_map/ppermute | solution.py:28
  64.1 3.6 %shard_map.104 = (bf16[256,384]{1,0:T(8,128)(2,1)S(1)}, bf16[256,2048]{1,0:T(8,128)(2,1)S(1)}) custom-call(s32[5]{0:T(128)S(1)} %stack.23.ids, bf16[4,128,256]{2,1,0:T(8,128)(2,1)S(1)} %get-tuple-element.51.refs_0_, bf16[4,128,256]{2,1,0:T(8,128)(2,1)S(1)} %collective-permute-done.15.refs_1_, bf16[4,128,256]{2,1,0:T(8,128)(2,1)S(1)} %collective-permute-done.16.refs_2_, ...), custom_call_target="tpu_custom_call" | custom-call | bytes 7012352 | tf_op jit(solution)/shard_map/pallas_call | solution.py:53
  67.8 3.0 %collective-permute-start.18 = (bf16[256,384]{1,0:T(8,128)(2,1)S(1)}, bf16[256,384]{1,0:T(8,128)(2,1)S(1)}, u32[]{:S(2)}, u32[]{:S(2)}) collective-permute-start(bf16[256,384]{1,0:T(8,128)(2,1)S(1)} %get-tuple-element.52.d_mine), channel_id=1, source_target_pairs={{0,128},{128,0},{1,129},{129,1},{2,130},{130,2},{3,131},{131,3},{4... | collective-permute-start | bytes 589832 | tf_op jit(solution)/shard_map/ppermute | solution.py:32
  70.8 12.6 %collective-permute-done.18.d_recv = bf16[256,384]{1,0:T(8,128)(2,1)S(1)} collective-permute-done((bf16[256,384]{1,0:T(8,128)(2,1)S(1)}, bf16[256,384]{1,0:T(8,128)(2,1)S(1)}, u32[]{:S(2)}, u32[]{:S(2)}) %collective-permute-start.18) | collective-permute-done | bytes 196640 | tf_op jit(solution)/shard_map/ppermute | solution.py:32
  83.4 3.0 %shard_map.105 = (bf16[3,4,256,384]{3,2,1,0:T(8,128)(2,1)S(1)}, bf16[3,4,256,384]{3,2,1,0:T(8,128)(2,1)S(1)}, bf16[256,1152]{1,0:T(8,128)(2,1)S(1)}, f32[128,128]{1,0:T(8,128)S(1)}, bf16[2,16,256]{2,1,0:T(8,128)(2,1)S(1)}) custom-call(s32[5]{0:T(128)S(1)} %stack.23.ids, bf16[272,768]{1,0:T(8,128)(2,1)S(1)} %get-tuple-element.49.mine, ...), custom_call_target="tpu_custom_call" | custom-call | flops 2147483648 | bytes 8683520 | tf_op jit(solution)/shard_map/pallas_call | solution.py:53
  87.2 2.8 %shard_map.106 = (bf16[4,272,256]{2,1,0:T(8,128)(2,1)S(1)}, bf16[4,272,256]{2,1,0:T(8,128)(2,1)S(1)}, bf16[4,272,256]{2,1,0:T(8,128)(2,1)S(1)}, bf16[4,272,256]{2,1,0:T(8,128)(2,1)S(1)}) custom-call(s32[5]{0:T(128)S(1)} %stack.23.ids, bf16[256,1152]{1,0:T(8,128)(2,1)S(1)} %get-tuple-element.55.acts, bf16[2,16,256]{2,1,0:T(8,128)(2,1)S(1)} %get-tuple-element.56.tail, ...), custom_call_target="tpu_custom_call" | custom-call | flops 1073741824 | bytes 7553024 | tf_op jit(solution)/shard_map/pallas_call | solution.py:53
  92.5 2.6 %collective-permute-start.25 = (bf16[3,256,384]{2,1,0:T(8,128)(2,1)S(1)}, bf16[3,256,384]{2,1,0:T(8,128)(2,1)S(1)}, u32[]{:S(2)}, u32[]{:S(2)}) collective-permute-start(bf16[3,256,384]{2,1,0:T(8,128)(2,1)S(1)} %get-tuple-element.66), channel_id=1, source_target_pairs={{0,96},{32,0},{64,32},{96,64},{1,97},{33,1},{65,33},{97,65},{2,98}... | collective-permute-start | bytes 1769480 | tf_op jit(solution)/shard_map/ppermute | solution.py:28
  97.0 7.4 %collective-permute-done.19.refs_1_ = bf16[4,272,256]{2,1,0:T(8,128)(2,1)S(1)} collective-permute-done((bf16[4,272,256]{2,1,0:T(8,128)(2,1)S(1)}, bf16[4,272,256]{2,1,0:T(8,128)(2,1)S(1)}, u32[]{:S(2)}, u32[]{:S(2)}) %collective-permute-start.19) | collective-permute-done | bytes 557088 | tf_op jit(solution)/shard_map/ppermute | solution.py:28
  105.7 4.6 %collective-permute-done.20.refs_2_ = bf16[4,272,256]{2,1,0:T(8,128)(2,1)S(1)} collective-permute-done((bf16[4,272,256]{2,1,0:T(8,128)(2,1)S(1)}, bf16[4,272,256]{2,1,0:T(8,128)(2,1)S(1)}, u32[]{:S(2)}, u32[]{:S(2)}) %collective-permute-start.20) | collective-permute-done | bytes 557088 | tf_op jit(solution)/shard_map/ppermute | solution.py:28
  110.3 12.8 %collective-permute-done.21.refs_3_ = bf16[4,272,256]{2,1,0:T(8,128)(2,1)S(1)} collective-permute-done((bf16[4,272,256]{2,1,0:T(8,128)(2,1)S(1)}, bf16[4,272,256]{2,1,0:T(8,128)(2,1)S(1)}, u32[]{:S(2)}, u32[]{:S(2)}) %collective-permute-start.21) | collective-permute-done | bytes 557088 | tf_op jit(solution)/shard_map/ppermute | solution.py:28
  123.9 8.6 %collective-permute-start.22 = (bf16[272,256]{1,0:T(8,128)(2,1)S(1)}, bf16[272,256]{1,0:T(8,128)(2,1)S(1)}, u32[]{:S(2)}, u32[]{:S(2)}) collective-permute-start(bf16[272,256]{1,0:T(8,128)(2,1)S(1)} %get-tuple-element.61), channel_id=1, source_target_pairs={{0,0},{4,4},{128,8},{132,12},{8,128},{12,132},{136,136},{140,140},... | collective-permute-start | bytes 417800 | tf_op jit(solution)/shard_map/ppermute | solution.py:337
  132.6 1.8 %collective-permute-start.23 = (bf16[272,256]{1,0:T(8,128)(2,1)S(1)}, bf16[272,256]{1,0:T(8,128)(2,1)S(1)}, u32[]{:S(2)}, u32[]{:S(2)}) collective-permute-start(bf16[272,256]{1,0:T(8,128)(2,1)S(1)} %get-tuple-element.62), channel_id=1, source_target_pairs={{4,0},{0,4},{132,8},{128,12},{12,128},{8,132},{140,136},{136,140},... | collective-permute-start | bytes 417800 | tf_op jit(solution)/shard_map/ppermute | solution.py:337
  134.4 3.9 %collective-permute-start.28 = (bf16[272,256]{1,0:T(8,128)(2,1)S(1)}, bf16[272,256]{1,0:T(8,128)(2,1)S(1)}, u32[]{:S(2)}, u32[]{:S(2)}) collective-permute-start(bf16[272,256]{1,0:T(8,128)(2,1)S(1)} %get-tuple-element.70), channel_id=1, source_target_pairs={{12,0},{8,4},{140,8},{136,12},{4,128},{0,132},{132,136},{128,140},... | collective-permute-start | bytes 417800 | tf_op jit(solution)/shard_map/ppermute | solution.py:337
  138.3 1.8 %shard_map.110 = (f32[256,384]{1,0:T(8,128)}, f32[256,384]{1,0:T(8,128)}, f32[384,256]{1,0:T(8,128)}) custom-call(s32[5]{0:T(128)S(1)} %stack.23.ids, bf16[3,256,384]{2,1,0:T(8,128)(2,1)S(1)} %get-tuple-element.74.p0, bf16[3,256,384]{2,1,0:T(8,128)(2,1)S(1)} %collective-permute-done.25.p1, bf16[3,256,384]{2,1,0:T(8,128)(2,1)S(1)} %collective-permute-done.29.p2, ...), custom_call_target="tpu_custom_call" | custom-call | bytes 2949120 | tf_op jit(solution)/shard_map/pallas_call | solution.py:53
  140.1 8.8 %collective-permute-done.23.p1 = bf16[272,256]{1,0:T(8,128)(2,1)S(1)} collective-permute-done((bf16[272,256]{1,0:T(8,128)(2,1)S(1)}, bf16[272,256]{1,0:T(8,128)(2,1)S(1)}, u32[]{:S(2)}, u32[]{:S(2)}) %collective-permute-start.23) | collective-permute-done | bytes 139296 | tf_op jit(solution)/shard_map/ppermute | solution.py:337
  148.9 3.9 %collective-permute-done.28.p3 = bf16[272,256]{1,0:T(8,128)(2,1)S(1)} collective-permute-done((bf16[272,256]{1,0:T(8,128)(2,1)S(1)}, bf16[272,256]{1,0:T(8,128)(2,1)S(1)}, u32[]{:S(2)}, u32[]{:S(2)}) %collective-permute-start.28) | collective-permute-done | bytes 139296 | tf_op jit(solution)/shard_map/ppermute | solution.py:337
  152.9 1.4 shard_map.109
  (57 shorter events, 18.3 us)
Async XLA Ops:
  6.8 21.5 %collective-permute-start.8 = (bf16[3,256,384]{2,1,0:T(8,128)(2,1)S(1)}, bf16[3,256,384]{2,1,0:T(8,128)(2,1)S(1)}, u32[]{:S(2)}, u32[]{:S(2)}) collective-permute-start(bf16[3,256,384]{2,1,0:T(8,128)(2,1)S(1)} %get-tuple-element.47.refs_4_.refs_0_), channel_id=1, source_target_pairs={{0,96},{32,0},{64,32},{96,64},{1,97},{33,1},{65,33},{97,65},{2,98}... | collective-permute-start | bytes 1769480 | tf_op jit(solution)/shard_map/ppermute | solution.py:28
  9.6 18.7 %collective-permute-start.7 = (bf16[3,256,384]{2,1,0:T(8,128)(2,1)S(1)}, bf16[3,256,384]{2,1,0:T(8,128)(2,1)S(1)}, u32[]{:S(2)}, u32[]{:S(2)}) collective-permute-start(bf16[3,256,384]{2,1,0:T(8,128)(2,1)S(1)} %get-tuple-element.47.refs_4_.refs_0_), channel_id=1, source_target_pairs={{0,32},{32,64},{64,96},{96,0},{1,33},{33,65},{65,97},{97,1},{2,34}... | collective-permute-start | bytes 1769480 | tf_op jit(solution)/shard_map/ppermute | solution.py:28
  9.6 5.8 %collective-permute-start.3 = (bf16[2,128,256]{2,1,0:T(8,128)(2,1)S(1)}, bf16[2,128,256]{2,1,0:T(8,128)(2,1)S(1)}, u32[]{:S(2)}, u32[]{:S(2)}) collective-permute-start(bf16[2,128,256]{2,1,0:T(8,128)(2,1)S(1)} %get-tuple-element.42), channel_id=1, source_target_pairs={{0,12},{4,8},{8,140},{12,136},{128,4},{132,0},{136,132},{140,128},... | collective-permute-start | bytes 393224 | tf_op jit(solution)/shard_map/ppermute | solution.py:276
  13.4 9.4 %collective-permute-start.2 = (bf16[2,128,256]{2,1,0:T(8,128)(2,1)S(1)}, bf16[2,128,256]{2,1,0:T(8,128)(2,1)S(1)}, u32[]{:S(2)}, u32[]{:S(2)}) collective-permute-start(bf16[2,128,256]{2,1,0:T(8,128)(2,1)S(1)} %get-tuple-element.42), channel_id=1, source_target_pairs={{0,8},{4,12},{8,136},{12,140},{128,0},{132,4},{136,128},{140,132},... | collective-permute-start | bytes 393224 | tf_op jit(solution)/shard_map/ppermute | solution.py:276
  15.5 8.9 %collective-permute-start.1 = (bf16[2,128,256]{2,1,0:T(8,128)(2,1)S(1)}, bf16[2,128,256]{2,1,0:T(8,128)(2,1)S(1)}, u32[]{:S(2)}, u32[]{:S(2)}) collective-permute-start(bf16[2,128,256]{2,1,0:T(8,128)(2,1)S(1)} %get-tuple-element.42), channel_id=1, source_target_pairs={{0,4},{4,0},{8,132},{12,128},{128,12},{132,8},{136,140},{140,136},... | collective-permute-start | bytes 393224 | tf_op jit(solution)/shard_map/ppermute | solution.py:276
  15.5 12.2 %collective-permute-start = (bf16[2,128,256]{2,1,0:T(8,128)(2,1)S(1)}, bf16[2,128,256]{2,1,0:T(8,128)(2,1)S(1)}, u32[]{:S(2)}, u32[]{:S(2)}) collective-permute-start(bf16[2,128,256]{2,1,0:T(8,128)(2,1)S(1)} %get-tuple-element.42), channel_id=1, source_target_pairs={{0,0},{4,4},{8,128},{12,132},{128,8},{132,12},{136,136},{140,140},... | collective-permute-start | bytes 393224 | tf_op jit(solution)/shard_map/ppermute | solution.py:276
  28.3 17.4 %collective-permute-start.9 = (bf16[3,256,384]{2,1,0:T(8,128)(2,1)S(1)}, bf16[3,256,384]{2,1,0:T(8,128)(2,1)S(1)}, u32[]{:S(2)}, u32[]{:S(2)}) collective-permute-start(bf16[3,256,384]{2,1,0:T(8,128)(2,1)S(1)} %get-tuple-element.47.refs_4_.refs_0_), channel_id=1, source_target_pairs={{0,64},{32,96},{64,0},{96,32},{1,65},{33,97},{65,1},{97,33},{2,66}... | collective-permute-start | bytes 1769480 | tf_op jit(solution)/shard_map/ppermute | solution.py:28
  30.0 9.0 %collective-permute-start.6 = (bf16[4,128,256]{2,1,0:T(8,128)(2,1)S(1)}, bf16[4,128,256]{2,1,0:T(8,128)(2,1)S(1)}, u32[]{:S(2)}, u32[]{:S(2)}) collective-permute-start(bf16[4,128,256]{2,1,0:T(8,128)(2,1)S(1)} %get-tuple-element.43.refs_0_), channel_id=1, source_target_pairs={{0,3},{1,0},{2,1},{3,2},{4,7},{5,4},{6,5},{7,6},{8,11},{9,8},{10,9... | collective-permute-start | bytes 786440 | tf_op jit(solution)/shard_map/ppermute | solution.py:28
  32.5 12.2 %collective-permute-start.5 = (bf16[4,128,256]{2,1,0:T(8,128)(2,1)S(1)}, bf16[4,128,256]{2,1,0:T(8,128)(2,1)S(1)}, u32[]{:S(2)}, u32[]{:S(2)}) collective-permute-start(bf16[4,128,256]{2,1,0:T(8,128)(2,1)S(1)} %get-tuple-element.43.refs_0_), channel_id=1, source_target_pairs={{0,2},{1,3},{2,0},{3,1},{4,6},{5,7},{6,4},{7,5},{8,10},{9,11},{10,... | collective-permute-start | bytes 786440 | tf_op jit(solution)/shard_map/ppermute | solution.py:28
  33.0 12.7 %collective-permute-start.4 = (bf16[4,128,256]{2,1,0:T(8,128)(2,1)S(1)}, bf16[4,128,256]{2,1,0:T(8,128)(2,1)S(1)}, u32[]{:S(2)}, u32[]{:S(2)}) collective-permute-start(bf16[4,128,256]{2,1,0:T(8,128)(2,1)S(1)} %get-tuple-element.43.refs_0_), channel_id=1, source_target_pairs={{0,1},{1,2},{2,3},{3,0},{4,5},{5,6},{6,7},{7,4},{8,9},{9,10},{10,1... | collective-permute-start | bytes 786440 | tf_op jit(solution)/shard_map/ppermute | solution.py:28
  33.6 15.1 %collective-permute-start.10 = (bf16[3,256,384]{2,1,0:T(8,128)(2,1)S(1)}, bf16[3,256,384]{2,1,0:T(8,128)(2,1)S(1)}, u32[]{:S(2)}, u32[]{:S(2)}) collective-permute-start(bf16[3,256,384]{2,1,0:T(8,128)(2,1)S(1)} %get-tuple-element.47.refs_4_.refs_0_), channel_id=1, source_target_pairs={{0,16},{16,0},{1,17},{17,1},{2,18},{18,2},{3,19},{19,3},{4,20},{20... | collective-permute-start | bytes 1769480 | tf_op jit(solution)/shard_map/ppermute | solution.py:32
  39.1 10.2 %collective-permute-start.11 = (bf16[3,256,384]{2,1,0:T(8,128)(2,1)S(1)}, bf16[3,256,384]{2,1,0:T(8,128)(2,1)S(1)}, u32[]{:S(2)}, u32[]{:S(2)}) collective-permute-start(bf16[3,256,384]{2,1,0:T(8,128)(2,1)S(1)} %collective-permute-done.7.refs_5_.refs_1_), channel_id=1, source_target_pairs={{0,16},{16,0},{1,17},{17,1},{2,18},{18,2},{3,19},{19,3},{4,20},{20... | collective-permute-start | bytes 1769480 | tf_op jit(solution)/shard_map/ppermute | solution.py:32
  44.7 5.4 %collective-permute-start.13 = (bf16[3,256,384]{2,1,0:T(8,128)(2,1)S(1)}, bf16[3,256,384]{2,1,0:T(8,128)(2,1)S(1)}, u32[]{:S(2)}, u32[]{:S(2)}) collective-permute-start(bf16[3,256,384]{2,1,0:T(8,128)(2,1)S(1)} %collective-permute-done.8.refs_7_.refs_3_), channel_id=1, source_target_pairs={{0,16},{16,0},{1,17},{17,1},{2,18},{18,2},{3,19},{19,3},{4,20},{20... | collective-permute-start | bytes 1769480 | tf_op jit(solution)/shard_map/ppermute | solution.py:32
  45.7 4.4 %collective-permute-start.12 = (bf16[3,256,384]{2,1,0:T(8,128)(2,1)S(1)}, bf16[3,256,384]{2,1,0:T(8,128)(2,1)S(1)}, u32[]{:S(2)}, u32[]{:S(2)}) collective-permute-start(bf16[3,256,384]{2,1,0:T(8,128)(2,1)S(1)} %collective-permute-done.9.refs_6_.refs_2_), channel_id=1, source_target_pairs={{0,16},{16,0},{1,17},{17,1},{2,18},{18,2},{3,19},{19,3},{4,20},{20... | collective-permute-start | bytes 1769480 | tf_op jit(solution)/shard_map/ppermute | solution.py:32
  48.4 8.7 %collective-permute-start.17 = (bf16[4,128,256]{2,1,0:T(8,128)(2,1)S(1)}, bf16[4,128,256]{2,1,0:T(8,128)(2,1)S(1)}, u32[]{:S(2)}, u32[]{:S(2)}) collective-permute-start(bf16[4,128,256]{2,1,0:T(8,128)(2,1)S(1)} %get-tuple-element.51.refs_0_), channel_id=1, source_target_pairs={{0,3},{1,0},{2,1},{3,2},{4,7},{5,4},{6,5},{7,6},{8,11},{9,8},{10,9... | collective-permute-start | bytes 786440 | tf_op jit(solution)/shard_map/ppermute | solution.py:28
  48.7 9.2 %collective-permute-start.16 = (bf16[4,128,256]{2,1,0:T(8,128)(2,1)S(1)}, bf16[4,128,256]{2,1,0:T(8,128)(2,1)S(1)}, u32[]{:S(2)}, u32[]{:S(2)}) collective-permute-start(bf16[4,128,256]{2,1,0:T(8,128)(2,1)S(1)} %get-tuple-element.51.refs_0_), channel_id=1, source_target_pairs={{0,2},{1,3},{2,0},{3,1},{4,6},{5,7},{6,4},{7,5},{8,10},{9,11},{10,... | collective-permute-start | bytes 786440 | tf_op jit(solution)/shard_map/ppermute | solution.py:28
  49.3 14.9 %collective-permute-start.15 = (bf16[4,128,256]{2,1,0:T(8,128)(2,1)S(1)}, bf16[4,128,256]{2,1,0:T(8,128)(2,1)S(1)}, u32[]{:S(2)}, u32[]{:S(2)}) collective-permute-start(bf16[4,128,256]{2,1,0:T(8,128)(2,1)S(1)} %get-tuple-element.51.refs_0_), channel_id=1, source_target_pairs={{0,1},{1,2},{2,3},{3,0},{4,5},{5,6},{6,7},{7,4},{8,9},{9,10},{10,1... | collective-permute-start | bytes 786440 | tf_op jit(solution)/shard_map/ppermute | solution.py:28
  54.1 29.3 %collective-permute-start.14 = (bf16[272,768]{1,0:T(8,128)(2,1)S(1)}, bf16[272,768]{1,0:T(8,128)(2,1)S(1)}, u32[]{:S(2)}, u32[]{:S(2)}) collective-permute-start(bf16[272,768]{1,0:T(8,128)(2,1)S(1)} %get-tuple-element.49.mine), channel_id=1, source_target_pairs={{0,128},{128,0},{1,129},{129,1},{2,130},{130,2},{3,131},{131,3},{4... | collective-permute-start | bytes 1253384 | tf_op jit(solution)/shard_map/ppermute | solution.py:32
  67.8 15.6 %collective-permute-start.18 = (bf16[256,384]{1,0:T(8,128)(2,1)S(1)}, bf16[256,384]{1,0:T(8,128)(2,1)S(1)}, u32[]{:S(2)}, u32[]{:S(2)}) collective-permute-start(bf16[256,384]{1,0:T(8,128)(2,1)S(1)} %get-tuple-element.52.d_mine), channel_id=1, source_target_pairs={{0,128},{128,0},{1,129},{129,1},{2,130},{130,2},{3,131},{131,3},{4... | collective-permute-start | bytes 589832 | tf_op jit(solution)/shard_map/ppermute | solution.py:32
  86.4 5.0 %collective-permute-start.24 = (bf16[3,4,256,384]{3,2,1,0:T(8,128)(2,1)S(1)}, bf16[3,4,256,384]{3,2,1,0:T(8,128)(2,1)S(1)}, u32[]{:S(2)}, u32[]{:S(2)}) collective-permute-start(bf16[3,4,256,384]{3,2,1,0:T(8,128)(2,1)S(1)} %get-tuple-element.65), channel_id=1, source_target_pairs={{0,16},{16,0},{1,17},{17,1},{2,18},{18,2},{3,19},{19,3},{4,20},{20... | collective-permute-start | bytes 7077896 | tf_op jit(solution)/shard_map/ppermute | solution.py:32
  90.0 14.3 %collective-permute-start.19 = (bf16[4,272,256]{2,1,0:T(8,128)(2,1)S(1)}, bf16[4,272,256]{2,1,0:T(8,128)(2,1)S(1)}, u32[]{:S(2)}, u32[]{:S(2)}) collective-permute-start(bf16[4,272,256]{2,1,0:T(8,128)(2,1)S(1)} %get-tuple-element.58), channel_id=1, source_target_pairs={{0,3},{1,0},{2,1},{3,2},{4,7},{5,4},{6,5},{7,6},{8,11},{9,8},{10,9... | collective-permute-start | bytes 1671176 | tf_op jit(solution)/shard_map/ppermute | solution.py:28
  92.5 60.4 %copy-start.1 = (bf16[128,256]{1,0:T(8,128)(2,1)S(1)}, bf16[128,256]{1,0:T(8,128)(2,1)}, u32[]{:S(2)}) copy-start(bf16[128,256]{1,0:T(8,128)(2,1)} %tokens.3) | copy-start | bytes 196612
  92.5 60.3 %copy-start.3 = (bf16[128,256]{1,0:T(8,128)(2,1)S(1)}, bf16[128,256]{1,0:T(8,128)(2,1)}, u32[]{:S(2)}) copy-start(bf16[128,256]{1,0:T(8,128)(2,1)} %cot.3) | copy-start | bytes 196612
  92.5 41.9 %collective-permute-start.25 = (bf16[3,256,384]{2,1,0:T(8,128)(2,1)S(1)}, bf16[3,256,384]{2,1,0:T(8,128)(2,1)S(1)}, u32[]{:S(2)}, u32[]{:S(2)}) collective-permute-start(bf16[3,256,384]{2,1,0:T(8,128)(2,1)S(1)} %get-tuple-element.66), channel_id=1, source_target_pairs={{0,96},{32,0},{64,32},{96,64},{1,97},{33,1},{65,33},{97,65},{2,98}... | collective-permute-start | bytes 1769480 | tf_op jit(solution)/shard_map/ppermute | solution.py:28
  95.1 39.3 %collective-permute-start.26 = (bf16[3,256,384]{2,1,0:T(8,128)(2,1)S(1)}, bf16[3,256,384]{2,1,0:T(8,128)(2,1)S(1)}, u32[]{:S(2)}, u32[]{:S(2)}) collective-permute-start(bf16[3,256,384]{2,1,0:T(8,128)(2,1)S(1)} %get-tuple-element.67), channel_id=1, source_target_pairs={{0,32},{32,64},{64,96},{96,0},{1,33},{33,65},{65,97},{97,1},{2,34}... | collective-permute-start | bytes 1769480 | tf_op jit(solution)/shard_map/ppermute | solution.py:28
  95.1 15.2 %collective-permute-start.20 = (bf16[4,272,256]{2,1,0:T(8,128)(2,1)S(1)}, bf16[4,272,256]{2,1,0:T(8,128)(2,1)S(1)}, u32[]{:S(2)}, u32[]{:S(2)}) collective-permute-start(bf16[4,272,256]{2,1,0:T(8,128)(2,1)S(1)} %get-tuple-element.59), channel_id=1, source_target_pairs={{0,2},{1,3},{2,0},{3,1},{4,6},{5,7},{6,4},{7,5},{8,10},{9,11},{10,... | collective-permute-start | bytes 1671176 | tf_op jit(solution)/shard_map/ppermute | solution.py:28
  96.3 26.8 %collective-permute-start.21 = (bf16[4,272,256]{2,1,0:T(8,128)(2,1)S(1)}, bf16[4,272,256]{2,1,0:T(8,128)(2,1)S(1)}, u32[]{:S(2)}, u32[]{:S(2)}) collective-permute-start(bf16[4,272,256]{2,1,0:T(8,128)(2,1)S(1)} %get-tuple-element.60), channel_id=1, source_target_pairs={{0,1},{1,2},{2,3},{3,0},{4,5},{5,6},{6,7},{7,4},{8,9},{9,10},{10,1... | collective-permute-start | bytes 1671176 | tf_op jit(solution)/shard_map/ppermute | solution.py:28
  104.4 34.0 %collective-permute-start.29 = (bf16[3,256,384]{2,1,0:T(8,128)(2,1)S(1)}, bf16[3,256,384]{2,1,0:T(8,128)(2,1)S(1)}, u32[]{:S(2)}, u32[]{:S(2)}) collective-permute-start(bf16[3,256,384]{2,1,0:T(8,128)(2,1)S(1)} %get-tuple-element.75), channel_id=1, source_target_pairs={{0,64},{32,96},{64,0},{96,32},{1,65},{33,97},{65,1},{97,33},{2,66}... | collective-permute-start | bytes 1769480 | tf_op jit(solution)/shard_map/ppermute | solution.py:28
  123.9 16.2 %collective-permute-start.22 = (bf16[272,256]{1,0:T(8,128)(2,1)S(1)}, bf16[272,256]{1,0:T(8,128)(2,1)S(1)}, u32[]{:S(2)}, u32[]{:S(2)}) collective-permute-start(bf16[272,256]{1,0:T(8,128)(2,1)S(1)} %get-tuple-element.61), channel_id=1, source_target_pairs={{0,0},{4,4},{128,8},{132,12},{8,128},{12,132},{136,136},{140,140},... | collective-permute-start | bytes 417800 | tf_op jit(solution)/shard_map/ppermute | solution.py:337
  132.6 16.3 %collective-permute-start.23 = (bf16[272,256]{1,0:T(8,128)(2,1)S(1)}, bf16[272,256]{1,0:T(8,128)(2,1)S(1)}, u32[]{:S(2)}, u32[]{:S(2)}) collective-permute-start(bf16[272,256]{1,0:T(8,128)(2,1)S(1)} %get-tuple-element.62), channel_id=1, source_target_pairs={{4,0},{0,4},{132,8},{128,12},{12,128},{8,132},{140,136},{136,140},... | collective-permute-start | bytes 417800 | tf_op jit(solution)/shard_map/ppermute | solution.py:337
  134.4 14.5 %collective-permute-start.27 = (bf16[272,256]{1,0:T(8,128)(2,1)S(1)}, bf16[272,256]{1,0:T(8,128)(2,1)S(1)}, u32[]{:S(2)}, u32[]{:S(2)}) collective-permute-start(bf16[272,256]{1,0:T(8,128)(2,1)S(1)} %get-tuple-element.68), channel_id=1, source_target_pairs={{8,0},{12,4},{136,8},{140,12},{0,128},{4,132},{128,136},{132,140},... | collective-permute-start | bytes 417800 | tf_op jit(solution)/shard_map/ppermute | solution.py:337
  134.4 18.4 %collective-permute-start.28 = (bf16[272,256]{1,0:T(8,128)(2,1)S(1)}, bf16[272,256]{1,0:T(8,128)(2,1)S(1)}, u32[]{:S(2)}, u32[]{:S(2)}) collective-permute-start(bf16[272,256]{1,0:T(8,128)(2,1)S(1)} %get-tuple-element.70), channel_id=1, source_target_pairs={{12,0},{8,4},{140,8},{136,12},{4,128},{0,132},{132,136},{128,140},... | collective-permute-start | bytes 417800 | tf_op jit(solution)/shard_map/ppermute | solution.py:337
  (7 other events, 65.5 us)

commit v2 on v1

v2 whole, which is shorter than its diff:
```python
import functools
import math

import jax
import jax.numpy as jnp
from jax import lax
from jax.experimental import pallas as pl
from jax.experimental.pallas import tpu as pltpu
from jax.sharding import Mesh
from jax.sharding import PartitionSpec as P

norm_epsilon = 1e-06
F32 = jnp.float32
BF16 = jnp.bfloat16
SMEM = pl.BlockSpec(memory_space=pltpu.SMEM)
VMEM = pl.BlockSpec(memory_space=pltpu.VMEM)
MIB = 1 << 20


def dot(left, right, left_dim, right_dim):
    return lax.dot_general(
        left, right, (((left_dim,), (right_dim,)), ((), ())), preferred_element_type=F32
    )


def shift(array, axis, by):
    return lax.ppermute(array, axis, [(i, (i + by) % 4) for i in range(4)])


def swap(array, axis):
    return lax.ppermute(array, axis, [(0, 1), (1, 0)])


def z_pairs(k):
    k1, k2 = k // 2, k % 2
    return [
        (4 * zs + 2 * h + l, 4 * h + 2 * (zs ^ k1) + (l ^ k2))
        for zs in range(2)
        for h in range(2)
        for l in range(2)
    ]


def split_float(value):
    head = value.astype(BF16).astype(F32)
    return head, value - head


def call(body, ids, operands, specs, outs, scratch=(), limit=8, flops=0):
    size = sum(a.size * a.dtype.itemsize for a in operands)
    size += sum(2 * math.prod(shape) for shape, _ in outs)
    return pl.pallas_call(
        body,
        out_shape=[jax.ShapeDtypeStruct(s, d) for s, d in outs],
        in_specs=[SMEM] + specs,
        out_specs=[VMEM] * len(outs),
        scratch_shapes=list(scratch),
        compiler_params=pltpu.CompilerParams(vmem_limit_bytes=limit * MIB),
        cost_estimate=pl.CostEstimate(flops=flops, bytes_accessed=size, transcendentals=0),
    )(ids, *operands)


def block_place(ids, i):
    q = lax.rem(ids[1] - i % 4 + 4, 4) * 2 + (ids[2] ^ (i // 4))
    return q, lax.rem(ids[4] - lax.rem(q, 4) + 4, 4), (ids[3] % 2) ^ (q // 4)


def stack_kernel(ids, p0, p1, p2, p3, tokens, cot):
    for k, piece in enumerate((p0, p1, p2, p3)):
        tokens[k] = piece[0]
        cot[k] = piece[1]


def forward_products_kernel(ids, *refs):
    pieces, weights, (gain, send, mixed, x_all, acc) = refs[:4], refs[4:12], refs[12:]
    for s in range(4):
        x_all[s] = pieces[s][...]
    total = [jnp.zeros((128, 1), F32) for _ in range(2)]
    for i in range(8):
        q, s, k2 = block_place(ids, i)
        row = gain[ids[0] * 8 + q]
        at = slice(256 * i, 256 * i + 256)
        for k1 in range(2):
            value = x_all[s, 2 * k1 + k2].astype(F32)
            total[k1] = total[k1] + jnp.sum(value * value, axis=1, keepdims=True)
            mixed[128 * k1 : 128 * k1 + 128, at] = (value * row).astype(BF16)
        for w in range(2):
            part = dot(mixed[:, at], weights[i][w], 1, 0)
            cols = slice(384 * w, 384 * w + 384)
            acc[:, cols] = part if i == 0 else acc[:, cols] + part
    send[:256] = acc[...].astype(BF16)
    send[256:, :] = jnp.zeros((16, 768), BF16)
    for k1 in range(2):
        head, rest = split_float(jnp.broadcast_to(total[k1], (128, 128)).T[:16])
        send[256:, 128 * k1 : 128 * k1 + 128] = head.astype(BF16)
        send[256:, 256 + 128 * k1 : 384 + 128 * k1] = rest.astype(BF16)


def backward_products_kernel(ids, *refs):
    pieces, weights, (send, mixed, x_all, acc) = refs[:4], refs[4:12], refs[12:]
    for s in range(4):
        x_all[s] = pieces[s][...]
    for i in range(8):
        _, s, k2 = block_place(ids, i)
        at = slice(256 * i, 256 * i + 256)
        for k1 in range(2):
            mixed[128 * k1 : 128 * k1 + 128, at] = x_all[s, 2 * k1 + k2]
        part = dot(mixed[:, at], weights[i][2], 1, 0)
        acc[...] = part if i == 0 else acc[...] + part
    send[...] = acc[...].astype(BF16)


def activations(mine, recv):
    tail = mine[256:257].astype(F32) + recv[256:257].astype(F32)
    total = jnp.concatenate([tail[:, :128] + tail[:, 256:384], tail[:, 128:256] + tail[:, 384:512]])
    cols = [jnp.broadcast_to(total[k : k + 1], (128, 128)).T[:, 0:1] for k in range(2)]
    inv_rms = lax.rsqrt(jnp.concatenate(cols) / 4096 + norm_epsilon)
    pre = (mine[:256].astype(F32) + recv[:256].astype(F32)) * inv_rms
    gate, up = pre[:, :384], pre[:, 384:]
    root = 0.7978845608028654
    tanh = jnp.tanh(root * (gate + 0.044715 * (gate * gate * gate)))
    cdf = 0.5 * (1.0 + tanh)
    slope = cdf + 0.5 * gate * (1.0 - tanh * tanh) * root * (1.0 + 3 * 0.044715 * (gate * gate))
    return inv_rms, gate, up, gate * cdf, slope


def scatter_blocks(ids, held, value):
    for i in range(8):
        _, s, k2 = block_place(ids, i)
        block = value(i).astype(BF16)
        held[s, k2] = block[:128]
        held[s, 2 + k2] = block[128:]


def forward_outputs_kernel(ids, mine, recv, *refs):
    weights, inner, outs, held = refs[:8], refs[8], refs[9:13], refs[13]
    _, _, up, activated, _ = activations(mine, recv)
    inner[...] = (activated * up).astype(BF16)
    scatter_blocks(ids, held, lambda i: dot(inner[...], weights[i][2], 1, 1))
    for s in range(4):
        outs[s][...] = held[s]


def gradients_kernel(
    ids, mine, recv, d_mine, d_recv, inner, tokens, cot, kept, sent, acts, scale, tail
):
    inv_rms, gate, up, activated, slope = activations(mine, recv)
    d_inner = (d_mine[...].astype(F32) + d_recv[...].astype(F32)) * inv_rms
    d_gate = (d_inner * up * slope).astype(BF16)
    d_up = (d_inner * activated).astype(BF16)
    acts[:, :384] = d_gate
    acts[:, 384:] = d_up
    own = (ids[3] // 2) ^ ids[0]
    picked = jnp.where(own == 0, inv_rms[:128], inv_rms[128:])
    scale[...] = jnp.broadcast_to(picked, (128, 128))
    tau = jnp.sum(d_gate.astype(F32) * gate + d_up.astype(F32) * up, axis=1, keepdims=True)
    for k1 in range(2):
        rows = jnp.broadcast_to(tau[128 * k1 : 128 * k1 + 128], (128, 128)).T[:16]
        head, rest = split_float(rows)
        tail[k1, :, :128] = head.astype(BF16)
        tail[k1, :, 128:] = rest.astype(BF16)
    for cc, out in ((1, sent), (0, kept)):
        for w in range(3):
            right = inner[...] if w == 2 else acts[:, 384 * w : 384 * w + 384]
            source = cot if w == 2 else tokens
            left = source[:, 1024 * cc : 1024 * cc + 1024]
            out[w] = dot(left, right, 0, 0).astype(BF16).reshape(4, 256, 384)


def backward_outputs_kernel(ids, acts, tail, *refs):
    weights, outs, held = refs[:8], refs[8:12], refs[12]

    def feat(i):
        return dot(acts[:, :384], weights[i][0], 1, 1) + dot(acts[:, 384:], weights[i][1], 1, 1)

    scatter_blocks(ids, held, feat)
    for s in range(4):
        outs[s][:, :128] = held[s]
        for k in range(4):
            outs[s][k, 128:] = tail[k // 2]


def core_sum_kernel(ids, kept, recv, *outs):
    for t in range(4):
        outs[t][...] = (kept[:, t].astype(F32) + recv[:, t].astype(F32)).astype(BF16)


def sum_refs(refs, at):
    total = refs[0][at].astype(F32)
    for ref in refs[1:]:
        total = total + ref[at].astype(F32)
    return total


def x_sum_kernel(first, ids, *refs):
    forward, backward, outs = refs[:4], refs[4:8], refs[8:]
    for k in range(2):
        outs[k][:128] = sum_refs(forward, first + k).astype(BF16)
        outs[k][128:256] = sum_refs(backward, (first + k, slice(0, 128))).astype(BF16)
        tail = sum_refs(backward, (first + k, slice(128, 144)))
        head, rest = split_float(tail[:, :128] + tail[:, 128:])
        outs[k][256:, :128] = head.astype(BF16)
        outs[k][256:, 128:] = rest.astype(BF16)


def scatter_x(parts):
    return [parts[0]] + [shift(parts[s], "x", -s) for s in (1, 2, 3)]


def finish_kernel(ids, p0, p1, p2, p3, tokens, cot, gain, scale, mixed_out, d_tokens):
    parts = (p0, p1, p2, p3)
    local = tokens[...].astype(F32)
    mixed_out[...] = (local + sum_refs(parts, slice(0, 128))).astype(BF16)
    tail = sum_refs(parts, slice(256, 272))
    tau = (tail[:, :128] + tail[:, 128:])[0:1]
    tau = jnp.broadcast_to(tau, (128, 128)).T
    coef = (scale[...] * tau * (1.0 / 4096))[:, 0:1]
    feat = sum_refs(parts, slice(128, 256)) * gain[ids[3] * 4 + ids[4]]
    d_tokens[...] = cot[...].astype(F32) + feat - local * coef


def grads_sum_kernel(ids, p0, p1, p2, p3, grad_gate, grad_up, grad_down):
    parts = (p0, p1, p2, p3)
    grad_gate[...] = sum_refs(parts, 0)
    grad_up[...] = sum_refs(parts, 1)
    grad_down[...] = sum_refs(parts, 2).T


def after(value, *events):
    return lax.optimization_barrier((value, *events))[0]


def on_device(tokens, norm_gain, gate_weight, up_weight, down_weight, out_cotangent):
    ids = jnp.stack([lax.axis_index(n) for n in ("zh", "y", "c", "zl", "x")]).astype(jnp.int32)
    gain = norm_gain.reshape(16, 1, 256)

    pair = jnp.stack([tokens, out_cotangent])
    own = jnp.stack([gate_weight, up_weight, down_weight.T])
    by_z = [lax.ppermute(pair, ("zh", "zl"), z_pairs(k)) for k in range(4)]
    tok_z, cot_z = call(stack_kernel, ids, by_z, [VMEM] * 4, [((4, 128, 256), BF16)] * 2)
    y1, y3, *_ = lax.optimization_barrier((shift(own, "y", 1), shift(own, "y", 3), *by_z))
    y2 = shift(after(own, y1, y3), "y", 2)
    tok_x = [shift(tok_z, "x", s) for s in (1, 2, 3)]
    y2 = after(y2, *tok_x)
    cot_z = after(cot_z, *tok_x)
    tok_x = [tok_z] + tok_x
    by_y = [own, y1, y2, y3]
    weights = by_y + [swap(piece, "c") for piece in by_y]

    x_all = pltpu.VMEM((4, 4, 128, 256), BF16)
    send, tok_all = call(
        forward_products_kernel,
        ids,
        [*tok_x, *weights, gain],
        [VMEM] * 13,
        [((272, 768), BF16), ((256, 2048), BF16)],
        [x_all, pltpu.VMEM((256, 768), F32)],
    )
    cot_x = [cot_z] + [shift(cot_z, "x", s) for s in (1, 2, 3)]
    d_send, cot_all = call(
        backward_products_kernel,
        ids,
        [*cot_x, *weights],
        [VMEM] * 12,
        [((256, 384), BF16), ((256, 2048), BF16)],
        [x_all, pltpu.VMEM((256, 384), F32)],
    )
    recv = swap(send, "zh")
    held = pltpu.VMEM((4, 4, 128, 256), BF16)
    inner, *forward = call(
        forward_outputs_kernel,
        ids,
        [after(send, d_send), recv, *weights],
        [VMEM] * 10,
        [((256, 384), BF16)] + [((4, 128, 256), BF16)] * 4,
        [held],
        8,
        1 << 29,
    )
    forward = scatter_x(forward)
    inner = after(inner, *forward[1:])
    kept, sent, acts, scale, tail = call(
        gradients_kernel,
        ids,
        [send, recv, d_send, swap(d_send, "zh"), inner, tok_all, cot_all],
        [VMEM] * 7,
        [((3, 4, 256, 384), BF16)] * 2
        + [((256, 768), BF16), ((128, 128), F32), ((2, 16, 256), BF16)],
        (),
        16,
        1 << 31,
    )
    backward = call(
        backward_outputs_kernel,
        ids,
        [acts, tail, *weights],
        [VMEM] * 10,
        [((4, 144, 256), BF16)] * 4,
        [held],
        8,
        1 << 30,
    )
    backward = scatter_x(backward)
    sums = list(
        call(core_sum_kernel, ids, [kept, swap(sent, "c")], [VMEM] * 2, [((3, 256, 384), BF16)] * 4)
    )
    near = [shift(sums[1], "y", -1), shift(sums[3], "y", 1)]
    blocks = []
    for k in (0, 2):
        body = functools.partial(x_sum_kernel, k)
        parts = [*forward, *backward]
        blocks += call(body, ids, parts, [VMEM] * 8, [((272, 256), BF16)] * 2)
    blocks[2:] = [after(blocks[2], near[0]), after(blocks[3], near[1])]
    far = shift(after(sums[2], blocks[0]), "y", 2)
    blocks = [
        lax.ppermute(blocks[k], ("zh", "zl"), [(t, s) for s, t in z_pairs(k)]) for k in range(4)
    ]
    grad_gate, grad_up, grad_down = call(
        grads_sum_kernel,
        ids,
        [sums[0], near[0], far, near[1]],
        [VMEM] * 4,
        [((256, 384), F32), ((256, 384), F32), ((384, 256), F32)],
        (),
        16,
    )
    scale = after(scale, grad_gate)
    mixed_out, d_tokens = call(
        finish_kernel,
        ids,
        [*blocks, tokens, out_cotangent, gain, scale],
        [VMEM] * 8,
        [((128, 256), BF16), ((128, 256), F32)],
    )
    return (mixed_out, d_tokens, grad_gate, grad_up, grad_down)


def solution(mesh):
    split = Mesh(mesh.devices.reshape(2, 4, 2, 4, 4), ("zh", "y", "c", "zl", "x"))
    grp, dev = ("zh", "y", "c"), ("zl", "x")
    in_specs = (P(grp, dev), P(), P(grp, dev), P(grp, dev), P(dev, grp), P(grp, dev))
    out_specs = (P(grp, dev), P(grp, dev), P(grp, dev), P(grp, dev), P(dev, grp))
    return jax.shard_map(
        on_device, mesh=split, in_specs=in_specs, out_specs=out_specs, check_vma=False
    )
```

time: 155 us -> 145 us (0.935)
  waiting for transfers between devices: 66.1 us -> 57.7 us
  starting transfers between devices: 62.1 us -> 66.7 us
  local copies, waits for them, and re-layouts: 5.28 us -> 1.2 us
  Pallas kernels: 19.9 us -> 16 us
  other arithmetic: 0 us -> 1.99 us
    ppermute x7, waiting for transfers between devices: 13.9 us -> 2.31 us  [swap(): return lax.ppermute(array, axis, [(0, 1), (1, 0)])]
    unnamed x18 -> x7, local copies, waits for them, and re-layouts: 5.19 us -> 1.11 us
    pallas_call x10 -> x11, Pallas kernels: 19.9 us -> 16 us  [call(): pl.pallas_call(body, out_shape=[jax.ShapeDtypeStruct(s, d) for s, d in ou...]
    ppermute x15 -> x18, waiting for transfers between devices: 32.3 us -> 34.7 us  [shift(): return lax.ppermute(array, axis, [(i, (i + by) % 4) for i in range(4)])]
    another operation x0 -> x2, other arithmetic: none -> 1.99 us  [the longest x1 1.11 us: on_device(): own = jnp.stack([gate_weight, up_weight, down_weight.T])]
    ppermute x15 -> x18, starting transfers between devices: 15.7 us -> 17.7 us  [shift(): return lax.ppermute(array, axis, [(i, (i + by) % 4) for i in range(4)])]
    ppermute x7, starting transfers between devices: 21.2 us -> 23.1 us  [swap(): return lax.ppermute(array, axis, [(0, 1), (1, 0)])]
  transfers between devices with their start and end apart: 30 -> 33, of which waited for: 13 -> 17; matrix products, arithmetic and copies ran while one was open for 0% -> 1% of each run, Pallas kernels for 9% -> 6%
where the time goes in v2:
time: 145 us; the launch traced here: 144 us
  starting transfers between devices  66.7 us (46%)
  waiting for transfers between devices  57.7 us (40%)
  Pallas kernels  16 us (11%)
  other arithmetic  1.99 us (1%)
    ppermute x18, waiting for transfers between devices, shift(): return lax.ppermute(array, axis, [(i, (i + by) % 4) for i in range(4)])  34.7 us
    ppermute x7, starting transfers between devices, swap(): return lax.ppermute(array, axis, [(0, 1), (1, 0)])  23.1 us
    ppermute x18, starting transfers between devices, shift(): return lax.ppermute(array, axis, [(i, (i + by) % 4) for i in range(4)])  17.7 us
    pallas_call x11, Pallas kernels, call(): pl.pallas_call(body, out_shape=[jax.ShapeDtypeStruct(s, d) for s, d in ou...  16 us
    ppermute x4, starting transfers between devices, on_device(): lax.ppermute(blocks[k], ('zh', 'zl'), [(t, s) for s, t in z_pairs(k)])  15 us
    ppermute x4, waiting for transfers between devices, on_device(): lax.ppermute(blocks[k], ('zh', 'zl'), [(t, s) for s, t in z_pairs(k)])  13.5 us
    ppermute x4, starting transfers between devices, on_device(): by_z = [lax.ppermute(pair, ('zh', 'zl'), z_pairs(k)) for k in range(4)]  10.9 us
    ppermute x4, waiting for transfers between devices, on_device(): by_z = [lax.ppermute(pair, ('zh', 'zl'), z_pairs(k)) for k in range(4)]  7.21 us
  transfers between devices with their start and end apart: 33, of which 17 were waited for; matrix products, arithmetic and copies ran while one was open for 1% of the time, Pallas kernels for 6%

profile of v2, /device:TPU:97, one launch (start us, length us, event | category | flops | bytes accessed | tf_op | source)
XLA Modules:
  0.0 144.4 jit_solution(5445595906266904423)
XLA Ops:
  2.8 2.8 %collective-permute-start.8 = (bf16[3,256,384]{2,1,0:T(8,128)(2,1)S(1)}, bf16[3,256,384]{2,1,0:T(8,128)(2,1)S(1)}, u32[]{:S(2)}, u32[]{:S(2)}) collective-permute-start(bf16[3,256,384]{2,1,0:T(8,128)(2,1)S(1)} %pad_maximum_fusion.refs_4_.refs_0_), channel_id=1, source_target_pairs={{0,96},{32,0},{64,32},{96,64},{1,97},{33,1},{65,33},{97,65},{2,98}... | collective-permute-start | bytes 1769480 | tf_op jit(solution)/shard_map/ppermute | solution.py:27
  6.6 3.8 %collective-permute-start.3 = (bf16[2,128,256]{2,1,0:T(8,128)(2,1)S(1)}, bf16[2,128,256]{2,1,0:T(8,128)(2,1)S(1)}, u32[]{:S(2)}, u32[]{:S(2)}) collective-permute-start(bf16[2,128,256]{2,1,0:T(8,128)(2,1)S(1)} %pad_maximum_fusion.1), channel_id=1, source_target_pairs={{0,12},{4,8},{8,140},{12,136},{128,4},{132,0},{136,132},{140,128},... | collective-permute-start | bytes 393224 | tf_op jit(solution)/shard_map/ppermute | solution.py:239
  10.4 2.1 %collective-permute-start.2 = (bf16[2,128,256]{2,1,0:T(8,128)(2,1)S(1)}, bf16[2,128,256]{2,1,0:T(8,128)(2,1)S(1)}, u32[]{:S(2)}, u32[]{:S(2)}) collective-permute-start(bf16[2,128,256]{2,1,0:T(8,128)(2,1)S(1)} %pad_maximum_fusion.1), channel_id=1, source_target_pairs={{0,8},{4,12},{8,136},{12,140},{128,0},{132,4},{136,128},{140,132},... | collective-permute-start | bytes 393224 | tf_op jit(solution)/shard_map/ppermute | solution.py:239
  12.5 5.0 %collective-permute-start = (bf16[2,128,256]{2,1,0:T(8,128)(2,1)S(1)}, bf16[2,128,256]{2,1,0:T(8,128)(2,1)S(1)}, u32[]{:S(2)}, u32[]{:S(2)}) collective-permute-start(bf16[2,128,256]{2,1,0:T(8,128)(2,1)S(1)} %pad_maximum_fusion.1), channel_id=1, source_target_pairs={{0,0},{4,4},{8,128},{12,132},{128,8},{132,12},{136,136},{140,140},... | collective-permute-start | bytes 393224 | tf_op jit(solution)/shard_map/ppermute | solution.py:239
  17.5 2.3 %collective-permute-done.2.p2 = bf16[2,128,256]{2,1,0:T(8,128)(2,1)S(1)} collective-permute-done((bf16[2,128,256]{2,1,0:T(8,128)(2,1)S(1)}, bf16[2,128,256]{2,1,0:T(8,128)(2,1)S(1)}, u32[]{:S(2)}, u32[]{:S(2)}) %collective-permute-start.2) | collective-permute-done | bytes 131104 | tf_op jit(solution)/shard_map/ppermute | solution.py:239
  19.8 1.7 %collective-permute-done.1.p1 = bf16[2,128,256]{2,1,0:T(8,128)(2,1)S(1)} collective-permute-done((bf16[2,128,256]{2,1,0:T(8,128)(2,1)S(1)}, bf16[2,128,256]{2,1,0:T(8,128)(2,1)S(1)}, u32[]{:S(2)}, u32[]{:S(2)}) %collective-permute-start.1) | collective-permute-done | bytes 131104 | tf_op jit(solution)/shard_map/ppermute | solution.py:239
  21.4 3.3 %collective-permute-done.p0 = bf16[2,128,256]{2,1,0:T(8,128)(2,1)S(1)} collective-permute-done((bf16[2,128,256]{2,1,0:T(8,128)(2,1)S(1)}, bf16[2,128,256]{2,1,0:T(8,128)(2,1)S(1)}, u32[]{:S(2)}, u32[]{:S(2)}) %collective-permute-start) | collective-permute-done | bytes 131104 | tf_op jit(solution)/shard_map/ppermute | solution.py:239
  24.7 1.6 %collective-permute-start.9 = (bf16[3,256,384]{2,1,0:T(8,128)(2,1)S(1)}, bf16[3,256,384]{2,1,0:T(8,128)(2,1)S(1)}, u32[]{:S(2)}, u32[]{:S(2)}) collective-permute-start(bf16[3,256,384]{2,1,0:T(8,128)(2,1)S(1)} %pad_maximum_fusion.refs_4_.refs_0_), channel_id=1, source_target_pairs={{0,64},{32,96},{64,0},{96,32},{1,65},{33,97},{65,1},{97,33},{2,66}... | collective-permute-start | bytes 1769480 | tf_op jit(solution)/shard_map/ppermute | solution.py:27
  27.0 2.6 %collective-permute-start.6 = (bf16[4,128,256]{2,1,0:T(8,128)(2,1)S(1)}, bf16[4,128,256]{2,1,0:T(8,128)(2,1)S(1)}, u32[]{:S(2)}, u32[]{:S(2)}) collective-permute-start(bf16[4,128,256]{2,1,0:T(8,128)(2,1)S(1)} %get-tuple-element.49.refs_0_), channel_id=1, source_target_pairs={{0,3},{1,0},{2,1},{3,2},{4,7},{5,4},{6,5},{7,6},{8,11},{9,8},{10,9... | collective-permute-start | bytes 786440 | tf_op jit(solution)/shard_map/ppermute | solution.py:27
  30.7 5.0 %collective-permute-start.10 = (bf16[3,256,384]{2,1,0:T(8,128)(2,1)S(1)}, bf16[3,256,384]{2,1,0:T(8,128)(2,1)S(1)}, u32[]{:S(2)}, u32[]{:S(2)}) collective-permute-start(bf16[3,256,384]{2,1,0:T(8,128)(2,1)S(1)} %pad_maximum_fusion.refs_4_.refs_0_), channel_id=1, source_target_pairs={{0,16},{16,0},{1,17},{17,1},{2,18},{18,2},{3,19},{19,3},{4,20},{20... | collective-permute-start | bytes 1769480 | tf_op jit(solution)/shard_map/ppermute | solution.py:31
  36.1 5.6 %collective-permute-start.11 = (bf16[3,256,384]{2,1,0:T(8,128)(2,1)S(1)}, bf16[3,256,384]{2,1,0:T(8,128)(2,1)S(1)}, u32[]{:S(2)}, u32[]{:S(2)}) collective-permute-start(bf16[3,256,384]{2,1,0:T(8,128)(2,1)S(1)} %collective-permute-done.7.refs_5_.refs_1_), channel_id=1, source_target_pairs={{0,16},{16,0},{1,17},{17,1},{2,18},{18,2},{3,19},{19,3},{4,20},{20... | collective-permute-start | bytes 1769480 | tf_op jit(solution)/shard_map/ppermute | solution.py:31
  42.8 2.7 %collective-permute-start.12 = (bf16[3,256,384]{2,1,0:T(8,128)(2,1)S(1)}, bf16[3,256,384]{2,1,0:T(8,128)(2,1)S(1)}, u32[]{:S(2)}, u32[]{:S(2)}) collective-permute-start(bf16[3,256,384]{2,1,0:T(8,128)(2,1)S(1)} %collective-permute-done.9.refs_6_.refs_2_), channel_id=1, source_target_pairs={{0,16},{16,0},{1,17},{17,1},{2,18},{18,2},{3,19},{19,3},{4,20},{20... | collective-permute-start | bytes 1769480 | tf_op jit(solution)/shard_map/ppermute | solution.py:31
  47.1 1.9 %shard_map.102 = (bf16[272,768]{1,0:T(8,128)(2,1)S(1)}, bf16[256,2048]{1,0:T(8,128)(2,1)S(1)}) custom-call(s32[5]{0:T(128)S(1)} %stack.44.ids, bf16[4,128,256]{2,1,0:T(8,128)(2,1)S(1)} %get-tuple-element.49.refs_0_, bf16[4,128,256]{2,1,0:T(8,128)(2,1)S(1)} %collective-permute-done.4.refs_1_, bf16[4,128,256]{2,1,0:T(8,128)(2,1)S(1)} %collective-permute-done.5.refs_2_, ...), custom_call_target="tpu_custom_call" | custom-call | bytes 7249920 | tf_op jit(solution)/shard_map/pallas_call | solution.py:52
  49.0 3.1 %collective-permute-start.17 = (bf16[272,768]{1,0:T(8,128)(2,1)S(1)}, bf16[272,768]{1,0:T(8,128)(2,1)S(1)}, u32[]{:S(2)}, u32[]{:S(2)}) collective-permute-start(bf16[272,768]{1,0:T(8,128)(2,1)S(1)} %get-tuple-element.58.mine), channel_id=1, source_target_pairs={{0,128},{128,0},{1,129},{129,1},{2,130},{130,2},{3,131},{131,3},{4... | collective-permute-start | bytes 1253384 | tf_op jit(solution)/shard_map/ppermute | solution.py:31
  54.1 5.2 %collective-permute-done.16.refs_3_ = bf16[4,128,256]{2,1,0:T(8,128)(2,1)S(1)} collective-permute-done((bf16[4,128,256]{2,1,0:T(8,128)(2,1)S(1)}, bf16[4,128,256]{2,1,0:T(8,128)(2,1)S(1)}, u32[]{:S(2)}, u32[]{:S(2)}) %collective-permute-start.16) | collective-permute-done | bytes 262176 | tf_op jit(solution)/shard_map/ppermute | solution.py:27
  59.3 2.7 %collective-permute-done.15.refs_2_ = bf16[4,128,256]{2,1,0:T(8,128)(2,1)S(1)} collective-permute-done((bf16[4,128,256]{2,1,0:T(8,128)(2,1)S(1)}, bf16[4,128,256]{2,1,0:T(8,128)(2,1)S(1)}, u32[]{:S(2)}, u32[]{:S(2)}) %collective-permute-start.15) | collective-permute-done | bytes 262176 | tf_op jit(solution)/shard_map/ppermute | solution.py:27
  62.0 6.2 %collective-permute-done.14.refs_1_ = bf16[4,128,256]{2,1,0:T(8,128)(2,1)S(1)} collective-permute-done((bf16[4,128,256]{2,1,0:T(8,128)(2,1)S(1)}, bf16[4,128,256]{2,1,0:T(8,128)(2,1)S(1)}, u32[]{:S(2)}, u32[]{:S(2)}) %collective-permute-start.14) | collective-permute-done | bytes 262176 | tf_op jit(solution)/shard_map/ppermute | solution.py:27
  69.6 1.7 %shard_map.104 = (bf16[256,384]{1,0:T(8,128)(2,1)S(1)}, bf16[4,128,256]{2,1,0:T(8,128)(2,1)S(1)}, bf16[4,128,256]{2,1,0:T(8,128)(2,1)S(1)}, bf16[4,128,256]{2,1,0:T(8,128)(2,1)S(1)}, bf16[4,128,256]{2,1,0:T(8,128)(2,1)S(1)}) custom-call(s32[5]{0:T(128)S(1)} %stack.44.ids, bf16[272,768]{1,0:T(8,128)(2,1)S(1)} %get-tuple-element.58.mine, ...), custom_call_target="tpu_custom_call" | custom-call | flops 536870912 | bytes 6799360 | tf_op jit(solution)/shard_map/pallas_call | solution.py:52
  72.8 5.1 %collective-permute-start.21 = (bf16[256,384]{1,0:T(8,128)(2,1)S(1)}, bf16[256,384]{1,0:T(8,128)(2,1)S(1)}, u32[]{:S(2)}, u32[]{:S(2)}) collective-permute-start(bf16[256,384]{1,0:T(8,128)(2,1)S(1)} %get-tuple-element.57.d_mine), channel_id=1, source_target_pairs={{0,128},{128,0},{1,129},{129,1},{2,130},{130,2},{3,131},{131,3},{4... | collective-permute-start | bytes 589832 | tf_op jit(solution)/shard_map/ppermute | solution.py:31
  79.1 7.6 %collective-permute-done.20.refs_3_ = bf16[4,128,256]{2,1,0:T(8,128)(2,1)S(1)} collective-permute-done((bf16[4,128,256]{2,1,0:T(8,128)(2,1)S(1)}, bf16[4,128,256]{2,1,0:T(8,128)(2,1)S(1)}, u32[]{:S(2)}, u32[]{:S(2)}) %collective-permute-start.20) | collective-permute-done | bytes 262176 | tf_op jit(solution)/shard_map/ppermute | solution.py:27
  86.8 3.0 %shard_map.105 = (bf16[3,4,256,384]{3,2,1,0:T(8,128)(2,1)S(1)}, bf16[3,4,256,384]{3,2,1,0:T(8,128)(2,1)S(1)}, bf16[256,768]{1,0:T(8,128)(2,1)S(1)}, f32[128,128]{1,0:T(8,128)S(1)}, bf16[2,16,256]{2,1,0:T(8,128)(2,1)S(1)}) custom-call(s32[5]{0:T(128)S(1)} %stack.44.ids, bf16[272,768]{1,0:T(8,128)(2,1)S(1)} %get-tuple-element.58.mine, ...), custom_call_target="tpu_custom_call" | custom-call | flops 2147483648 | bytes 8683520 | tf_op jit(solution)/shard_map/pallas_call | solution.py:52
  90.3 1.9 %shard_map.106 = (bf16[4,144,256]{2,1,0:T(8,128)(2,1)S(1)}, bf16[4,144,256]{2,1,0:T(8,128)(2,1)S(1)}, bf16[4,144,256]{2,1,0:T(8,128)(2,1)S(1)}, bf16[4,144,256]{2,1,0:T(8,128)(2,1)S(1)}) custom-call(s32[5]{0:T(128)S(1)} %stack.44.ids, bf16[256,768]{1,0:T(8,128)(2,1)S(1)} %get-tuple-element.67.acts, bf16[2,16,256]{2,1,0:T(8,128)(2,1)S(1)} %get-tuple-element.68.tail, ...), custom_call_target="tpu_custom_call" | custom-call | flops 1073741824 | bytes 6307840 | tf_op jit(solution)/shard_map/pallas_call | solution.py:52
  95.6 3.0 %collective-permute-start.28 = (bf16[3,256,384]{2,1,0:T(8,128)(2,1)S(1)}, bf16[3,256,384]{2,1,0:T(8,128)(2,1)S(1)}, u32[]{:S(2)}, u32[]{:S(2)}) collective-permute-start(bf16[3,256,384]{2,1,0:T(8,128)(2,1)S(1)} %get-tuple-element.78), channel_id=1, source_target_pairs={{0,96},{32,0},{64,32},{96,64},{1,97},{33,1},{65,33},{97,65},{2,98}... | collective-permute-start | bytes 1769480 | tf_op jit(solution)/shard_map/ppermute | solution.py:27
  98.6 2.3 %collective-permute-done.22.refs_5_ = bf16[4,144,256]{2,1,0:T(8,128)(2,1)S(1)} collective-permute-done((bf16[4,144,256]{2,1,0:T(8,128)(2,1)S(1)}, bf16[4,144,256]{2,1,0:T(8,128)(2,1)S(1)}, u32[]{:S(2)}, u32[]{:S(2)}) %collective-permute-start.22) | collective-permute-done | bytes 294944 | tf_op jit(solution)/shard_map/ppermute | solution.py:27
  100.9 2.0 %collective-permute-done.23.refs_6_ = bf16[4,144,256]{2,1,0:T(8,128)(2,1)S(1)} collective-permute-done((bf16[4,144,256]{2,1,0:T(8,128)(2,1)S(1)}, bf16[4,144,256]{2,1,0:T(8,128)(2,1)S(1)}, u32[]{:S(2)}, u32[]{:S(2)}) %collective-permute-start.23) | collective-permute-done | bytes 294944 | tf_op jit(solution)/shard_map/ppermute | solution.py:27
  103.0 6.9 %collective-permute-done.24.refs_7_ = bf16[4,144,256]{2,1,0:T(8,128)(2,1)S(1)} collective-permute-done((bf16[4,144,256]{2,1,0:T(8,128)(2,1)S(1)}, bf16[4,144,256]{2,1,0:T(8,128)(2,1)S(1)}, u32[]{:S(2)}, u32[]{:S(2)}) %collective-permute-start.24) | collective-permute-done | bytes 294944 | tf_op jit(solution)/shard_map/ppermute | solution.py:27
  112.0 9.2 %collective-permute-start.25 = (bf16[272,256]{1,0:T(8,128)(2,1)S(1)}, bf16[272,256]{1,0:T(8,128)(2,1)S(1)}, u32[]{:S(2)}, u32[]{:S(2)}) collective-permute-start(bf16[272,256]{1,0:T(8,128)(2,1)S(1)} %get-tuple-element.73), channel_id=1, source_target_pairs={{0,0},{4,4},{128,8},{132,12},{8,128},{12,132},{136,136},{140,140},... | collective-permute-start | bytes 417800 | tf_op jit(solution)/shard_map/ppermute | solution.py:316
  121.2 2.6 %collective-permute-start.26 = (bf16[272,256]{1,0:T(8,128)(2,1)S(1)}, bf16[272,256]{1,0:T(8,128)(2,1)S(1)}, u32[]{:S(2)}, u32[]{:S(2)}) collective-permute-start(bf16[272,256]{1,0:T(8,128)(2,1)S(1)} %get-tuple-element.74), channel_id=1, source_target_pairs={{4,0},{0,4},{132,8},{128,12},{12,128},{8,132},{140,136},{136,140},... | collective-permute-start | bytes 417800 | tf_op jit(solution)/shard_map/ppermute | solution.py:316
  124.6 3.1 %collective-permute-start.31 = (bf16[272,256]{1,0:T(8,128)(2,1)S(1)}, bf16[272,256]{1,0:T(8,128)(2,1)S(1)}, u32[]{:S(2)}, u32[]{:S(2)}) collective-permute-start(bf16[272,256]{1,0:T(8,128)(2,1)S(1)} %get-tuple-element.82), channel_id=1, source_target_pairs={{12,0},{8,4},{140,8},{136,12},{4,128},{0,132},{132,136},{128,140},... | collective-permute-start | bytes 417800 | tf_op jit(solution)/shard_map/ppermute | solution.py:316
  127.7 1.8 %shard_map.110 = (f32[256,384]{1,0:T(8,128)}, f32[256,384]{1,0:T(8,128)}, f32[384,256]{1,0:T(8,128)}) custom-call(s32[5]{0:T(128)S(1)} %stack.44.ids, bf16[3,256,384]{2,1,0:T(8,128)(2,1)S(1)} %get-tuple-element.84.p0, bf16[3,256,384]{2,1,0:T(8,128)(2,1)S(1)} %collective-permute-done.28.p1, bf16[3,256,384]{2,1,0:T(8,128)(2,1)S(1)} %collective-permute-done.32.p2, ...), custom_call_target="tpu_custom_call" | custom-call | bytes 2949120 | tf_op jit(solution)/shard_map/pallas_call | solution.py:52
  129.5 7.7 %collective-permute-done.26.p1 = bf16[272,256]{1,0:T(8,128)(2,1)S(1)} collective-permute-done((bf16[272,256]{1,0:T(8,128)(2,1)S(1)}, bf16[272,256]{1,0:T(8,128)(2,1)S(1)}, u32[]{:S(2)}, u32[]{:S(2)}) %collective-permute-start.26) | collective-permute-done | bytes 139296 | tf_op jit(solution)/shard_map/ppermute | solution.py:316
  137.2 5.8 %collective-permute-done.31.p3 = bf16[272,256]{1,0:T(8,128)(2,1)S(1)} collective-permute-done((bf16[272,256]{1,0:T(8,128)(2,1)S(1)}, bf16[272,256]{1,0:T(8,128)(2,1)S(1)}, u32[]{:S(2)}, u32[]{:S(2)}) %collective-permute-start.31) | collective-permute-done | bytes 139296 | tf_op jit(solution)/shard_map/ppermute | solution.py:316
  (55 shorter events, 22.2 us)
Async XLA Ops:
  2.8 21.9 %collective-permute-start.8 = (bf16[3,256,384]{2,1,0:T(8,128)(2,1)S(1)}, bf16[3,256,384]{2,1,0:T(8,128)(2,1)S(1)}, u32[]{:S(2)}, u32[]{:S(2)}) collective-permute-start(bf16[3,256,384]{2,1,0:T(8,128)(2,1)S(1)} %pad_maximum_fusion.refs_4_.refs_0_), channel_id=1, source_target_pairs={{0,96},{32,0},{64,32},{96,64},{1,97},{33,1},{65,33},{97,65},{2,98}... | collective-permute-start | bytes 1769480 | tf_op jit(solution)/shard_map/ppermute | solution.py:27
  5.7 19.0 %collective-permute-start.7 = (bf16[3,256,384]{2,1,0:T(8,128)(2,1)S(1)}, bf16[3,256,384]{2,1,0:T(8,128)(2,1)S(1)}, u32[]{:S(2)}, u32[]{:S(2)}) collective-permute-start(bf16[3,256,384]{2,1,0:T(8,128)(2,1)S(1)} %pad_maximum_fusion.refs_4_.refs_0_), channel_id=1, source_target_pairs={{0,32},{32,64},{64,96},{96,0},{1,33},{33,65},{65,97},{97,1},{2,34}... | collective-permute-start | bytes 1769480 | tf_op jit(solution)/shard_map/ppermute | solution.py:27
  6.6 5.9 %collective-permute-start.3 = (bf16[2,128,256]{2,1,0:T(8,128)(2,1)S(1)}, bf16[2,128,256]{2,1,0:T(8,128)(2,1)S(1)}, u32[]{:S(2)}, u32[]{:S(2)}) collective-permute-start(bf16[2,128,256]{2,1,0:T(8,128)(2,1)S(1)} %pad_maximum_fusion.1), channel_id=1, source_target_pairs={{0,12},{4,8},{8,140},{12,136},{128,4},{132,0},{136,132},{140,128},... | collective-permute-start | bytes 393224 | tf_op jit(solution)/shard_map/ppermute | solution.py:239
  10.4 9.4 %collective-permute-start.2 = (bf16[2,128,256]{2,1,0:T(8,128)(2,1)S(1)}, bf16[2,128,256]{2,1,0:T(8,128)(2,1)S(1)}, u32[]{:S(2)}, u32[]{:S(2)}) collective-permute-start(bf16[2,128,256]{2,1,0:T(8,128)(2,1)S(1)} %pad_maximum_fusion.1), channel_id=1, source_target_pairs={{0,8},{4,12},{8,136},{12,140},{128,0},{132,4},{136,128},{140,132},... | collective-permute-start | bytes 393224 | tf_op jit(solution)/shard_map/ppermute | solution.py:239
  12.5 9.0 %collective-permute-start.1 = (bf16[2,128,256]{2,1,0:T(8,128)(2,1)S(1)}, bf16[2,128,256]{2,1,0:T(8,128)(2,1)S(1)}, u32[]{:S(2)}, u32[]{:S(2)}) collective-permute-start(bf16[2,128,256]{2,1,0:T(8,128)(2,1)S(1)} %pad_maximum_fusion.1), channel_id=1, source_target_pairs={{0,4},{4,0},{8,132},{12,128},{128,12},{132,8},{136,140},{140,136},... | collective-permute-start | bytes 393224 | tf_op jit(solution)/shard_map/ppermute | solution.py:239
  12.5 12.2 %collective-permute-start = (bf16[2,128,256]{2,1,0:T(8,128)(2,1)S(1)}, bf16[2,128,256]{2,1,0:T(8,128)(2,1)S(1)}, u32[]{:S(2)}, u32[]{:S(2)}) collective-permute-start(bf16[2,128,256]{2,1,0:T(8,128)(2,1)S(1)} %pad_maximum_fusion.1), channel_id=1, source_target_pairs={{0,0},{4,4},{8,128},{12,132},{128,8},{132,12},{136,136},{140,140},... | collective-permute-start | bytes 393224 | tf_op jit(solution)/shard_map/ppermute | solution.py:239
  24.7 18.1 %collective-permute-start.9 = (bf16[3,256,384]{2,1,0:T(8,128)(2,1)S(1)}, bf16[3,256,384]{2,1,0:T(8,128)(2,1)S(1)}, u32[]{:S(2)}, u32[]{:S(2)}) collective-permute-start(bf16[3,256,384]{2,1,0:T(8,128)(2,1)S(1)} %pad_maximum_fusion.refs_4_.refs_0_), channel_id=1, source_target_pairs={{0,64},{32,96},{64,0},{96,32},{1,65},{33,97},{65,1},{97,33},{2,66}... | collective-permute-start | bytes 1769480 | tf_op jit(solution)/shard_map/ppermute | solution.py:27
  27.0 9.1 %collective-permute-start.6 = (bf16[4,128,256]{2,1,0:T(8,128)(2,1)S(1)}, bf16[4,128,256]{2,1,0:T(8,128)(2,1)S(1)}, u32[]{:S(2)}, u32[]{:S(2)}) collective-permute-start(bf16[4,128,256]{2,1,0:T(8,128)(2,1)S(1)} %get-tuple-element.49.refs_0_), channel_id=1, source_target_pairs={{0,3},{1,0},{2,1},{3,2},{4,7},{5,4},{6,5},{7,6},{8,11},{9,8},{10,9... | collective-permute-start | bytes 786440 | tf_op jit(solution)/shard_map/ppermute | solution.py:27
  29.6 12.2 %collective-permute-start.5 = (bf16[4,128,256]{2,1,0:T(8,128)(2,1)S(1)}, bf16[4,128,256]{2,1,0:T(8,128)(2,1)S(1)}, u32[]{:S(2)}, u32[]{:S(2)}) collective-permute-start(bf16[4,128,256]{2,1,0:T(8,128)(2,1)S(1)} %get-tuple-element.49.refs_0_), channel_id=1, source_target_pairs={{0,2},{1,3},{2,0},{3,1},{4,6},{5,7},{6,4},{7,5},{8,10},{9,11},{10,... | collective-permute-start | bytes 786440 | tf_op jit(solution)/shard_map/ppermute | solution.py:27
  30.1 12.7 %collective-permute-start.4 = (bf16[4,128,256]{2,1,0:T(8,128)(2,1)S(1)}, bf16[4,128,256]{2,1,0:T(8,128)(2,1)S(1)}, u32[]{:S(2)}, u32[]{:S(2)}) collective-permute-start(bf16[4,128,256]{2,1,0:T(8,128)(2,1)S(1)} %get-tuple-element.49.refs_0_), channel_id=1, source_target_pairs={{0,1},{1,2},{2,3},{3,0},{4,5},{5,6},{6,7},{7,4},{8,9},{9,10},{10,1... | collective-permute-start | bytes 786440 | tf_op jit(solution)/shard_map/ppermute | solution.py:27
  30.7 14.7 %collective-permute-start.10 = (bf16[3,256,384]{2,1,0:T(8,128)(2,1)S(1)}, bf16[3,256,384]{2,1,0:T(8,128)(2,1)S(1)}, u32[]{:S(2)}, u32[]{:S(2)}) collective-permute-start(bf16[3,256,384]{2,1,0:T(8,128)(2,1)S(1)} %pad_maximum_fusion.refs_4_.refs_0_), channel_id=1, source_target_pairs={{0,16},{16,0},{1,17},{17,1},{2,18},{18,2},{3,19},{19,3},{4,20},{20... | collective-permute-start | bytes 1769480 | tf_op jit(solution)/shard_map/ppermute | solution.py:31
  36.1 9.3 %collective-permute-start.11 = (bf16[3,256,384]{2,1,0:T(8,128)(2,1)S(1)}, bf16[3,256,384]{2,1,0:T(8,128)(2,1)S(1)}, u32[]{:S(2)}, u32[]{:S(2)}) collective-permute-start(bf16[3,256,384]{2,1,0:T(8,128)(2,1)S(1)} %collective-permute-done.7.refs_5_.refs_1_), channel_id=1, source_target_pairs={{0,16},{16,0},{1,17},{17,1},{2,18},{18,2},{3,19},{19,3},{4,20},{20... | collective-permute-start | bytes 1769480 | tf_op jit(solution)/shard_map/ppermute | solution.py:31
  42.8 4.3 %collective-permute-start.12 = (bf16[3,256,384]{2,1,0:T(8,128)(2,1)S(1)}, bf16[3,256,384]{2,1,0:T(8,128)(2,1)S(1)}, u32[]{:S(2)}, u32[]{:S(2)}) collective-permute-start(bf16[3,256,384]{2,1,0:T(8,128)(2,1)S(1)} %collective-permute-done.9.refs_6_.refs_2_), channel_id=1, source_target_pairs={{0,16},{16,0},{1,17},{17,1},{2,18},{18,2},{3,19},{19,3},{4,20},{20... | collective-permute-start | bytes 1769480 | tf_op jit(solution)/shard_map/ppermute | solution.py:31
  49.0 20.6 %collective-permute-start.17 = (bf16[272,768]{1,0:T(8,128)(2,1)S(1)}, bf16[272,768]{1,0:T(8,128)(2,1)S(1)}, u32[]{:S(2)}, u32[]{:S(2)}) collective-permute-start(bf16[272,768]{1,0:T(8,128)(2,1)S(1)} %get-tuple-element.58.mine), channel_id=1, source_target_pairs={{0,128},{128,0},{1,129},{129,1},{2,130},{130,2},{3,131},{131,3},{4... | collective-permute-start | bytes 1253384 | tf_op jit(solution)/shard_map/ppermute | solution.py:31
  52.1 7.2 %collective-permute-start.16 = (bf16[4,128,256]{2,1,0:T(8,128)(2,1)S(1)}, bf16[4,128,256]{2,1,0:T(8,128)(2,1)S(1)}, u32[]{:S(2)}, u32[]{:S(2)}) collective-permute-start(bf16[4,128,256]{2,1,0:T(8,128)(2,1)S(1)} %get-tuple-element.56.refs_0_), channel_id=1, source_target_pairs={{0,3},{1,0},{2,1},{3,2},{4,7},{5,4},{6,5},{7,6},{8,11},{9,8},{10,9... | collective-permute-start | bytes 786440 | tf_op jit(solution)/shard_map/ppermute | solution.py:27
  53.5 8.5 %collective-permute-start.15 = (bf16[4,128,256]{2,1,0:T(8,128)(2,1)S(1)}, bf16[4,128,256]{2,1,0:T(8,128)(2,1)S(1)}, u32[]{:S(2)}, u32[]{:S(2)}) collective-permute-start(bf16[4,128,256]{2,1,0:T(8,128)(2,1)S(1)} %get-tuple-element.56.refs_0_), channel_id=1, source_target_pairs={{0,2},{1,3},{2,0},{3,1},{4,6},{5,7},{6,4},{7,5},{8,10},{9,11},{10,... | collective-permute-start | bytes 786440 | tf_op jit(solution)/shard_map/ppermute | solution.py:27
  53.5 14.7 %collective-permute-start.14 = (bf16[4,128,256]{2,1,0:T(8,128)(2,1)S(1)}, bf16[4,128,256]{2,1,0:T(8,128)(2,1)S(1)}, u32[]{:S(2)}, u32[]{:S(2)}) collective-permute-start(bf16[4,128,256]{2,1,0:T(8,128)(2,1)S(1)} %get-tuple-element.56.refs_0_), channel_id=1, source_target_pairs={{0,1},{1,2},{2,3},{3,0},{4,5},{5,6},{6,7},{7,4},{8,9},{9,10},{10,1... | collective-permute-start | bytes 786440 | tf_op jit(solution)/shard_map/ppermute | solution.py:27
  71.2 7.1 %collective-permute-start.18 = (bf16[4,128,256]{2,1,0:T(8,128)(2,1)S(1)}, bf16[4,128,256]{2,1,0:T(8,128)(2,1)S(1)}, u32[]{:S(2)}, u32[]{:S(2)}) collective-permute-start(bf16[4,128,256]{2,1,0:T(8,128)(2,1)S(1)} %get-tuple-element.60), channel_id=1, source_target_pairs={{0,3},{1,0},{2,1},{3,2},{4,7},{5,4},{6,5},{7,6},{8,11},{9,8},{10,9... | collective-permute-start | bytes 786440 | tf_op jit(solution)/shard_map/ppermute | solution.py:27
  71.3 7.8 %collective-permute-start.19 = (bf16[4,128,256]{2,1,0:T(8,128)(2,1)S(1)}, bf16[4,128,256]{2,1,0:T(8,128)(2,1)S(1)}, u32[]{:S(2)}, u32[]{:S(2)}) collective-permute-start(bf16[4,128,256]{2,1,0:T(8,128)(2,1)S(1)} %get-tuple-element.61), channel_id=1, source_target_pairs={{0,2},{1,3},{2,0},{3,1},{4,6},{5,7},{6,4},{7,5},{8,10},{9,11},{10,... | collective-permute-start | bytes 786440 | tf_op jit(solution)/shard_map/ppermute | solution.py:27
  72.1 14.7 %collective-permute-start.20 = (bf16[4,128,256]{2,1,0:T(8,128)(2,1)S(1)}, bf16[4,128,256]{2,1,0:T(8,128)(2,1)S(1)}, u32[]{:S(2)}, u32[]{:S(2)}) collective-permute-start(bf16[4,128,256]{2,1,0:T(8,128)(2,1)S(1)} %get-tuple-element.62), channel_id=1, source_target_pairs={{0,1},{1,2},{2,3},{3,0},{4,5},{5,6},{6,7},{7,4},{8,9},{9,10},{10,1... | collective-permute-start | bytes 786440 | tf_op jit(solution)/shard_map/ppermute | solution.py:27
  72.8 14.0 %collective-permute-start.21 = (bf16[256,384]{1,0:T(8,128)(2,1)S(1)}, bf16[256,384]{1,0:T(8,128)(2,1)S(1)}, u32[]{:S(2)}, u32[]{:S(2)}) collective-permute-start(bf16[256,384]{1,0:T(8,128)(2,1)S(1)} %get-tuple-element.57.d_mine), channel_id=1, source_target_pairs={{0,128},{128,0},{1,129},{129,1},{2,130},{130,2},{3,131},{131,3},{4... | collective-permute-start | bytes 589832 | tf_op jit(solution)/shard_map/ppermute | solution.py:31
  89.7 4.7 %collective-permute-start.27 = (bf16[3,4,256,384]{3,2,1,0:T(8,128)(2,1)S(1)}, bf16[3,4,256,384]{3,2,1,0:T(8,128)(2,1)S(1)}, u32[]{:S(2)}, u32[]{:S(2)}) collective-permute-start(bf16[3,4,256,384]{3,2,1,0:T(8,128)(2,1)S(1)} %get-tuple-element.77), channel_id=1, source_target_pairs={{0,16},{16,0},{1,17},{17,1},{2,18},{18,2},{3,19},{19,3},{4,20},{20... | collective-permute-start | bytes 7077896 | tf_op jit(solution)/shard_map/ppermute | solution.py:31
  92.2 8.7 %collective-permute-start.22 = (bf16[4,144,256]{2,1,0:T(8,128)(2,1)S(1)}, bf16[4,144,256]{2,1,0:T(8,128)(2,1)S(1)}, u32[]{:S(2)}, u32[]{:S(2)}) collective-permute-start(bf16[4,144,256]{2,1,0:T(8,128)(2,1)S(1)} %get-tuple-element.70), channel_id=1, source_target_pairs={{0,3},{1,0},{2,1},{3,2},{4,7},{5,4},{6,5},{7,6},{8,11},{9,8},{10,9... | collective-permute-start | bytes 884744 | tf_op jit(solution)/shard_map/ppermute | solution.py:27
  93.1 9.9 %collective-permute-start.23 = (bf16[4,144,256]{2,1,0:T(8,128)(2,1)S(1)}, bf16[4,144,256]{2,1,0:T(8,128)(2,1)S(1)}, u32[]{:S(2)}, u32[]{:S(2)}) collective-permute-start(bf16[4,144,256]{2,1,0:T(8,128)(2,1)S(1)} %get-tuple-element.71), channel_id=1, source_target_pairs={{0,2},{1,3},{2,0},{3,1},{4,6},{5,7},{6,4},{7,5},{8,10},{9,11},{10,... | collective-permute-start | bytes 884744 | tf_op jit(solution)/shard_map/ppermute | solution.py:27
  93.3 16.6 %collective-permute-start.24 = (bf16[4,144,256]{2,1,0:T(8,128)(2,1)S(1)}, bf16[4,144,256]{2,1,0:T(8,128)(2,1)S(1)}, u32[]{:S(2)}, u32[]{:S(2)}) collective-permute-start(bf16[4,144,256]{2,1,0:T(8,128)(2,1)S(1)} %get-tuple-element.72), channel_id=1, source_target_pairs={{0,1},{1,2},{2,3},{3,0},{4,5},{5,6},{6,7},{7,4},{8,9},{9,10},{10,1... | collective-permute-start | bytes 884744 | tf_op jit(solution)/shard_map/ppermute | solution.py:27
  95.6 28.9 %collective-permute-start.28 = (bf16[3,256,384]{2,1,0:T(8,128)(2,1)S(1)}, bf16[3,256,384]{2,1,0:T(8,128)(2,1)S(1)}, u32[]{:S(2)}, u32[]{:S(2)}) collective-permute-start(bf16[3,256,384]{2,1,0:T(8,128)(2,1)S(1)} %get-tuple-element.78), channel_id=1, source_target_pairs={{0,96},{32,0},{64,32},{96,64},{1,97},{33,1},{65,33},{97,65},{2,98}... | collective-permute-start | bytes 1769480 | tf_op jit(solution)/shard_map/ppermute | solution.py:27
  98.6 26.0 %collective-permute-start.30 = (bf16[3,256,384]{2,1,0:T(8,128)(2,1)S(1)}, bf16[3,256,384]{2,1,0:T(8,128)(2,1)S(1)}, u32[]{:S(2)}, u32[]{:S(2)}) collective-permute-start(bf16[3,256,384]{2,1,0:T(8,128)(2,1)S(1)} %get-tuple-element.81), channel_id=1, source_target_pairs={{0,32},{32,64},{64,96},{96,0},{1,33},{33,65},{65,97},{97,1},{2,34}... | collective-permute-start | bytes 1769480 | tf_op jit(solution)/shard_map/ppermute | solution.py:27
  110.6 17.1 %collective-permute-start.32 = (bf16[3,256,384]{2,1,0:T(8,128)(2,1)S(1)}, bf16[3,256,384]{2,1,0:T(8,128)(2,1)S(1)}, u32[]{:S(2)}, u32[]{:S(2)}) collective-permute-start(bf16[3,256,384]{2,1,0:T(8,128)(2,1)S(1)} %get-tuple-element.86), channel_id=1, source_target_pairs={{0,64},{32,96},{64,0},{96,32},{1,65},{33,97},{65,1},{97,33},{2,66}... | collective-permute-start | bytes 1769480 | tf_op jit(solution)/shard_map/ppermute | solution.py:27
  112.0 25.2 %collective-permute-start.25 = (bf16[272,256]{1,0:T(8,128)(2,1)S(1)}, bf16[272,256]{1,0:T(8,128)(2,1)S(1)}, u32[]{:S(2)}, u32[]{:S(2)}) collective-permute-start(bf16[272,256]{1,0:T(8,128)(2,1)S(1)} %get-tuple-element.73), channel_id=1, source_target_pairs={{0,0},{4,4},{128,8},{132,12},{8,128},{12,132},{136,136},{140,140},... | collective-permute-start | bytes 417800 | tf_op jit(solution)/shard_map/ppermute | solution.py:316
  121.2 16.0 %collective-permute-start.26 = (bf16[272,256]{1,0:T(8,128)(2,1)S(1)}, bf16[272,256]{1,0:T(8,128)(2,1)S(1)}, u32[]{:S(2)}, u32[]{:S(2)}) collective-permute-start(bf16[272,256]{1,0:T(8,128)(2,1)S(1)} %get-tuple-element.74), channel_id=1, source_target_pairs={{4,0},{0,4},{132,8},{128,12},{12,128},{8,132},{140,136},{136,140},... | collective-permute-start | bytes 417800 | tf_op jit(solution)/shard_map/ppermute | solution.py:316
  124.5 12.7 %collective-permute-start.29 = (bf16[272,256]{1,0:T(8,128)(2,1)S(1)}, bf16[272,256]{1,0:T(8,128)(2,1)S(1)}, u32[]{:S(2)}, u32[]{:S(2)}) collective-permute-start(bf16[272,256]{1,0:T(8,128)(2,1)S(1)} %get-tuple-element.79), channel_id=1, source_target_pairs={{8,0},{12,4},{136,8},{140,12},{0,128},{4,132},{128,136},{132,140},... | collective-permute-start | bytes 417800 | tf_op jit(solution)/shard_map/ppermute | solution.py:316
  124.6 18.4 %collective-permute-start.31 = (bf16[272,256]{1,0:T(8,128)(2,1)S(1)}, bf16[272,256]{1,0:T(8,128)(2,1)S(1)}, u32[]{:S(2)}, u32[]{:S(2)}) collective-permute-start(bf16[272,256]{1,0:T(8,128)(2,1)S(1)} %get-tuple-element.82), channel_id=1, source_target_pairs={{12,0},{8,4},{140,8},{136,12},{4,128},{0,132},{132,136},{128,140},... | collective-permute-start | bytes 417800 | tf_op jit(solution)/shard_map/ppermute | solution.py:316
  (4 other events, 115.0 us)

commit v3 on v2

--- a/solution.py
+++ b/solution.py
@@ -141,9 +141,7 @@
         outs[s][...] = held[s]
 
 
-def gradients_kernel(
-    ids, mine, recv, d_mine, d_recv, inner, tokens, cot, kept, sent, acts, scale, tail
-):
+def elementwise_kernel(ids, mine, recv, d_mine, d_recv, acts, scale, tail):
     inv_rms, gate, up, activated, slope = activations(mine, recv)
     d_inner = (d_mine[...].astype(F32) + d_recv[...].astype(F32)) * inv_rms
     d_gate = (d_inner * up * slope).astype(BF16)
@@ -159,6 +157,9 @@
         head, rest = split_float(rows)
         tail[k1, :, :128] = head.astype(BF16)
         tail[k1, :, 128:] = rest.astype(BF16)
+
+
+def gradients_kernel(ids, acts, inner, tokens, cot, kept, sent):
     for cc, out in ((1, sent), (0, kept)):
         for w in range(3):
             right = inner[...] if w == 2 else acts[:, 384 * w : 384 * w + 384]
@@ -278,17 +279,12 @@
         1 << 29,
     )
     forward = scatter_x(forward)
-    inner = after(inner, *forward[1:])
-    kept, sent, acts, scale, tail = call(
-        gradients_kernel,
-        ids,
-        [send, recv, d_send, swap(d_send, "zh"), inner, tok_all, cot_all],
-        [VMEM] * 7,
-        [((3, 4, 256, 384), BF16)] * 2
-        + [((256, 768), BF16), ((128, 128), F32), ((2, 16, 256), BF16)],
-        (),
-        16,
-        1 << 31,
+    acts, scale, tail = call(
+        elementwise_kernel,
+        ids,
+        [send, recv, d_send, swap(d_send, "zh")],
+        [VMEM] * 4,
+        [((256, 768), BF16), ((128, 128), F32), ((2, 16, 256), BF16)],
     )
     backward = call(
         backward_outputs_kernel,
@@ -299,6 +295,16 @@
         [held],
         8,
         1 << 30,
+    )
+    kept, sent = call(
+        gradients_kernel,
+        ids,
+        [acts, after(inner, *forward[1:], backward[0]), tok_all, cot_all],
+        [VMEM] * 4,
+        [((3, 4, 256, 384), BF16)] * 2,
+        (),
+        16,
+        1 << 31,
     )
     backward = scatter_x(backward)
     sums = list(

time: 145 us -> 143 us (0.986)
  the two profiles are of different devices: /device:TPU:97 before, /device:TPU:64 now
where the time goes in v3:
time: 143 us
  waiting for transfers between devices  83.7 us (59%)
  starting transfers between devices  38.5 us (27%)
  Pallas kernels  16.7 us (12%)
  other arithmetic  1.99 us (1%)
    ppermute x18, waiting for transfers between devices, shift(): return lax.ppermute(array, axis, [(i, (i + by) % 4) for i in range(4)])  52 us
    ppermute x18, starting transfers between devices, shift(): return lax.ppermute(array, axis, [(i, (i + by) % 4) for i in range(4)])  20.7 us
    pallas_call x12, Pallas kernels, call(): pl.pallas_call(body, out_shape=[jax.ShapeDtypeStruct(s, d) for s, d in ou...  16.7 us
    ppermute x4, waiting for transfers between devices, on_device(): by_z = [lax.ppermute(pair, ('zh', 'zl'), z_pairs(k)) for k in range(4)]  16.1 us
    ppermute x7, waiting for transfers between devices, swap(): return lax.ppermute(array, axis, [(0, 1), (1, 0)])  9.37 us
    ppermute x4, starting transfers between devices, on_device(): by_z = [lax.ppermute(pair, ('zh', 'zl'), z_pairs(k)) for k in range(4)]  8.48 us
    ppermute x4, waiting for transfers between devices, on_device(): lax.ppermute(blocks[k], ('zh', 'zl'), [(t, s) for s, t in z_pairs(k)])  6.25 us
    ppermute x7, starting transfers between devices, swap(): return lax.ppermute(array, axis, [(0, 1), (1, 0)])  5.89 us
  transfers between devices with their start and end apart: 33, of which 19 were waited for; matrix products, arithmetic and copies ran while one was open for 1% of the time, Pallas kernels for 8%

profile of v3, /device:TPU:64, one launch (start us, length us, event | category | flops | bytes accessed | tf_op | source)
XLA Modules:
  0.0 143.0 jit_solution(14084679206603158018)
XLA Ops:
  2.8 3.1 %collective-permute-start.8 = (bf16[3,256,384]{2,1,0:T(8,128)(2,1)S(1)}, bf16[3,256,384]{2,1,0:T(8,128)(2,1)S(1)}, u32[]{:S(2)}, u32[]{:S(2)}) collective-permute-start(bf16[3,256,384]{2,1,0:T(8,128)(2,1)S(1)} %pad_maximum_fusion.refs_4_.refs_0_), channel_id=1, source_target_pairs={{0,96},{32,0},{64,32},{96,64},{1,97},{33,1},{65,33},{97,65},{2,98}... | collective-permute-start | bytes 1769480 | tf_op jit(solution)/shard_map/ppermute | solution.py:27
  6.8 5.0 %collective-permute-start.3 = (bf16[2,128,256]{2,1,0:T(8,128)(2,1)S(1)}, bf16[2,128,256]{2,1,0:T(8,128)(2,1)S(1)}, u32[]{:S(2)}, u32[]{:S(2)}) collective-permute-start(bf16[2,128,256]{2,1,0:T(8,128)(2,1)S(1)} %pad_maximum_fusion.1), channel_id=1, source_target_pairs={{0,12},{4,8},{8,140},{12,136},{128,4},{132,0},{136,132},{140,128},... | collective-permute-start | bytes 393224 | tf_op jit(solution)/shard_map/ppermute | solution.py:240
  11.9 1.5 %collective-permute-start.2 = (bf16[2,128,256]{2,1,0:T(8,128)(2,1)S(1)}, bf16[2,128,256]{2,1,0:T(8,128)(2,1)S(1)}, u32[]{:S(2)}, u32[]{:S(2)}) collective-permute-start(bf16[2,128,256]{2,1,0:T(8,128)(2,1)S(1)} %pad_maximum_fusion.1), channel_id=1, source_target_pairs={{0,8},{4,12},{8,136},{12,140},{128,0},{132,4},{136,128},{140,132},... | collective-permute-start | bytes 393224 | tf_op jit(solution)/shard_map/ppermute | solution.py:240
  13.4 8.6 %collective-permute-done.3.p3 = bf16[2,128,256]{2,1,0:T(8,128)(2,1)S(1)} collective-permute-done((bf16[2,128,256]{2,1,0:T(8,128)(2,1)S(1)}, bf16[2,128,256]{2,1,0:T(8,128)(2,1)S(1)}, u32[]{:S(2)}, u32[]{:S(2)}) %collective-permute-start.3) | collective-permute-done | bytes 131104 | tf_op jit(solution)/shard_map/ppermute | solution.py:240
  22.0 1.9 %collective-permute-start = (bf16[2,128,256]{2,1,0:T(8,128)(2,1)S(1)}, bf16[2,128,256]{2,1,0:T(8,128)(2,1)S(1)}, u32[]{:S(2)}, u32[]{:S(2)}) collective-permute-start(bf16[2,128,256]{2,1,0:T(8,128)(2,1)S(1)} %pad_maximum_fusion.1), channel_id=1, source_target_pairs={{0,0},{4,4},{8,128},{12,132},{128,8},{132,12},{136,136},{140,140},... | collective-permute-start | bytes 393224 | tf_op jit(solution)/shard_map/ppermute | solution.py:240
  25.3 6.1 %collective-permute-done.p0 = bf16[2,128,256]{2,1,0:T(8,128)(2,1)S(1)} collective-permute-done((bf16[2,128,256]{2,1,0:T(8,128)(2,1)S(1)}, bf16[2,128,256]{2,1,0:T(8,128)(2,1)S(1)}, u32[]{:S(2)}, u32[]{:S(2)}) %collective-permute-start) | collective-permute-done | bytes 131104 | tf_op jit(solution)/shard_map/ppermute | solution.py:240
  31.5 1.9 %collective-permute-start.9 = (bf16[3,256,384]{2,1,0:T(8,128)(2,1)S(1)}, bf16[3,256,384]{2,1,0:T(8,128)(2,1)S(1)}, u32[]{:S(2)}, u32[]{:S(2)}) collective-permute-start(bf16[3,256,384]{2,1,0:T(8,128)(2,1)S(1)} %pad_maximum_fusion.refs_4_.refs_0_), channel_id=1, source_target_pairs={{0,64},{32,96},{64,0},{96,32},{1,65},{33,97},{65,1},{97,33},{2,66}... | collective-permute-start | bytes 1769480 | tf_op jit(solution)/shard_map/ppermute | solution.py:27
  34.1 2.8 %collective-permute-start.6 = (bf16[4,128,256]{2,1,0:T(8,128)(2,1)S(1)}, bf16[4,128,256]{2,1,0:T(8,128)(2,1)S(1)}, u32[]{:S(2)}, u32[]{:S(2)}) collective-permute-start(bf16[4,128,256]{2,1,0:T(8,128)(2,1)S(1)} %get-tuple-element.49.refs_0_), channel_id=1, source_target_pairs={{0,3},{1,0},{2,1},{3,2},{4,7},{5,4},{6,5},{7,6},{8,11},{9,8},{10,9... | collective-permute-start | bytes 786440 | tf_op jit(solution)/shard_map/ppermute | solution.py:27
  38.6 8.6 %collective-permute-done.6.refs_3_ = bf16[4,128,256]{2,1,0:T(8,128)(2,1)S(1)} collective-permute-done((bf16[4,128,256]{2,1,0:T(8,128)(2,1)S(1)}, bf16[4,128,256]{2,1,0:T(8,128)(2,1)S(1)}, u32[]{:S(2)}, u32[]{:S(2)}) %collective-permute-start.6) | collective-permute-done | bytes 262176 | tf_op jit(solution)/shard_map/ppermute | solution.py:27
  47.7 3.2 %collective-permute-done.4.refs_1_ = bf16[4,128,256]{2,1,0:T(8,128)(2,1)S(1)} collective-permute-done((bf16[4,128,256]{2,1,0:T(8,128)(2,1)S(1)}, bf16[4,128,256]{2,1,0:T(8,128)(2,1)S(1)}, u32[]{:S(2)}, u32[]{:S(2)}) %collective-permute-start.4) | collective-permute-done | bytes 262176 | tf_op jit(solution)/shard_map/ppermute | solution.py:27
  50.9 2.0 %collective-permute-done.12.refs_10_.refs_6_ = bf16[3,256,384]{2,1,0:T(8,128)(2,1)S(1)} collective-permute-done((bf16[3,256,384]{2,1,0:T(8,128)(2,1)S(1)}, bf16[3,256,384]{2,1,0:T(8,128)(2,1)S(1)}, u32[]{:S(2)}, u32[]{:S(2)}) %collective-permute-start.12) | collective-permute-done | bytes 589856 | tf_op jit(solution)/shard_map/ppermute | solution.py:31
  52.8 1.9 %shard_map.102 = (bf16[272,768]{1,0:T(8,128)(2,1)S(1)}, bf16[256,2048]{1,0:T(8,128)(2,1)S(1)}) custom-call(s32[5]{0:T(128)S(1)} %stack.44.ids, bf16[4,128,256]{2,1,0:T(8,128)(2,1)S(1)} %get-tuple-element.49.refs_0_, bf16[4,128,256]{2,1,0:T(8,128)(2,1)S(1)} %collective-permute-done.4.refs_1_, bf16[4,128,256]{2,1,0:T(8,128)(2,1)S(1)} %collective-permute-done.5.refs_2_, ...), custom_call_target="tpu_custom_call" | custom-call | bytes 7249920 | tf_op jit(solution)/shard_map/pallas_call | solution.py:52
  54.9 1.7 %collective-permute-start.16 = (bf16[4,128,256]{2,1,0:T(8,128)(2,1)S(1)}, bf16[4,128,256]{2,1,0:T(8,128)(2,1)S(1)}, u32[]{:S(2)}, u32[]{:S(2)}) collective-permute-start(bf16[4,128,256]{2,1,0:T(8,128)(2,1)S(1)} %get-tuple-element.56.refs_0_), channel_id=1, source_target_pairs={{0,3},{1,0},{2,1},{3,2},{4,7},{5,4},{6,5},{7,6},{8,11},{9,8},{10,9... | collective-permute-start | bytes 786440 | tf_op jit(solution)/shard_map/ppermute | solution.py:27
  57.6 6.5 %collective-permute-done.16.refs_3_ = bf16[4,128,256]{2,1,0:T(8,128)(2,1)S(1)} collective-permute-done((bf16[4,128,256]{2,1,0:T(8,128)(2,1)S(1)}, bf16[4,128,256]{2,1,0:T(8,128)(2,1)S(1)}, u32[]{:S(2)}, u32[]{:S(2)}) %collective-permute-start.16) | collective-permute-done | bytes 262176 | tf_op jit(solution)/shard_map/ppermute | solution.py:27
  64.1 3.2 %collective-permute-done.15.refs_2_ = bf16[4,128,256]{2,1,0:T(8,128)(2,1)S(1)} collective-permute-done((bf16[4,128,256]{2,1,0:T(8,128)(2,1)S(1)}, bf16[4,128,256]{2,1,0:T(8,128)(2,1)S(1)}, u32[]{:S(2)}, u32[]{:S(2)}) %collective-permute-start.15) | collective-permute-done | bytes 262176 | tf_op jit(solution)/shard_map/ppermute | solution.py:27
  67.3 4.2 %collective-permute-done.14.refs_1_ = bf16[4,128,256]{2,1,0:T(8,128)(2,1)S(1)} collective-permute-done((bf16[4,128,256]{2,1,0:T(8,128)(2,1)S(1)}, bf16[4,128,256]{2,1,0:T(8,128)(2,1)S(1)}, u32[]{:S(2)}, u32[]{:S(2)}) %collective-permute-start.14) | collective-permute-done | bytes 262176 | tf_op jit(solution)/shard_map/ppermute | solution.py:27
  72.8 5.7 %collective-permute-start.21 = (bf16[256,384]{1,0:T(8,128)(2,1)S(1)}, bf16[256,384]{1,0:T(8,128)(2,1)S(1)}, u32[]{:S(2)}, u32[]{:S(2)}) collective-permute-start(bf16[256,384]{1,0:T(8,128)(2,1)S(1)} %get-tuple-element.57.d_mine), channel_id=1, source_target_pairs={{0,128},{128,0},{1,129},{129,1},{2,130},{130,2},{3,131},{131,3},{4... | collective-permute-start | bytes 589832 | tf_op jit(solution)/shard_map/ppermute | solution.py:31
  78.5 1.7 %shard_map.104 = (bf16[256,384]{1,0:T(8,128)(2,1)S(1)}, bf16[4,128,256]{2,1,0:T(8,128)(2,1)S(1)}, bf16[4,128,256]{2,1,0:T(8,128)(2,1)S(1)}, bf16[4,128,256]{2,1,0:T(8,128)(2,1)S(1)}, bf16[4,128,256]{2,1,0:T(8,128)(2,1)S(1)}) custom-call(s32[5]{0:T(128)S(1)} %stack.44.ids, bf16[272,768]{1,0:T(8,128)(2,1)S(1)} %get-tuple-element.58.mine, ...), custom_call_target="tpu_custom_call" | custom-call | flops 536870912 | bytes 6799360 | tf_op jit(solution)/shard_map/pallas_call | solution.py:52
  82.3 5.3 %collective-permute-done.21.d_recv = bf16[256,384]{1,0:T(8,128)(2,1)S(1)} collective-permute-done((bf16[256,384]{1,0:T(8,128)(2,1)S(1)}, bf16[256,384]{1,0:T(8,128)(2,1)S(1)}, u32[]{:S(2)}, u32[]{:S(2)}) %collective-permute-start.21) | collective-permute-done | bytes 196640 | tf_op jit(solution)/shard_map/ppermute | solution.py:31
  88.8 1.9 %shard_map.106 = (bf16[4,144,256]{2,1,0:T(8,128)(2,1)S(1)}, bf16[4,144,256]{2,1,0:T(8,128)(2,1)S(1)}, bf16[4,144,256]{2,1,0:T(8,128)(2,1)S(1)}, bf16[4,144,256]{2,1,0:T(8,128)(2,1)S(1)}) custom-call(s32[5]{0:T(128)S(1)} %stack.44.ids, bf16[256,768]{1,0:T(8,128)(2,1)S(1)} %get-tuple-element.63.acts, bf16[2,16,256]{2,1,0:T(8,128)(2,1)S(1)} %get-tuple-element.64.tail, ...), custom_call_target="tpu_custom_call" | custom-call | flops 1073741824 | bytes 6307840 | tf_op jit(solution)/shard_map/pallas_call | solution.py:52
  91.9 3.1 %collective-permute-done.20.refs_3_ = bf16[4,128,256]{2,1,0:T(8,128)(2,1)S(1)} collective-permute-done((bf16[4,128,256]{2,1,0:T(8,128)(2,1)S(1)}, bf16[4,128,256]{2,1,0:T(8,128)(2,1)S(1)}, u32[]{:S(2)}, u32[]{:S(2)}) %collective-permute-start.20) | collective-permute-done | bytes 262176 | tf_op jit(solution)/shard_map/ppermute | solution.py:27
  95.0 2.4 %shard_map.109 = (bf16[3,4,256,384]{3,2,1,0:T(8,128)(2,1)S(1)}, bf16[3,4,256,384]{3,2,1,0:T(8,128)(2,1)S(1)}) custom-call(s32[5]{0:T(128)S(1)} %stack.44.ids, bf16[256,768]{1,0:T(8,128)(2,1)S(1)} %get-tuple-element.63.acts, bf16[256,384]{1,0:T(8,128)(2,1)S(1)} %get-tuple-element.73.inner, bf16[256,2048]{1,0:T(8,128)(2,1)S(1)} %get-tuple-element.74.tokens, ...), custom_call_target="tpu_custom_call" | custom-call | flops 2147483648 | bytes 7405568 | tf_op jit(solution)/shard_map/pallas_call | solution.py:52
  100.0 2.1 %collective-permute-done.27.recv = bf16[3,4,256,384]{3,2,1,0:T(8,128)(2,1)S(1)} collective-permute-done((bf16[3,4,256,384]{3,2,1,0:T(8,128)(2,1)S(1)}, bf16[3,4,256,384]{3,2,1,0:T(8,128)(2,1)S(1)}, u32[]{:S(2)}, u32[]{:S(2)}) %collective-permute-start.27) | collective-permute-done | bytes 2359328 | tf_op jit(solution)/shard_map/ppermute | solution.py:31
  103.2 1.4 collective-permute-start.28
  105.4 2.0 %collective-permute-done.22.refs_5_ = bf16[4,144,256]{2,1,0:T(8,128)(2,1)S(1)} collective-permute-done((bf16[4,144,256]{2,1,0:T(8,128)(2,1)S(1)}, bf16[4,144,256]{2,1,0:T(8,128)(2,1)S(1)}, u32[]{:S(2)}, u32[]{:S(2)}) %collective-permute-start.22) | collective-permute-done | bytes 294944 | tf_op jit(solution)/shard_map/ppermute | solution.py:27
  107.4 2.7 %collective-permute-done.23.refs_6_ = bf16[4,144,256]{2,1,0:T(8,128)(2,1)S(1)} collective-permute-done((bf16[4,144,256]{2,1,0:T(8,128)(2,1)S(1)}, bf16[4,144,256]{2,1,0:T(8,128)(2,1)S(1)}, u32[]{:S(2)}, u32[]{:S(2)}) %collective-permute-start.23) | collective-permute-done | bytes 294944 | tf_op jit(solution)/shard_map/ppermute | solution.py:27
  110.1 5.5 %collective-permute-done.24.refs_7_ = bf16[4,144,256]{2,1,0:T(8,128)(2,1)S(1)} collective-permute-done((bf16[4,144,256]{2,1,0:T(8,128)(2,1)S(1)}, bf16[4,144,256]{2,1,0:T(8,128)(2,1)S(1)}, u32[]{:S(2)}, u32[]{:S(2)}) %collective-permute-start.24) | collective-permute-done | bytes 294944 | tf_op jit(solution)/shard_map/ppermute | solution.py:27
  116.3 1.7 %collective-permute-start.32 = (bf16[3,256,384]{2,1,0:T(8,128)(2,1)S(1)}, bf16[3,256,384]{2,1,0:T(8,128)(2,1)S(1)}, u32[]{:S(2)}, u32[]{:S(2)}) collective-permute-start(bf16[3,256,384]{2,1,0:T(8,128)(2,1)S(1)} %get-tuple-element.86), channel_id=1, source_target_pairs={{0,64},{32,96},{64,0},{96,32},{1,65},{33,97},{65,1},{97,33},{2,66}... | collective-permute-start | bytes 1769480 | tf_op jit(solution)/shard_map/ppermute | solution.py:27
  118.0 2.2 %collective-permute-start.25 = (bf16[272,256]{1,0:T(8,128)(2,1)S(1)}, bf16[272,256]{1,0:T(8,128)(2,1)S(1)}, u32[]{:S(2)}, u32[]{:S(2)}) collective-permute-start(bf16[272,256]{1,0:T(8,128)(2,1)S(1)} %get-tuple-element.69), channel_id=1, source_target_pairs={{0,0},{4,4},{128,8},{132,12},{8,128},{12,132},{136,136},{140,140},... | collective-permute-start | bytes 417800 | tf_op jit(solution)/shard_map/ppermute | solution.py:322
  122.1 11.4 %collective-permute-done.30.p3 = bf16[3,256,384]{2,1,0:T(8,128)(2,1)S(1)} collective-permute-done((bf16[3,256,384]{2,1,0:T(8,128)(2,1)S(1)}, bf16[3,256,384]{2,1,0:T(8,128)(2,1)S(1)}, u32[]{:S(2)}, u32[]{:S(2)}) %collective-permute-start.30) | collective-permute-done | bytes 589856 | tf_op jit(solution)/shard_map/ppermute | solution.py:27
  133.5 1.8 %shard_map.111 = (f32[256,384]{1,0:T(8,128)}, f32[256,384]{1,0:T(8,128)}, f32[384,256]{1,0:T(8,128)}) custom-call(s32[5]{0:T(128)S(1)} %stack.44.ids, bf16[3,256,384]{2,1,0:T(8,128)(2,1)S(1)} %get-tuple-element.84.p0, bf16[3,256,384]{2,1,0:T(8,128)(2,1)S(1)} %collective-permute-done.28.p1, bf16[3,256,384]{2,1,0:T(8,128)(2,1)S(1)} %collective-permute-done.32.p2, ...), custom_call_target="tpu_custom_call" | custom-call | bytes 2949120 | tf_op jit(solution)/shard_map/pallas_call | solution.py:52
  135.3 6.2 %collective-permute-done.31.p3 = bf16[272,256]{1,0:T(8,128)(2,1)S(1)} collective-permute-done((bf16[272,256]{1,0:T(8,128)(2,1)S(1)}, bf16[272,256]{1,0:T(8,128)(2,1)S(1)}, u32[]{:S(2)}, u32[]{:S(2)}) %collective-permute-start.31) | collective-permute-done | bytes 139296 | tf_op jit(solution)/shard_map/ppermute | solution.py:322
  (56 shorter events, 22.8 us)
Async XLA Ops:
  2.8 28.6 %collective-permute-start.8 = (bf16[3,256,384]{2,1,0:T(8,128)(2,1)S(1)}, bf16[3,256,384]{2,1,0:T(8,128)(2,1)S(1)}, u32[]{:S(2)}, u32[]{:S(2)}) collective-permute-start(bf16[3,256,384]{2,1,0:T(8,128)(2,1)S(1)} %pad_maximum_fusion.refs_4_.refs_0_), channel_id=1, source_target_pairs={{0,96},{32,0},{64,32},{96,64},{1,97},{33,1},{65,33},{97,65},{2,98}... | collective-permute-start | bytes 1769480 | tf_op jit(solution)/shard_map/ppermute | solution.py:27
  5.9 25.5 %collective-permute-start.7 = (bf16[3,256,384]{2,1,0:T(8,128)(2,1)S(1)}, bf16[3,256,384]{2,1,0:T(8,128)(2,1)S(1)}, u32[]{:S(2)}, u32[]{:S(2)}) collective-permute-start(bf16[3,256,384]{2,1,0:T(8,128)(2,1)S(1)} %pad_maximum_fusion.refs_4_.refs_0_), channel_id=1, source_target_pairs={{0,32},{32,64},{64,96},{96,0},{1,33},{33,65},{65,97},{97,1},{2,34}... | collective-permute-start | bytes 1769480 | tf_op jit(solution)/shard_map/ppermute | solution.py:27
  6.8 15.2 %collective-permute-start.3 = (bf16[2,128,256]{2,1,0:T(8,128)(2,1)S(1)}, bf16[2,128,256]{2,1,0:T(8,128)(2,1)S(1)}, u32[]{:S(2)}, u32[]{:S(2)}) collective-permute-start(bf16[2,128,256]{2,1,0:T(8,128)(2,1)S(1)} %pad_maximum_fusion.1), channel_id=1, source_target_pairs={{0,12},{4,8},{8,140},{12,136},{128,4},{132,0},{136,132},{140,128},... | collective-permute-start | bytes 393224 | tf_op jit(solution)/shard_map/ppermute | solution.py:240
  11.9 12.1 %collective-permute-start.2 = (bf16[2,128,256]{2,1,0:T(8,128)(2,1)S(1)}, bf16[2,128,256]{2,1,0:T(8,128)(2,1)S(1)}, u32[]{:S(2)}, u32[]{:S(2)}) collective-permute-start(bf16[2,128,256]{2,1,0:T(8,128)(2,1)S(1)} %pad_maximum_fusion.1), channel_id=1, source_target_pairs={{0,8},{4,12},{8,136},{12,140},{128,0},{132,4},{136,128},{140,132},... | collective-permute-start | bytes 393224 | tf_op jit(solution)/shard_map/ppermute | solution.py:240
  13.3 12.0 %collective-permute-start.1 = (bf16[2,128,256]{2,1,0:T(8,128)(2,1)S(1)}, bf16[2,128,256]{2,1,0:T(8,128)(2,1)S(1)}, u32[]{:S(2)}, u32[]{:S(2)}) collective-permute-start(bf16[2,128,256]{2,1,0:T(8,128)(2,1)S(1)} %pad_maximum_fusion.1), channel_id=1, source_target_pairs={{0,4},{4,0},{8,132},{12,128},{128,12},{132,8},{136,140},{140,136},... | collective-permute-start | bytes 393224 | tf_op jit(solution)/shard_map/ppermute | solution.py:240
  22.0 9.4 %collective-permute-start = (bf16[2,128,256]{2,1,0:T(8,128)(2,1)S(1)}, bf16[2,128,256]{2,1,0:T(8,128)(2,1)S(1)}, u32[]{:S(2)}, u32[]{:S(2)}) collective-permute-start(bf16[2,128,256]{2,1,0:T(8,128)(2,1)S(1)} %pad_maximum_fusion.1), channel_id=1, source_target_pairs={{0,0},{4,4},{8,128},{12,132},{128,8},{132,12},{136,136},{140,140},... | collective-permute-start | bytes 393224 | tf_op jit(solution)/shard_map/ppermute | solution.py:240
  31.5 19.4 %collective-permute-start.9 = (bf16[3,256,384]{2,1,0:T(8,128)(2,1)S(1)}, bf16[3,256,384]{2,1,0:T(8,128)(2,1)S(1)}, u32[]{:S(2)}, u32[]{:S(2)}) collective-permute-start(bf16[3,256,384]{2,1,0:T(8,128)(2,1)S(1)} %pad_maximum_fusion.refs_4_.refs_0_), channel_id=1, source_target_pairs={{0,64},{32,96},{64,0},{96,32},{1,65},{33,97},{65,1},{97,33},{2,66}... | collective-permute-start | bytes 1769480 | tf_op jit(solution)/shard_map/ppermute | solution.py:27
  34.1 13.1 %collective-permute-start.6 = (bf16[4,128,256]{2,1,0:T(8,128)(2,1)S(1)}, bf16[4,128,256]{2,1,0:T(8,128)(2,1)S(1)}, u32[]{:S(2)}, u32[]{:S(2)}) collective-permute-start(bf16[4,128,256]{2,1,0:T(8,128)(2,1)S(1)} %get-tuple-element.49.refs_0_), channel_id=1, source_target_pairs={{0,3},{1,0},{2,1},{3,2},{4,7},{5,4},{6,5},{7,6},{8,11},{9,8},{10,9... | collective-permute-start | bytes 786440 | tf_op jit(solution)/shard_map/ppermute | solution.py:27
  36.9 10.8 %collective-permute-start.5 = (bf16[4,128,256]{2,1,0:T(8,128)(2,1)S(1)}, bf16[4,128,256]{2,1,0:T(8,128)(2,1)S(1)}, u32[]{:S(2)}, u32[]{:S(2)}) collective-permute-start(bf16[4,128,256]{2,1,0:T(8,128)(2,1)S(1)} %get-tuple-element.49.refs_0_), channel_id=1, source_target_pairs={{0,2},{1,3},{2,0},{3,1},{4,6},{5,7},{6,4},{7,5},{8,10},{9,11},{10,... | collective-permute-start | bytes 786440 | tf_op jit(solution)/shard_map/ppermute | solution.py:27
  37.7 13.1 %collective-permute-start.4 = (bf16[4,128,256]{2,1,0:T(8,128)(2,1)S(1)}, bf16[4,128,256]{2,1,0:T(8,128)(2,1)S(1)}, u32[]{:S(2)}, u32[]{:S(2)}) collective-permute-start(bf16[4,128,256]{2,1,0:T(8,128)(2,1)S(1)} %get-tuple-element.49.refs_0_), channel_id=1, source_target_pairs={{0,1},{1,2},{2,3},{3,0},{4,5},{5,6},{6,7},{7,4},{8,9},{9,10},{10,1... | collective-permute-start | bytes 786440 | tf_op jit(solution)/shard_map/ppermute | solution.py:27
  38.6 12.3 %collective-permute-start.10 = (bf16[3,256,384]{2,1,0:T(8,128)(2,1)S(1)}, bf16[3,256,384]{2,1,0:T(8,128)(2,1)S(1)}, u32[]{:S(2)}, u32[]{:S(2)}) collective-permute-start(bf16[3,256,384]{2,1,0:T(8,128)(2,1)S(1)} %pad_maximum_fusion.refs_4_.refs_0_), channel_id=1, source_target_pairs={{0,16},{16,0},{1,17},{17,1},{2,18},{18,2},{3,19},{19,3},{4,20},{20... | collective-permute-start | bytes 1769480 | tf_op jit(solution)/shard_map/ppermute | solution.py:31
  47.2 3.7 %collective-permute-start.11 = (bf16[3,256,384]{2,1,0:T(8,128)(2,1)S(1)}, bf16[3,256,384]{2,1,0:T(8,128)(2,1)S(1)}, u32[]{:S(2)}, u32[]{:S(2)}) collective-permute-start(bf16[3,256,384]{2,1,0:T(8,128)(2,1)S(1)} %collective-permute-done.7.refs_5_.refs_1_), channel_id=1, source_target_pairs={{0,16},{16,0},{1,17},{17,1},{2,18},{18,2},{3,19},{19,3},{4,20},{20... | collective-permute-start | bytes 1769480 | tf_op jit(solution)/shard_map/ppermute | solution.py:31
  47.7 3.2 %collective-permute-start.13 = (bf16[3,256,384]{2,1,0:T(8,128)(2,1)S(1)}, bf16[3,256,384]{2,1,0:T(8,128)(2,1)S(1)}, u32[]{:S(2)}, u32[]{:S(2)}) collective-permute-start(bf16[3,256,384]{2,1,0:T(8,128)(2,1)S(1)} %collective-permute-done.8.refs_7_.refs_3_), channel_id=1, source_target_pairs={{0,16},{16,0},{1,17},{17,1},{2,18},{18,2},{3,19},{19,3},{4,20},{20... | collective-permute-start | bytes 1769480 | tf_op jit(solution)/shard_map/ppermute | solution.py:31
  54.8 23.7 %collective-permute-start.17 = (bf16[272,768]{1,0:T(8,128)(2,1)S(1)}, bf16[272,768]{1,0:T(8,128)(2,1)S(1)}, u32[]{:S(2)}, u32[]{:S(2)}) collective-permute-start(bf16[272,768]{1,0:T(8,128)(2,1)S(1)} %get-tuple-element.58.mine), channel_id=1, source_target_pairs={{0,128},{128,0},{1,129},{129,1},{2,130},{130,2},{3,131},{131,3},{4... | collective-permute-start | bytes 1253384 | tf_op jit(solution)/shard_map/ppermute | solution.py:31
  54.9 9.2 %collective-permute-start.16 = (bf16[4,128,256]{2,1,0:T(8,128)(2,1)S(1)}, bf16[4,128,256]{2,1,0:T(8,128)(2,1)S(1)}, u32[]{:S(2)}, u32[]{:S(2)}) collective-permute-start(bf16[4,128,256]{2,1,0:T(8,128)(2,1)S(1)} %get-tuple-element.56.refs_0_), channel_id=1, source_target_pairs={{0,3},{1,0},{2,1},{3,2},{4,7},{5,4},{6,5},{7,6},{8,11},{9,8},{10,9... | collective-permute-start | bytes 786440 | tf_op jit(solution)/shard_map/ppermute | solution.py:27
  56.6 10.7 %collective-permute-start.15 = (bf16[4,128,256]{2,1,0:T(8,128)(2,1)S(1)}, bf16[4,128,256]{2,1,0:T(8,128)(2,1)S(1)}, u32[]{:S(2)}, u32[]{:S(2)}) collective-permute-start(bf16[4,128,256]{2,1,0:T(8,128)(2,1)S(1)} %get-tuple-element.56.refs_0_), channel_id=1, source_target_pairs={{0,2},{1,3},{2,0},{3,1},{4,6},{5,7},{6,4},{7,5},{8,10},{9,11},{10,... | collective-permute-start | bytes 786440 | tf_op jit(solution)/shard_map/ppermute | solution.py:27
  56.6 14.9 %collective-permute-start.14 = (bf16[4,128,256]{2,1,0:T(8,128)(2,1)S(1)}, bf16[4,128,256]{2,1,0:T(8,128)(2,1)S(1)}, u32[]{:S(2)}, u32[]{:S(2)}) collective-permute-start(bf16[4,128,256]{2,1,0:T(8,128)(2,1)S(1)} %get-tuple-element.56.refs_0_), channel_id=1, source_target_pairs={{0,1},{1,2},{2,3},{3,0},{4,5},{5,6},{6,7},{7,4},{8,9},{9,10},{10,1... | collective-permute-start | bytes 786440 | tf_op jit(solution)/shard_map/ppermute | solution.py:27
  72.8 14.7 %collective-permute-start.21 = (bf16[256,384]{1,0:T(8,128)(2,1)S(1)}, bf16[256,384]{1,0:T(8,128)(2,1)S(1)}, u32[]{:S(2)}, u32[]{:S(2)}) collective-permute-start(bf16[256,384]{1,0:T(8,128)(2,1)S(1)} %get-tuple-element.57.d_mine), channel_id=1, source_target_pairs={{0,128},{128,0},{1,129},{129,1},{2,130},{130,2},{3,131},{131,3},{4... | collective-permute-start | bytes 589832 | tf_op jit(solution)/shard_map/ppermute | solution.py:31
  80.1 10.6 %collective-permute-start.18 = (bf16[4,128,256]{2,1,0:T(8,128)(2,1)S(1)}, bf16[4,128,256]{2,1,0:T(8,128)(2,1)S(1)}, u32[]{:S(2)}, u32[]{:S(2)}) collective-permute-start(bf16[4,128,256]{2,1,0:T(8,128)(2,1)S(1)} %get-tuple-element.60), channel_id=1, source_target_pairs={{0,3},{1,0},{2,1},{3,2},{4,7},{5,4},{6,5},{7,6},{8,11},{9,8},{10,9... | collective-permute-start | bytes 786440 | tf_op jit(solution)/shard_map/ppermute | solution.py:27
  81.1 10.8 %collective-permute-start.19 = (bf16[4,128,256]{2,1,0:T(8,128)(2,1)S(1)}, bf16[4,128,256]{2,1,0:T(8,128)(2,1)S(1)}, u32[]{:S(2)}, u32[]{:S(2)}) collective-permute-start(bf16[4,128,256]{2,1,0:T(8,128)(2,1)S(1)} %get-tuple-element.61), channel_id=1, source_target_pairs={{0,2},{1,3},{2,0},{3,1},{4,6},{5,7},{6,4},{7,5},{8,10},{9,11},{10,... | collective-permute-start | bytes 786440 | tf_op jit(solution)/shard_map/ppermute | solution.py:27
  81.4 13.6 %collective-permute-start.20 = (bf16[4,128,256]{2,1,0:T(8,128)(2,1)S(1)}, bf16[4,128,256]{2,1,0:T(8,128)(2,1)S(1)}, u32[]{:S(2)}, u32[]{:S(2)}) collective-permute-start(bf16[4,128,256]{2,1,0:T(8,128)(2,1)S(1)} %get-tuple-element.62), channel_id=1, source_target_pairs={{0,1},{1,2},{2,3},{3,0},{4,5},{5,6},{6,7},{7,4},{8,9},{9,10},{10,1... | collective-permute-start | bytes 786440 | tf_op jit(solution)/shard_map/ppermute | solution.py:27
  97.4 4.6 %collective-permute-start.27 = (bf16[3,4,256,384]{3,2,1,0:T(8,128)(2,1)S(1)}, bf16[3,4,256,384]{3,2,1,0:T(8,128)(2,1)S(1)}, u32[]{:S(2)}, u32[]{:S(2)}) collective-permute-start(bf16[3,4,256,384]{3,2,1,0:T(8,128)(2,1)S(1)} %get-tuple-element.77), channel_id=1, source_target_pairs={{0,16},{16,0},{1,17},{17,1},{2,18},{18,2},{3,19},{19,3},{4,20},{20... | collective-permute-start | bytes 7077896 | tf_op jit(solution)/shard_map/ppermute | solution.py:31
  97.5 9.9 %collective-permute-start.22 = (bf16[4,144,256]{2,1,0:T(8,128)(2,1)S(1)}, bf16[4,144,256]{2,1,0:T(8,128)(2,1)S(1)}, u32[]{:S(2)}, u32[]{:S(2)}) collective-permute-start(bf16[4,144,256]{2,1,0:T(8,128)(2,1)S(1)} %get-tuple-element.66), channel_id=1, source_target_pairs={{0,3},{1,0},{2,1},{3,2},{4,7},{5,4},{6,5},{7,6},{8,11},{9,8},{10,9... | collective-permute-start | bytes 884744 | tf_op jit(solution)/shard_map/ppermute | solution.py:27
  98.7 11.4 %collective-permute-start.23 = (bf16[4,144,256]{2,1,0:T(8,128)(2,1)S(1)}, bf16[4,144,256]{2,1,0:T(8,128)(2,1)S(1)}, u32[]{:S(2)}, u32[]{:S(2)}) collective-permute-start(bf16[4,144,256]{2,1,0:T(8,128)(2,1)S(1)} %get-tuple-element.67), channel_id=1, source_target_pairs={{0,2},{1,3},{2,0},{3,1},{4,6},{5,7},{6,4},{7,5},{8,10},{9,11},{10,... | collective-permute-start | bytes 884744 | tf_op jit(solution)/shard_map/ppermute | solution.py:27
  99.1 16.4 %collective-permute-start.24 = (bf16[4,144,256]{2,1,0:T(8,128)(2,1)S(1)}, bf16[4,144,256]{2,1,0:T(8,128)(2,1)S(1)}, u32[]{:S(2)}, u32[]{:S(2)}) collective-permute-start(bf16[4,144,256]{2,1,0:T(8,128)(2,1)S(1)} %get-tuple-element.68), channel_id=1, source_target_pairs={{0,1},{1,2},{2,3},{3,0},{4,5},{5,6},{6,7},{7,4},{8,9},{9,10},{10,1... | collective-permute-start | bytes 884744 | tf_op jit(solution)/shard_map/ppermute | solution.py:27
  103.2 18.8 %collective-permute-start.28 = (bf16[3,256,384]{2,1,0:T(8,128)(2,1)S(1)}, bf16[3,256,384]{2,1,0:T(8,128)(2,1)S(1)}, u32[]{:S(2)}, u32[]{:S(2)}) collective-permute-start(bf16[3,256,384]{2,1,0:T(8,128)(2,1)S(1)} %get-tuple-element.78), channel_id=1, source_target_pairs={{0,96},{32,0},{64,32},{96,64},{1,97},{33,1},{65,33},{97,65},{2,98}... | collective-permute-start | bytes 1769480 | tf_op jit(solution)/shard_map/ppermute | solution.py:27
  104.6 28.9 %collective-permute-start.30 = (bf16[3,256,384]{2,1,0:T(8,128)(2,1)S(1)}, bf16[3,256,384]{2,1,0:T(8,128)(2,1)S(1)}, u32[]{:S(2)}, u32[]{:S(2)}) collective-permute-start(bf16[3,256,384]{2,1,0:T(8,128)(2,1)S(1)} %get-tuple-element.81), channel_id=1, source_target_pairs={{0,32},{32,64},{64,96},{96,0},{1,33},{33,65},{65,97},{97,1},{2,34}... | collective-permute-start | bytes 1769480 | tf_op jit(solution)/shard_map/ppermute | solution.py:27
  116.3 17.2 %collective-permute-start.32 = (bf16[3,256,384]{2,1,0:T(8,128)(2,1)S(1)}, bf16[3,256,384]{2,1,0:T(8,128)(2,1)S(1)}, u32[]{:S(2)}, u32[]{:S(2)}) collective-permute-start(bf16[3,256,384]{2,1,0:T(8,128)(2,1)S(1)} %get-tuple-element.86), channel_id=1, source_target_pairs={{0,64},{32,96},{64,0},{96,32},{1,65},{33,97},{65,1},{97,33},{2,66}... | collective-permute-start | bytes 1769480 | tf_op jit(solution)/shard_map/ppermute | solution.py:27
  118.0 17.3 %collective-permute-start.25 = (bf16[272,256]{1,0:T(8,128)(2,1)S(1)}, bf16[272,256]{1,0:T(8,128)(2,1)S(1)}, u32[]{:S(2)}, u32[]{:S(2)}) collective-permute-start(bf16[272,256]{1,0:T(8,128)(2,1)S(1)} %get-tuple-element.69), channel_id=1, source_target_pairs={{0,0},{4,4},{128,8},{132,12},{8,128},{12,132},{136,136},{140,140},... | collective-permute-start | bytes 417800 | tf_op jit(solution)/shard_map/ppermute | solution.py:322
  120.2 15.1 %collective-permute-start.26 = (bf16[272,256]{1,0:T(8,128)(2,1)S(1)}, bf16[272,256]{1,0:T(8,128)(2,1)S(1)}, u32[]{:S(2)}, u32[]{:S(2)}) collective-permute-start(bf16[272,256]{1,0:T(8,128)(2,1)S(1)} %get-tuple-element.70), channel_id=1, source_target_pairs={{4,0},{0,4},{132,8},{128,12},{12,128},{8,132},{140,136},{136,140},... | collective-permute-start | bytes 417800 | tf_op jit(solution)/shard_map/ppermute | solution.py:322
  122.0 13.3 %collective-permute-start.29 = (bf16[272,256]{1,0:T(8,128)(2,1)S(1)}, bf16[272,256]{1,0:T(8,128)(2,1)S(1)}, u32[]{:S(2)}, u32[]{:S(2)}) collective-permute-start(bf16[272,256]{1,0:T(8,128)(2,1)S(1)} %get-tuple-element.79), channel_id=1, source_target_pairs={{8,0},{12,4},{136,8},{140,12},{0,128},{4,132},{128,136},{132,140},... | collective-permute-start | bytes 417800 | tf_op jit(solution)/shard_map/ppermute | solution.py:322
  133.5 8.1 %collective-permute-start.31 = (bf16[272,256]{1,0:T(8,128)(2,1)S(1)}, bf16[272,256]{1,0:T(8,128)(2,1)S(1)}, u32[]{:S(2)}, u32[]{:S(2)}) collective-permute-start(bf16[272,256]{1,0:T(8,128)(2,1)S(1)} %get-tuple-element.82), channel_id=1, source_target_pairs={{12,0},{8,4},{140,8},{136,12},{4,128},{0,132},{132,136},{128,140},... | collective-permute-start | bytes 417800 | tf_op jit(solution)/shard_map/ppermute | solution.py:322
  (4 other events, 104.8 us)

commit v4 on v3

--- a/solution.py
+++ b/solution.py
@@ -65,7 +65,7 @@
     return q, lax.rem(ids[4] - lax.rem(q, 4) + 4, 4), (ids[3] % 2) ^ (q // 4)
 
 
-def stack_kernel(ids, p0, p1, p2, p3, tokens, cot):
+def stack_kernel(ids, p0, p2, p3, p1, tokens, cot):
     for k, piece in enumerate((p0, p1, p2, p3)):
         tokens[k] = piece[0]
         cot[k] = piece[1]
@@ -238,8 +238,8 @@
     pair = jnp.stack([tokens, out_cotangent])
     own = jnp.stack([gate_weight, up_weight, down_weight.T])
     by_z = [lax.ppermute(pair, ("zh", "zl"), z_pairs(k)) for k in range(4)]
-    tok_z, cot_z = call(stack_kernel, ids, by_z, [VMEM] * 4, [((4, 128, 256), BF16)] * 2)
-    y1, y3, *_ = lax.optimization_barrier((shift(own, "y", 1), shift(own, "y", 3), *by_z))
+    tok_z, cot_z = call(stack_kernel, ids, [by_z[k] for k in (0, 2, 3, 1)], [VMEM] * 4, [((4, 128, 256), BF16)] * 2)
+    y1, y3, *_ = lax.optimization_barrier((shift(own, "y", 1), shift(own, "y", 3), *[by_z[k] for k in (0, 2, 3, 1)]))
     y2 = shift(after(own, y1, y3), "y", 2)
     tok_x = [shift(tok_z, "x", s) for s in (1, 2, 3)]
     y2 = after(y2, *tok_x)
@@ -316,8 +316,8 @@
         body = functools.partial(x_sum_kernel, k)
         parts = [*forward, *backward]
         blocks += call(body, ids, parts, [VMEM] * 8, [((272, 256), BF16)] * 2)
-    blocks[2:] = [after(blocks[2], near[0]), after(blocks[3], near[1])]
-    far = shift(after(sums[2], blocks[0]), "y", 2)
+    blocks[3] = after(blocks[3], *near)
+    far = shift(after(sums[2], blocks[2]), "y", 2)
     blocks = [
         lax.ppermute(blocks[k], ("zh", "zl"), [(t, s) for s, t in z_pairs(k)]) for k in range(4)
     ]

time: 143 us -> 139 us (0.972)
  the two profiles are of different devices: /device:TPU:64 before, /device:TPU:97 now
where the time goes in v4:
time: 139 us; the launch traced here: 138 us
  waiting for transfers between devices  64.4 us (46%)
  starting transfers between devices  53.1 us (38%)
  Pallas kernels  16.7 us (12%)
  other arithmetic  1.99 us (1%)
    ppermute x18, waiting for transfers between devices, shift(): return lax.ppermute(array, axis, [(i, (i + by) % 4) for i in range(4)])  37.8 us
    ppermute x7, starting transfers between devices, swap(): return lax.ppermute(array, axis, [(0, 1), (1, 0)])  19.8 us
    pallas_call x12, Pallas kernels, call(): pl.pallas_call(body, out_shape=[jax.ShapeDtypeStruct(s, d) for s, d in ou...  16.7 us
    ppermute x18, starting transfers between devices, shift(): return lax.ppermute(array, axis, [(i, (i + by) % 4) for i in range(4)])  16.3 us
    ppermute x4, waiting for transfers between devices, on_device(): by_z = [lax.ppermute(pair, ('zh', 'zl'), z_pairs(k)) for k in range(4)]  9.23 us
    ppermute x4, starting transfers between devices, on_device(): by_z = [lax.ppermute(pair, ('zh', 'zl'), z_pairs(k)) for k in range(4)]  9.01 us
    ppermute x7, waiting for transfers between devices, swap(): return lax.ppermute(array, axis, [(0, 1), (1, 0)])  8.98 us
    ppermute x4, waiting for transfers between devices, on_device(): lax.ppermute(blocks[k], ('zh', 'zl'), [(t, s) for s, t in z_pairs(k)])  8.38 us
  transfers between devices with their start and end apart: 33, of which 17 were waited for; matrix products, arithmetic and copies ran while one was open for 1% of the time, Pallas kernels for 8%

profile of v4, /device:TPU:97, one launch (start us, length us, event | category | flops | bytes accessed | tf_op | source)
XLA Modules:
  0.0 138.2 jit_solution(9335829484152047617)
XLA Ops:
  2.8 2.8 %collective-permute-start.8 = (bf16[3,256,384]{2,1,0:T(8,128)(2,1)S(1)}, bf16[3,256,384]{2,1,0:T(8,128)(2,1)S(1)}, u32[]{:S(2)}, u32[]{:S(2)}) collective-permute-start(bf16[3,256,384]{2,1,0:T(8,128)(2,1)S(1)} %pad_maximum_fusion.refs_4_.refs_0_), channel_id=1, source_target_pairs={{0,96},{32,0},{64,32},{96,64},{1,97},{33,1},{65,33},{97,65},{2,98}... | collective-permute-start | bytes 1769480 | tf_op jit(solution)/shard_map/ppermute | solution.py:27
  6.6 2.9 %collective-permute-start.3 = (bf16[2,128,256]{2,1,0:T(8,128)(2,1)S(1)}, bf16[2,128,256]{2,1,0:T(8,128)(2,1)S(1)}, u32[]{:S(2)}, u32[]{:S(2)}) collective-permute-start(bf16[2,128,256]{2,1,0:T(8,128)(2,1)S(1)} %pad_maximum_fusion.1), channel_id=1, source_target_pairs={{0,4},{4,0},{8,132},{12,128},{128,12},{132,8},{136,140},{140,136},... | collective-permute-start | bytes 393224 | tf_op jit(solution)/shard_map/ppermute | solution.py:240
  9.5 1.6 %collective-permute-start.2 = (bf16[2,128,256]{2,1,0:T(8,128)(2,1)S(1)}, bf16[2,128,256]{2,1,0:T(8,128)(2,1)S(1)}, u32[]{:S(2)}, u32[]{:S(2)}) collective-permute-start(bf16[2,128,256]{2,1,0:T(8,128)(2,1)S(1)} %pad_maximum_fusion.1), channel_id=1, source_target_pairs={{0,12},{4,8},{8,140},{12,136},{128,4},{132,0},{136,132},{140,128},... | collective-permute-start | bytes 393224 | tf_op jit(solution)/shard_map/ppermute | solution.py:240
  11.1 1.4 %collective-permute-start.1 = (bf16[2,128,256]{2,1,0:T(8,128)(2,1)S(1)}, bf16[2,128,256]{2,1,0:T(8,128)(2,1)S(1)}, u32[]{:S(2)}, u32[]{:S(2)}) collective-permute-start(bf16[2,128,256]{2,1,0:T(8,128)(2,1)S(1)} %pad_maximum_fusion.1), channel_id=1, source_target_pairs={{0,8},{4,12},{8,136},{12,140},{128,0},{132,4},{136,128},{140,132},... | collective-permute-start | bytes 393224 | tf_op jit(solution)/shard_map/ppermute | solution.py:240
  12.6 3.2 %collective-permute-done.3.p1 = bf16[2,128,256]{2,1,0:T(8,128)(2,1)S(1)} collective-permute-done((bf16[2,128,256]{2,1,0:T(8,128)(2,1)S(1)}, bf16[2,128,256]{2,1,0:T(8,128)(2,1)S(1)}, u32[]{:S(2)}, u32[]{:S(2)}) %collective-permute-start.3) | collective-permute-done | bytes 131104 | tf_op jit(solution)/shard_map/ppermute | solution.py:240
  15.8 3.0 %collective-permute-start = (bf16[2,128,256]{2,1,0:T(8,128)(2,1)S(1)}, bf16[2,128,256]{2,1,0:T(8,128)(2,1)S(1)}, u32[]{:S(2)}, u32[]{:S(2)}) collective-permute-start(bf16[2,128,256]{2,1,0:T(8,128)(2,1)S(1)} %pad_maximum_fusion.1), channel_id=1, source_target_pairs={{0,0},{4,4},{8,128},{12,132},{128,8},{132,12},{136,136},{140,140},... | collective-permute-start | bytes 393224 | tf_op jit(solution)/shard_map/ppermute | solution.py:240
  18.8 5.4 %collective-permute-done.1.p2 = bf16[2,128,256]{2,1,0:T(8,128)(2,1)S(1)} collective-permute-done((bf16[2,128,256]{2,1,0:T(8,128)(2,1)S(1)}, bf16[2,128,256]{2,1,0:T(8,128)(2,1)S(1)}, u32[]{:S(2)}, u32[]{:S(2)}) %collective-permute-start.1) | collective-permute-done | bytes 131104 | tf_op jit(solution)/shard_map/ppermute | solution.py:240
  24.8 1.6 %collective-permute-start.9 = (bf16[3,256,384]{2,1,0:T(8,128)(2,1)S(1)}, bf16[3,256,384]{2,1,0:T(8,128)(2,1)S(1)}, u32[]{:S(2)}, u32[]{:S(2)}) collective-permute-start(bf16[3,256,384]{2,1,0:T(8,128)(2,1)S(1)} %pad_maximum_fusion.refs_4_.refs_0_), channel_id=1, source_target_pairs={{0,64},{32,96},{64,0},{96,32},{1,65},{33,97},{65,1},{97,33},{2,66}... | collective-permute-start | bytes 1769480 | tf_op jit(solution)/shard_map/ppermute | solution.py:27
  27.1 2.6 %collective-permute-start.6 = (bf16[4,128,256]{2,1,0:T(8,128)(2,1)S(1)}, bf16[4,128,256]{2,1,0:T(8,128)(2,1)S(1)}, u32[]{:S(2)}, u32[]{:S(2)}) collective-permute-start(bf16[4,128,256]{2,1,0:T(8,128)(2,1)S(1)} %get-tuple-element.48.refs_0_), channel_id=1, source_target_pairs={{0,3},{1,0},{2,1},{3,2},{4,7},{5,4},{6,5},{7,6},{8,11},{9,8},{10,9... | collective-permute-start | bytes 786440 | tf_op jit(solution)/shard_map/ppermute | solution.py:27
  30.8 4.6 %collective-permute-start.10 = (bf16[3,256,384]{2,1,0:T(8,128)(2,1)S(1)}, bf16[3,256,384]{2,1,0:T(8,128)(2,1)S(1)}, u32[]{:S(2)}, u32[]{:S(2)}) collective-permute-start(bf16[3,256,384]{2,1,0:T(8,128)(2,1)S(1)} %pad_maximum_fusion.refs_4_.refs_0_), channel_id=1, source_target_pairs={{0,16},{16,0},{1,17},{17,1},{2,18},{18,2},{3,19},{19,3},{4,20},{20... | collective-permute-start | bytes 1769480 | tf_op jit(solution)/shard_map/ppermute | solution.py:31
  36.2 5.6 %collective-permute-start.11 = (bf16[3,256,384]{2,1,0:T(8,128)(2,1)S(1)}, bf16[3,256,384]{2,1,0:T(8,128)(2,1)S(1)}, u32[]{:S(2)}, u32[]{:S(2)}) collective-permute-start(bf16[3,256,384]{2,1,0:T(8,128)(2,1)S(1)} %collective-permute-done.7.refs_5_.refs_1_), channel_id=1, source_target_pairs={{0,16},{16,0},{1,17},{17,1},{2,18},{18,2},{3,19},{19,3},{4,20},{20... | collective-permute-start | bytes 1769480 | tf_op jit(solution)/shard_map/ppermute | solution.py:31
  43.1 2.4 %collective-permute-start.12 = (bf16[3,256,384]{2,1,0:T(8,128)(2,1)S(1)}, bf16[3,256,384]{2,1,0:T(8,128)(2,1)S(1)}, u32[]{:S(2)}, u32[]{:S(2)}) collective-permute-start(bf16[3,256,384]{2,1,0:T(8,128)(2,1)S(1)} %collective-permute-done.9.refs_6_.refs_2_), channel_id=1, source_target_pairs={{0,16},{16,0},{1,17},{17,1},{2,18},{18,2},{3,19},{19,3},{4,20},{20... | collective-permute-start | bytes 1769480 | tf_op jit(solution)/shard_map/ppermute | solution.py:31
  45.5 1.6 %collective-permute-done.12.refs_10_.refs_6_ = bf16[3,256,384]{2,1,0:T(8,128)(2,1)S(1)} collective-permute-done((bf16[3,256,384]{2,1,0:T(8,128)(2,1)S(1)}, bf16[3,256,384]{2,1,0:T(8,128)(2,1)S(1)}, u32[]{:S(2)}, u32[]{:S(2)}) %collective-permute-start.12) | collective-permute-done | bytes 589856 | tf_op jit(solution)/shard_map/ppermute | solution.py:31
  47.2 1.9 %shard_map.102 = (bf16[272,768]{1,0:T(8,128)(2,1)S(1)}, bf16[256,2048]{1,0:T(8,128)(2,1)S(1)}) custom-call(s32[5]{0:T(128)S(1)} %stack.44.ids, bf16[4,128,256]{2,1,0:T(8,128)(2,1)S(1)} %get-tuple-element.48.refs_0_, bf16[4,128,256]{2,1,0:T(8,128)(2,1)S(1)} %collective-permute-done.4.refs_1_, bf16[4,128,256]{2,1,0:T(8,128)(2,1)S(1)} %collective-permute-done.5.refs_2_, ...), custom_call_target="tpu_custom_call" | custom-call | bytes 7249920 | tf_op jit(solution)/shard_map/pallas_call | solution.py:52
  51.4 5.5 %collective-permute-done.16.refs_3_ = bf16[4,128,256]{2,1,0:T(8,128)(2,1)S(1)} collective-permute-done((bf16[4,128,256]{2,1,0:T(8,128)(2,1)S(1)}, bf16[4,128,256]{2,1,0:T(8,128)(2,1)S(1)}, u32[]{:S(2)}, u32[]{:S(2)}) %collective-permute-start.16) | collective-permute-done | bytes 262176 | tf_op jit(solution)/shard_map/ppermute | solution.py:27
  56.9 2.4 %collective-permute-done.15.refs_2_ = bf16[4,128,256]{2,1,0:T(8,128)(2,1)S(1)} collective-permute-done((bf16[4,128,256]{2,1,0:T(8,128)(2,1)S(1)}, bf16[4,128,256]{2,1,0:T(8,128)(2,1)S(1)}, u32[]{:S(2)}, u32[]{:S(2)}) %collective-permute-start.15) | collective-permute-done | bytes 262176 | tf_op jit(solution)/shard_map/ppermute | solution.py:27
  59.3 6.4 %collective-permute-done.14.refs_1_ = bf16[4,128,256]{2,1,0:T(8,128)(2,1)S(1)} collective-permute-done((bf16[4,128,256]{2,1,0:T(8,128)(2,1)S(1)}, bf16[4,128,256]{2,1,0:T(8,128)(2,1)S(1)}, u32[]{:S(2)}, u32[]{:S(2)}) %collective-permute-start.14) | collective-permute-done | bytes 262176 | tf_op jit(solution)/shard_map/ppermute | solution.py:27
  67.0 5.0 %collective-permute-start.21 = (bf16[256,384]{1,0:T(8,128)(2,1)S(1)}, bf16[256,384]{1,0:T(8,128)(2,1)S(1)}, u32[]{:S(2)}, u32[]{:S(2)}) collective-permute-start(bf16[256,384]{1,0:T(8,128)(2,1)S(1)} %get-tuple-element.56.d_mine), channel_id=1, source_target_pairs={{0,128},{128,0},{1,129},{129,1},{2,130},{130,2},{3,131},{131,3},{4... | collective-permute-start | bytes 589832 | tf_op jit(solution)/shard_map/ppermute | solution.py:31
  72.0 1.7 %shard_map.104 = (bf16[256,384]{1,0:T(8,128)(2,1)S(1)}, bf16[4,128,256]{2,1,0:T(8,128)(2,1)S(1)}, bf16[4,128,256]{2,1,0:T(8,128)(2,1)S(1)}, bf16[4,128,256]{2,1,0:T(8,128)(2,1)S(1)}, bf16[4,128,256]{2,1,0:T(8,128)(2,1)S(1)}) custom-call(s32[5]{0:T(128)S(1)} %stack.44.ids, bf16[272,768]{1,0:T(8,128)(2,1)S(1)} %get-tuple-element.57.mine, ...), custom_call_target="tpu_custom_call" | custom-call | flops 536870912 | bytes 6799360 | tf_op jit(solution)/shard_map/pallas_call | solution.py:52
  75.3 4.7 %collective-permute-done.21.d_recv = bf16[256,384]{1,0:T(8,128)(2,1)S(1)} collective-permute-done((bf16[256,384]{1,0:T(8,128)(2,1)S(1)}, bf16[256,384]{1,0:T(8,128)(2,1)S(1)}, u32[]{:S(2)}, u32[]{:S(2)}) %collective-permute-start.21) | collective-permute-done | bytes 196640 | tf_op jit(solution)/shard_map/ppermute | solution.py:31
  81.3 1.9 %shard_map.106 = (bf16[4,144,256]{2,1,0:T(8,128)(2,1)S(1)}, bf16[4,144,256]{2,1,0:T(8,128)(2,1)S(1)}, bf16[4,144,256]{2,1,0:T(8,128)(2,1)S(1)}, bf16[4,144,256]{2,1,0:T(8,128)(2,1)S(1)}) custom-call(s32[5]{0:T(128)S(1)} %stack.44.ids, bf16[256,768]{1,0:T(8,128)(2,1)S(1)} %get-tuple-element.62.acts, bf16[2,16,256]{2,1,0:T(8,128)(2,1)S(1)} %get-tuple-element.63.tail, ...), custom_call_target="tpu_custom_call" | custom-call | flops 1073741824 | bytes 6307840 | tf_op jit(solution)/shard_map/pallas_call | solution.py:52
  83.3 6.0 %collective-permute-done.20.refs_3_ = bf16[4,128,256]{2,1,0:T(8,128)(2,1)S(1)} collective-permute-done((bf16[4,128,256]{2,1,0:T(8,128)(2,1)S(1)}, bf16[4,128,256]{2,1,0:T(8,128)(2,1)S(1)}, u32[]{:S(2)}, u32[]{:S(2)}) %collective-permute-start.20) | collective-permute-done | bytes 262176 | tf_op jit(solution)/shard_map/ppermute | solution.py:27
  89.2 2.4 %shard_map.109 = (bf16[3,4,256,384]{3,2,1,0:T(8,128)(2,1)S(1)}, bf16[3,4,256,384]{3,2,1,0:T(8,128)(2,1)S(1)}) custom-call(s32[5]{0:T(128)S(1)} %stack.44.ids, bf16[256,768]{1,0:T(8,128)(2,1)S(1)} %get-tuple-element.62.acts, bf16[256,384]{1,0:T(8,128)(2,1)S(1)} %get-tuple-element.73.inner, bf16[256,2048]{1,0:T(8,128)(2,1)S(1)} %get-tuple-element.74.tokens, ...), custom_call_target="tpu_custom_call" | custom-call | flops 2147483648 | bytes 7405568 | tf_op jit(solution)/shard_map/pallas_call | solution.py:52
  93.7 2.7 %collective-permute-done.28.recv = bf16[3,4,256,384]{3,2,1,0:T(8,128)(2,1)S(1)} collective-permute-done((bf16[3,4,256,384]{3,2,1,0:T(8,128)(2,1)S(1)}, bf16[3,4,256,384]{3,2,1,0:T(8,128)(2,1)S(1)}, u32[]{:S(2)}, u32[]{:S(2)}) %collective-permute-start.28) | collective-permute-done | bytes 2359328 | tf_op jit(solution)/shard_map/ppermute | solution.py:31
  100.8 2.0 %collective-permute-done.23.refs_6_ = bf16[4,144,256]{2,1,0:T(8,128)(2,1)S(1)} collective-permute-done((bf16[4,144,256]{2,1,0:T(8,128)(2,1)S(1)}, bf16[4,144,256]{2,1,0:T(8,128)(2,1)S(1)}, u32[]{:S(2)}, u32[]{:S(2)}) %collective-permute-start.23) | collective-permute-done | bytes 294944 | tf_op jit(solution)/shard_map/ppermute | solution.py:27
  102.8 7.0 %collective-permute-done.24.refs_7_ = bf16[4,144,256]{2,1,0:T(8,128)(2,1)S(1)} collective-permute-done((bf16[4,144,256]{2,1,0:T(8,128)(2,1)S(1)}, bf16[4,144,256]{2,1,0:T(8,128)(2,1)S(1)}, u32[]{:S(2)}, u32[]{:S(2)}) %collective-permute-start.24) | collective-permute-done | bytes 294944 | tf_op jit(solution)/shard_map/ppermute | solution.py:27
  111.9 1.7 %collective-permute-start.27 = (bf16[272,256]{1,0:T(8,128)(2,1)S(1)}, bf16[272,256]{1,0:T(8,128)(2,1)S(1)}, u32[]{:S(2)}, u32[]{:S(2)}) collective-permute-start(bf16[272,256]{1,0:T(8,128)(2,1)S(1)} %get-tuple-element.70), channel_id=1, source_target_pairs={{8,0},{12,4},{136,8},{140,12},{0,128},{4,132},{128,136},{132,140},... | collective-permute-start | bytes 417800 | tf_op jit(solution)/shard_map/ppermute | solution.py:322
  114.3 3.3 %collective-permute-start.25 = (bf16[272,256]{1,0:T(8,128)(2,1)S(1)}, bf16[272,256]{1,0:T(8,128)(2,1)S(1)}, u32[]{:S(2)}, u32[]{:S(2)}) collective-permute-start(bf16[272,256]{1,0:T(8,128)(2,1)S(1)} %get-tuple-element.68), channel_id=1, source_target_pairs={{0,0},{4,4},{128,8},{132,12},{8,128},{12,132},{136,136},{140,140},... | collective-permute-start | bytes 417800 | tf_op jit(solution)/shard_map/ppermute | solution.py:322
  117.6 2.9 %collective-permute-start.26 = (bf16[272,256]{1,0:T(8,128)(2,1)S(1)}, bf16[272,256]{1,0:T(8,128)(2,1)S(1)}, u32[]{:S(2)}, u32[]{:S(2)}) collective-permute-start(bf16[272,256]{1,0:T(8,128)(2,1)S(1)} %get-tuple-element.69), channel_id=1, source_target_pairs={{4,0},{0,4},{132,8},{128,12},{12,128},{8,132},{140,136},{136,140},... | collective-permute-start | bytes 417800 | tf_op jit(solution)/shard_map/ppermute | solution.py:322
  120.6 6.1 %collective-permute-done.32.p2 = bf16[3,256,384]{2,1,0:T(8,128)(2,1)S(1)} collective-permute-done((bf16[3,256,384]{2,1,0:T(8,128)(2,1)S(1)}, bf16[3,256,384]{2,1,0:T(8,128)(2,1)S(1)}, u32[]{:S(2)}, u32[]{:S(2)}) %collective-permute-start.32) | collective-permute-done | bytes 589856 | tf_op jit(solution)/shard_map/ppermute | solution.py:27
  126.6 1.8 %shard_map.111 = (f32[256,384]{1,0:T(8,128)}, f32[256,384]{1,0:T(8,128)}, f32[384,256]{1,0:T(8,128)}) custom-call(s32[5]{0:T(128)S(1)} %stack.44.ids, bf16[3,256,384]{2,1,0:T(8,128)(2,1)S(1)} %get-tuple-element.82.p0, bf16[3,256,384]{2,1,0:T(8,128)(2,1)S(1)} %collective-permute-done.29.p1, bf16[3,256,384]{2,1,0:T(8,128)(2,1)S(1)} %collective-permute-done.32.p2, ...), custom_call_target="tpu_custom_call" | custom-call | bytes 2949120 | tf_op jit(solution)/shard_map/pallas_call | solution.py:52
  128.4 8.4 %collective-permute-done.26.p1 = bf16[272,256]{1,0:T(8,128)(2,1)S(1)} collective-permute-done((bf16[272,256]{1,0:T(8,128)(2,1)S(1)}, bf16[272,256]{1,0:T(8,128)(2,1)S(1)}, u32[]{:S(2)}, u32[]{:S(2)}) %collective-permute-start.26) | collective-permute-done | bytes 139296 | tf_op jit(solution)/shard_map/ppermute | solution.py:322
  (56 shorter events, 24.7 us)
Async XLA Ops:
  2.8 22.0 %collective-permute-start.8 = (bf16[3,256,384]{2,1,0:T(8,128)(2,1)S(1)}, bf16[3,256,384]{2,1,0:T(8,128)(2,1)S(1)}, u32[]{:S(2)}, u32[]{:S(2)}) collective-permute-start(bf16[3,256,384]{2,1,0:T(8,128)(2,1)S(1)} %pad_maximum_fusion.refs_4_.refs_0_), channel_id=1, source_target_pairs={{0,96},{32,0},{64,32},{96,64},{1,97},{33,1},{65,33},{97,65},{2,98}... | collective-permute-start | bytes 1769480 | tf_op jit(solution)/shard_map/ppermute | solution.py:27
  5.7 19.1 %collective-permute-start.7 = (bf16[3,256,384]{2,1,0:T(8,128)(2,1)S(1)}, bf16[3,256,384]{2,1,0:T(8,128)(2,1)S(1)}, u32[]{:S(2)}, u32[]{:S(2)}) collective-permute-start(bf16[3,256,384]{2,1,0:T(8,128)(2,1)S(1)} %pad_maximum_fusion.refs_4_.refs_0_), channel_id=1, source_target_pairs={{0,32},{32,64},{64,96},{96,0},{1,33},{33,65},{65,97},{97,1},{2,34}... | collective-permute-start | bytes 1769480 | tf_op jit(solution)/shard_map/ppermute | solution.py:27
  6.6 9.2 %collective-permute-start.3 = (bf16[2,128,256]{2,1,0:T(8,128)(2,1)S(1)}, bf16[2,128,256]{2,1,0:T(8,128)(2,1)S(1)}, u32[]{:S(2)}, u32[]{:S(2)}) collective-permute-start(bf16[2,128,256]{2,1,0:T(8,128)(2,1)S(1)} %pad_maximum_fusion.1), channel_id=1, source_target_pairs={{0,4},{4,0},{8,132},{12,128},{128,12},{132,8},{136,140},{140,136},... | collective-permute-start | bytes 393224 | tf_op jit(solution)/shard_map/ppermute | solution.py:240
  9.5 9.3 %collective-permute-start.2 = (bf16[2,128,256]{2,1,0:T(8,128)(2,1)S(1)}, bf16[2,128,256]{2,1,0:T(8,128)(2,1)S(1)}, u32[]{:S(2)}, u32[]{:S(2)}) collective-permute-start(bf16[2,128,256]{2,1,0:T(8,128)(2,1)S(1)} %pad_maximum_fusion.1), channel_id=1, source_target_pairs={{0,12},{4,8},{8,140},{12,136},{128,4},{132,0},{136,132},{140,128},... | collective-permute-start | bytes 393224 | tf_op jit(solution)/shard_map/ppermute | solution.py:240
  11.1 13.1 %collective-permute-start.1 = (bf16[2,128,256]{2,1,0:T(8,128)(2,1)S(1)}, bf16[2,128,256]{2,1,0:T(8,128)(2,1)S(1)}, u32[]{:S(2)}, u32[]{:S(2)}) collective-permute-start(bf16[2,128,256]{2,1,0:T(8,128)(2,1)S(1)} %pad_maximum_fusion.1), channel_id=1, source_target_pairs={{0,8},{4,12},{8,136},{12,140},{128,0},{132,4},{136,128},{140,132},... | collective-permute-start | bytes 393224 | tf_op jit(solution)/shard_map/ppermute | solution.py:240
  15.8 9.0 %collective-permute-start = (bf16[2,128,256]{2,1,0:T(8,128)(2,1)S(1)}, bf16[2,128,256]{2,1,0:T(8,128)(2,1)S(1)}, u32[]{:S(2)}, u32[]{:S(2)}) collective-permute-start(bf16[2,128,256]{2,1,0:T(8,128)(2,1)S(1)} %pad_maximum_fusion.1), channel_id=1, source_target_pairs={{0,0},{4,4},{8,128},{12,132},{128,8},{132,12},{136,136},{140,140},... | collective-permute-start | bytes 393224 | tf_op jit(solution)/shard_map/ppermute | solution.py:240
  24.8 18.3 %collective-permute-start.9 = (bf16[3,256,384]{2,1,0:T(8,128)(2,1)S(1)}, bf16[3,256,384]{2,1,0:T(8,128)(2,1)S(1)}, u32[]{:S(2)}, u32[]{:S(2)}) collective-permute-start(bf16[3,256,384]{2,1,0:T(8,128)(2,1)S(1)} %pad_maximum_fusion.refs_4_.refs_0_), channel_id=1, source_target_pairs={{0,64},{32,96},{64,0},{96,32},{1,65},{33,97},{65,1},{97,33},{2,66}... | collective-permute-start | bytes 1769480 | tf_op jit(solution)/shard_map/ppermute | solution.py:27
  27.1 9.1 %collective-permute-start.6 = (bf16[4,128,256]{2,1,0:T(8,128)(2,1)S(1)}, bf16[4,128,256]{2,1,0:T(8,128)(2,1)S(1)}, u32[]{:S(2)}, u32[]{:S(2)}) collective-permute-start(bf16[4,128,256]{2,1,0:T(8,128)(2,1)S(1)} %get-tuple-element.48.refs_0_), channel_id=1, source_target_pairs={{0,3},{1,0},{2,1},{3,2},{4,7},{5,4},{6,5},{7,6},{8,11},{9,8},{10,9... | collective-permute-start | bytes 786440 | tf_op jit(solution)/shard_map/ppermute | solution.py:27
  29.7 12.2 %collective-permute-start.5 = (bf16[4,128,256]{2,1,0:T(8,128)(2,1)S(1)}, bf16[4,128,256]{2,1,0:T(8,128)(2,1)S(1)}, u32[]{:S(2)}, u32[]{:S(2)}) collective-permute-start(bf16[4,128,256]{2,1,0:T(8,128)(2,1)S(1)} %get-tuple-element.48.refs_0_), channel_id=1, source_target_pairs={{0,2},{1,3},{2,0},{3,1},{4,6},{5,7},{6,4},{7,5},{8,10},{9,11},{10,... | collective-permute-start | bytes 786440 | tf_op jit(solution)/shard_map/ppermute | solution.py:27
  30.2 12.9 %collective-permute-start.4 = (bf16[4,128,256]{2,1,0:T(8,128)(2,1)S(1)}, bf16[4,128,256]{2,1,0:T(8,128)(2,1)S(1)}, u32[]{:S(2)}, u32[]{:S(2)}) collective-permute-start(bf16[4,128,256]{2,1,0:T(8,128)(2,1)S(1)} %get-tuple-element.48.refs_0_), channel_id=1, source_target_pairs={{0,1},{1,2},{2,3},{3,0},{4,5},{5,6},{6,7},{7,4},{8,9},{9,10},{10,1... | collective-permute-start | bytes 786440 | tf_op jit(solution)/shard_map/ppermute | solution.py:27
  30.8 14.7 %collective-permute-start.10 = (bf16[3,256,384]{2,1,0:T(8,128)(2,1)S(1)}, bf16[3,256,384]{2,1,0:T(8,128)(2,1)S(1)}, u32[]{:S(2)}, u32[]{:S(2)}) collective-permute-start(bf16[3,256,384]{2,1,0:T(8,128)(2,1)S(1)} %pad_maximum_fusion.refs_4_.refs_0_), channel_id=1, source_target_pairs={{0,16},{16,0},{1,17},{17,1},{2,18},{18,2},{3,19},{19,3},{4,20},{20... | collective-permute-start | bytes 1769480 | tf_op jit(solution)/shard_map/ppermute | solution.py:31
  36.2 9.3 %collective-permute-start.11 = (bf16[3,256,384]{2,1,0:T(8,128)(2,1)S(1)}, bf16[3,256,384]{2,1,0:T(8,128)(2,1)S(1)}, u32[]{:S(2)}, u32[]{:S(2)}) collective-permute-start(bf16[3,256,384]{2,1,0:T(8,128)(2,1)S(1)} %collective-permute-done.7.refs_5_.refs_1_), channel_id=1, source_target_pairs={{0,16},{16,0},{1,17},{17,1},{2,18},{18,2},{3,19},{19,3},{4,20},{20... | collective-permute-start | bytes 1769480 | tf_op jit(solution)/shard_map/ppermute | solution.py:31
  43.1 4.1 %collective-permute-start.12 = (bf16[3,256,384]{2,1,0:T(8,128)(2,1)S(1)}, bf16[3,256,384]{2,1,0:T(8,128)(2,1)S(1)}, u32[]{:S(2)}, u32[]{:S(2)}) collective-permute-start(bf16[3,256,384]{2,1,0:T(8,128)(2,1)S(1)} %collective-permute-done.9.refs_6_.refs_2_), channel_id=1, source_target_pairs={{0,16},{16,0},{1,17},{17,1},{2,18},{18,2},{3,19},{19,3},{4,20},{20... | collective-permute-start | bytes 1769480 | tf_op jit(solution)/shard_map/ppermute | solution.py:31
  49.1 23.0 %collective-permute-start.17 = (bf16[272,768]{1,0:T(8,128)(2,1)S(1)}, bf16[272,768]{1,0:T(8,128)(2,1)S(1)}, u32[]{:S(2)}, u32[]{:S(2)}) collective-permute-start(bf16[272,768]{1,0:T(8,128)(2,1)S(1)} %get-tuple-element.57.mine), channel_id=1, source_target_pairs={{0,128},{128,0},{1,129},{129,1},{2,130},{130,2},{3,131},{131,3},{4... | collective-permute-start | bytes 1253384 | tf_op jit(solution)/shard_map/ppermute | solution.py:31
  49.7 7.2 %collective-permute-start.16 = (bf16[4,128,256]{2,1,0:T(8,128)(2,1)S(1)}, bf16[4,128,256]{2,1,0:T(8,128)(2,1)S(1)}, u32[]{:S(2)}, u32[]{:S(2)}) collective-permute-start(bf16[4,128,256]{2,1,0:T(8,128)(2,1)S(1)} %get-tuple-element.55.refs_0_), channel_id=1, source_target_pairs={{0,3},{1,0},{2,1},{3,2},{4,7},{5,4},{6,5},{7,6},{8,11},{9,8},{10,9... | collective-permute-start | bytes 786440 | tf_op jit(solution)/shard_map/ppermute | solution.py:27
  50.8 8.5 %collective-permute-start.15 = (bf16[4,128,256]{2,1,0:T(8,128)(2,1)S(1)}, bf16[4,128,256]{2,1,0:T(8,128)(2,1)S(1)}, u32[]{:S(2)}, u32[]{:S(2)}) collective-permute-start(bf16[4,128,256]{2,1,0:T(8,128)(2,1)S(1)} %get-tuple-element.55.refs_0_), channel_id=1, source_target_pairs={{0,2},{1,3},{2,0},{3,1},{4,6},{5,7},{6,4},{7,5},{8,10},{9,11},{10,... | collective-permute-start | bytes 786440 | tf_op jit(solution)/shard_map/ppermute | solution.py:27
  50.8 14.9 %collective-permute-start.14 = (bf16[4,128,256]{2,1,0:T(8,128)(2,1)S(1)}, bf16[4,128,256]{2,1,0:T(8,128)(2,1)S(1)}, u32[]{:S(2)}, u32[]{:S(2)}) collective-permute-start(bf16[4,128,256]{2,1,0:T(8,128)(2,1)S(1)} %get-tuple-element.55.refs_0_), channel_id=1, source_target_pairs={{0,1},{1,2},{2,3},{3,0},{4,5},{5,6},{6,7},{7,4},{8,9},{9,10},{10,1... | collective-permute-start | bytes 786440 | tf_op jit(solution)/shard_map/ppermute | solution.py:27
  67.0 13.0 %collective-permute-start.21 = (bf16[256,384]{1,0:T(8,128)(2,1)S(1)}, bf16[256,384]{1,0:T(8,128)(2,1)S(1)}, u32[]{:S(2)}, u32[]{:S(2)}) collective-permute-start(bf16[256,384]{1,0:T(8,128)(2,1)S(1)} %get-tuple-element.56.d_mine), channel_id=1, source_target_pairs={{0,128},{128,0},{1,129},{129,1},{2,130},{130,2},{3,131},{131,3},{4... | collective-permute-start | bytes 589832 | tf_op jit(solution)/shard_map/ppermute | solution.py:31
  73.7 9.5 %collective-permute-start.18 = (bf16[4,128,256]{2,1,0:T(8,128)(2,1)S(1)}, bf16[4,128,256]{2,1,0:T(8,128)(2,1)S(1)}, u32[]{:S(2)}, u32[]{:S(2)}) collective-permute-start(bf16[4,128,256]{2,1,0:T(8,128)(2,1)S(1)} %get-tuple-element.59), channel_id=1, source_target_pairs={{0,3},{1,0},{2,1},{3,2},{4,7},{5,4},{6,5},{7,6},{8,11},{9,8},{10,9... | collective-permute-start | bytes 786440 | tf_op jit(solution)/shard_map/ppermute | solution.py:27
  73.8 9.4 %collective-permute-start.19 = (bf16[4,128,256]{2,1,0:T(8,128)(2,1)S(1)}, bf16[4,128,256]{2,1,0:T(8,128)(2,1)S(1)}, u32[]{:S(2)}, u32[]{:S(2)}) collective-permute-start(bf16[4,128,256]{2,1,0:T(8,128)(2,1)S(1)} %get-tuple-element.60), channel_id=1, source_target_pairs={{0,2},{1,3},{2,0},{3,1},{4,6},{5,7},{6,4},{7,5},{8,10},{9,11},{10,... | collective-permute-start | bytes 786440 | tf_op jit(solution)/shard_map/ppermute | solution.py:27
  74.5 14.7 %collective-permute-start.20 = (bf16[4,128,256]{2,1,0:T(8,128)(2,1)S(1)}, bf16[4,128,256]{2,1,0:T(8,128)(2,1)S(1)}, u32[]{:S(2)}, u32[]{:S(2)}) collective-permute-start(bf16[4,128,256]{2,1,0:T(8,128)(2,1)S(1)} %get-tuple-element.61), channel_id=1, source_target_pairs={{0,1},{1,2},{2,3},{3,0},{4,5},{5,6},{6,7},{7,4},{8,9},{9,10},{10,1... | collective-permute-start | bytes 786440 | tf_op jit(solution)/shard_map/ppermute | solution.py:27
  91.6 4.7 %collective-permute-start.28 = (bf16[3,4,256,384]{3,2,1,0:T(8,128)(2,1)S(1)}, bf16[3,4,256,384]{3,2,1,0:T(8,128)(2,1)S(1)}, u32[]{:S(2)}, u32[]{:S(2)}) collective-permute-start(bf16[3,4,256,384]{3,2,1,0:T(8,128)(2,1)S(1)} %get-tuple-element.77), channel_id=1, source_target_pairs={{0,16},{16,0},{1,17},{17,1},{2,18},{18,2},{3,19},{19,3},{4,20},{20... | collective-permute-start | bytes 7077896 | tf_op jit(solution)/shard_map/ppermute | solution.py:31
  92.2 8.6 %collective-permute-start.22 = (bf16[4,144,256]{2,1,0:T(8,128)(2,1)S(1)}, bf16[4,144,256]{2,1,0:T(8,128)(2,1)S(1)}, u32[]{:S(2)}, u32[]{:S(2)}) collective-permute-start(bf16[4,144,256]{2,1,0:T(8,128)(2,1)S(1)} %get-tuple-element.65), channel_id=1, source_target_pairs={{0,3},{1,0},{2,1},{3,2},{4,7},{5,4},{6,5},{7,6},{8,11},{9,8},{10,9... | collective-permute-start | bytes 884744 | tf_op jit(solution)/shard_map/ppermute | solution.py:27
  93.0 9.8 %collective-permute-start.23 = (bf16[4,144,256]{2,1,0:T(8,128)(2,1)S(1)}, bf16[4,144,256]{2,1,0:T(8,128)(2,1)S(1)}, u32[]{:S(2)}, u32[]{:S(2)}) collective-permute-start(bf16[4,144,256]{2,1,0:T(8,128)(2,1)S(1)} %get-tuple-element.66), channel_id=1, source_target_pairs={{0,2},{1,3},{2,0},{3,1},{4,6},{5,7},{6,4},{7,5},{8,10},{9,11},{10,... | collective-permute-start | bytes 884744 | tf_op jit(solution)/shard_map/ppermute | solution.py:27
  93.2 16.6 %collective-permute-start.24 = (bf16[4,144,256]{2,1,0:T(8,128)(2,1)S(1)}, bf16[4,144,256]{2,1,0:T(8,128)(2,1)S(1)}, u32[]{:S(2)}, u32[]{:S(2)}) collective-permute-start(bf16[4,144,256]{2,1,0:T(8,128)(2,1)S(1)} %get-tuple-element.67), channel_id=1, source_target_pairs={{0,1},{1,2},{2,3},{3,0},{4,5},{5,6},{6,7},{7,4},{8,9},{9,10},{10,1... | collective-permute-start | bytes 884744 | tf_op jit(solution)/shard_map/ppermute | solution.py:27
  97.5 20.2 %collective-permute-start.29 = (bf16[3,256,384]{2,1,0:T(8,128)(2,1)S(1)}, bf16[3,256,384]{2,1,0:T(8,128)(2,1)S(1)}, u32[]{:S(2)}, u32[]{:S(2)}) collective-permute-start(bf16[3,256,384]{2,1,0:T(8,128)(2,1)S(1)} %get-tuple-element.78), channel_id=1, source_target_pairs={{0,96},{32,0},{64,32},{96,64},{1,97},{33,1},{65,33},{97,65},{2,98}... | collective-permute-start | bytes 1769480 | tf_op jit(solution)/shard_map/ppermute | solution.py:27
  98.6 22.0 %collective-permute-start.30 = (bf16[3,256,384]{2,1,0:T(8,128)(2,1)S(1)}, bf16[3,256,384]{2,1,0:T(8,128)(2,1)S(1)}, u32[]{:S(2)}, u32[]{:S(2)}) collective-permute-start(bf16[3,256,384]{2,1,0:T(8,128)(2,1)S(1)} %get-tuple-element.79), channel_id=1, source_target_pairs={{0,32},{32,64},{64,96},{96,0},{1,33},{33,65},{65,97},{97,1},{2,34}... | collective-permute-start | bytes 1769480 | tf_op jit(solution)/shard_map/ppermute | solution.py:27
  110.5 16.1 %collective-permute-start.32 = (bf16[3,256,384]{2,1,0:T(8,128)(2,1)S(1)}, bf16[3,256,384]{2,1,0:T(8,128)(2,1)S(1)}, u32[]{:S(2)}, u32[]{:S(2)}) collective-permute-start(bf16[3,256,384]{2,1,0:T(8,128)(2,1)S(1)} %get-tuple-element.84), channel_id=1, source_target_pairs={{0,64},{32,96},{64,0},{96,32},{1,65},{33,97},{65,1},{97,33},{2,66}... | collective-permute-start | bytes 1769480 | tf_op jit(solution)/shard_map/ppermute | solution.py:27
  111.9 24.9 %collective-permute-start.27 = (bf16[272,256]{1,0:T(8,128)(2,1)S(1)}, bf16[272,256]{1,0:T(8,128)(2,1)S(1)}, u32[]{:S(2)}, u32[]{:S(2)}) collective-permute-start(bf16[272,256]{1,0:T(8,128)(2,1)S(1)} %get-tuple-element.70), channel_id=1, source_target_pairs={{8,0},{12,4},{136,8},{140,12},{0,128},{4,132},{128,136},{132,140},... | collective-permute-start | bytes 417800 | tf_op jit(solution)/shard_map/ppermute | solution.py:322
  114.3 14.1 %collective-permute-start.25 = (bf16[272,256]{1,0:T(8,128)(2,1)S(1)}, bf16[272,256]{1,0:T(8,128)(2,1)S(1)}, u32[]{:S(2)}, u32[]{:S(2)}) collective-permute-start(bf16[272,256]{1,0:T(8,128)(2,1)S(1)} %get-tuple-element.68), channel_id=1, source_target_pairs={{0,0},{4,4},{128,8},{132,12},{8,128},{12,132},{136,136},{140,140},... | collective-permute-start | bytes 417800 | tf_op jit(solution)/shard_map/ppermute | solution.py:322
  117.6 19.1 %collective-permute-start.26 = (bf16[272,256]{1,0:T(8,128)(2,1)S(1)}, bf16[272,256]{1,0:T(8,128)(2,1)S(1)}, u32[]{:S(2)}, u32[]{:S(2)}) collective-permute-start(bf16[272,256]{1,0:T(8,128)(2,1)S(1)} %get-tuple-element.69), channel_id=1, source_target_pairs={{4,0},{0,4},{132,8},{128,12},{12,128},{8,132},{140,136},{136,140},... | collective-permute-start | bytes 417800 | tf_op jit(solution)/shard_map/ppermute | solution.py:322
  120.5 16.2 %collective-permute-start.31 = (bf16[272,256]{1,0:T(8,128)(2,1)S(1)}, bf16[272,256]{1,0:T(8,128)(2,1)S(1)}, u32[]{:S(2)}, u32[]{:S(2)}) collective-permute-start(bf16[272,256]{1,0:T(8,128)(2,1)S(1)} %get-tuple-element.80), channel_id=1, source_target_pairs={{12,0},{8,4},{140,8},{136,12},{4,128},{0,132},{132,136},{128,140},... | collective-permute-start | bytes 417800 | tf_op jit(solution)/shard_map/ppermute | solution.py:322
  (4 other events, 102.8 us)

commit v5 on v4

--- a/solution.py
+++ b/solution.py
@@ -73,8 +73,8 @@
 
 def forward_products_kernel(ids, *refs):
     pieces, weights, (gain, send, mixed, x_all, acc) = refs[:4], refs[4:12], refs[12:]
-    for s in range(4):
-        x_all[s] = pieces[s][...]
+    for j, s in enumerate((0, 1, 3, 2)):
+        x_all[s] = pieces[j][...]
     total = [jnp.zeros((128, 1), F32) for _ in range(2)]
     for i in range(8):
         q, s, k2 = block_place(ids, i)
@@ -98,8 +98,8 @@
 
 def backward_products_kernel(ids, *refs):
     pieces, weights, (send, mixed, x_all, acc) = refs[:4], refs[4:12], refs[12:]
-    for s in range(4):
-        x_all[s] = pieces[s][...]
+    for j, s in enumerate((0, 1, 3, 2)):
+        x_all[s] = pieces[j][...]
     for i in range(8):
         _, s, k2 = block_place(ids, i)
         at = slice(256 * i, 256 * i + 256)
@@ -205,7 +205,7 @@
 
 
 def scatter_x(parts):
-    return [parts[0]] + [shift(parts[s], "x", -s) for s in (1, 2, 3)]
+    return [parts[0]] + [shift(parts[s], "x", -s) for s in (2, 1, 3)]
 
 
 def finish_kernel(ids, p0, p1, p2, p3, tokens, cot, gain, scale, mixed_out, d_tokens):
@@ -241,7 +241,7 @@
     tok_z, cot_z = call(stack_kernel, ids, [by_z[k] for k in (0, 2, 3, 1)], [VMEM] * 4, [((4, 128, 256), BF16)] * 2)
     y1, y3, *_ = lax.optimization_barrier((shift(own, "y", 1), shift(own, "y", 3), *[by_z[k] for k in (0, 2, 3, 1)]))
     y2 = shift(after(own, y1, y3), "y", 2)
-    tok_x = [shift(tok_z, "x", s) for s in (1, 2, 3)]
+    tok_x = [shift(tok_z, "x", s) for s in (1, 3, 2)]
     y2 = after(y2, *tok_x)
     cot_z = after(cot_z, *tok_x)
     tok_x = [tok_z] + tok_x
@@ -257,7 +257,7 @@
         [((272, 768), BF16), ((256, 2048), BF16)],
         [x_all, pltpu.VMEM((256, 768), F32)],
     )
-    cot_x = [cot_z] + [shift(cot_z, "x", s) for s in (1, 2, 3)]
+    cot_x = [cot_z] + [shift(cot_z, "x", s) for s in (1, 3, 2)]
     d_send, cot_all = call(
         backward_products_kernel,
         ids,

time: 139 us -> 138 us (level)
  the two profiles are of different devices: /device:TPU:97 before, /device:TPU:6 now
where the time goes in v5:
time: 138 us
  waiting for transfers between devices  65.1 us (47%)
  starting transfers between devices  51.8 us (38%)
  Pallas kernels  16.7 us (12%)
  other arithmetic  1.99 us (1%)
    ppermute x18, waiting for transfers between devices, shift(): return lax.ppermute(array, axis, [(i, (i + by) % 4) for i in range(4)])  38 us
    ppermute x18, starting transfers between devices, shift(): return lax.ppermute(array, axis, [(i, (i + by) % 4) for i in range(4)])  28.1 us
    pallas_call x12, Pallas kernels, call(): pl.pallas_call(body, out_shape=[jax.ShapeDtypeStruct(s, d) for s, d in ou...  16.7 us
    ppermute x4, waiting for transfers between devices, on_device(): by_z = [lax.ppermute(pair, ('zh', 'zl'), z_pairs(k)) for k in range(4)]  14.2 us
    ppermute x7, waiting for transfers between devices, swap(): return lax.ppermute(array, axis, [(0, 1), (1, 0)])  10.1 us
    ppermute x4, starting transfers between devices, on_device(): by_z = [lax.ppermute(pair, ('zh', 'zl'), z_pairs(k)) for k in range(4)]  9.97 us
    ppermute x4, starting transfers between devices, on_device(): lax.ppermute(blocks[k], ('zh', 'zl'), [(t, s) for s, t in z_pairs(k)])  7 us
    ppermute x7, starting transfers between devices, swap(): return lax.ppermute(array, axis, [(0, 1), (1, 0)])  6.72 us
  transfers between devices with their start and end apart: 33, of which 15 were waited for; matrix products, arithmetic and copies ran while one was open for 1% of the time, Pallas kernels for 8%

profile of v5, /device:TPU:6, one launch (start us, length us, event | category | flops | bytes accessed | tf_op | source)
XLA Modules:
  0.0 137.7 jit_solution(15651460239060641774)
XLA Ops:
  2.8 3.1 %collective-permute-start.8 = (bf16[3,256,384]{2,1,0:T(8,128)(2,1)S(1)}, bf16[3,256,384]{2,1,0:T(8,128)(2,1)S(1)}, u32[]{:S(2)}, u32[]{:S(2)}) collective-permute-start(bf16[3,256,384]{2,1,0:T(8,128)(2,1)S(1)} %pad_maximum_fusion.refs_4_.refs_0_), channel_id=1, source_target_pairs={{0,96},{32,0},{64,32},{96,64},{1,97},{33,1},{65,33},{97,65},{2,98}... | collective-permute-start | bytes 1769480 | tf_op jit(solution)/shard_map/ppermute | solution.py:27
  6.8 2.0 %collective-permute-start.3 = (bf16[2,128,256]{2,1,0:T(8,128)(2,1)S(1)}, bf16[2,128,256]{2,1,0:T(8,128)(2,1)S(1)}, u32[]{:S(2)}, u32[]{:S(2)}) collective-permute-start(bf16[2,128,256]{2,1,0:T(8,128)(2,1)S(1)} %pad_maximum_fusion.1), channel_id=1, source_target_pairs={{0,4},{4,0},{8,132},{12,128},{128,12},{132,8},{136,140},{140,136},... | collective-permute-start | bytes 393224 | tf_op jit(solution)/shard_map/ppermute | solution.py:240
  8.8 5.8 %collective-permute-start.2 = (bf16[2,128,256]{2,1,0:T(8,128)(2,1)S(1)}, bf16[2,128,256]{2,1,0:T(8,128)(2,1)S(1)}, u32[]{:S(2)}, u32[]{:S(2)}) collective-permute-start(bf16[2,128,256]{2,1,0:T(8,128)(2,1)S(1)} %pad_maximum_fusion.1), channel_id=1, source_target_pairs={{0,12},{4,8},{8,140},{12,136},{128,4},{132,0},{136,132},{140,128},... | collective-permute-start | bytes 393224 | tf_op jit(solution)/shard_map/ppermute | solution.py:240
  16.8 1.5 %collective-permute-done.2.p3 = bf16[2,128,256]{2,1,0:T(8,128)(2,1)S(1)} collective-permute-done((bf16[2,128,256]{2,1,0:T(8,128)(2,1)S(1)}, bf16[2,128,256]{2,1,0:T(8,128)(2,1)S(1)}, u32[]{:S(2)}, u32[]{:S(2)}) %collective-permute-start.2) | collective-permute-done | bytes 131104 | tf_op jit(solution)/shard_map/ppermute | solution.py:240
  18.3 12.7 %collective-permute-done.1.p2 = bf16[2,128,256]{2,1,0:T(8,128)(2,1)S(1)} collective-permute-done((bf16[2,128,256]{2,1,0:T(8,128)(2,1)S(1)}, bf16[2,128,256]{2,1,0:T(8,128)(2,1)S(1)}, u32[]{:S(2)}, u32[]{:S(2)}) %collective-permute-start.1) | collective-permute-done | bytes 131104 | tf_op jit(solution)/shard_map/ppermute | solution.py:240
  31.1 2.0 %collective-permute-start.9 = (bf16[3,256,384]{2,1,0:T(8,128)(2,1)S(1)}, bf16[3,256,384]{2,1,0:T(8,128)(2,1)S(1)}, u32[]{:S(2)}, u32[]{:S(2)}) collective-permute-start(bf16[3,256,384]{2,1,0:T(8,128)(2,1)S(1)} %pad_maximum_fusion.refs_4_.refs_0_), channel_id=1, source_target_pairs={{0,64},{32,96},{64,0},{96,32},{1,65},{33,97},{65,1},{97,33},{2,66}... | collective-permute-start | bytes 1769480 | tf_op jit(solution)/shard_map/ppermute | solution.py:27
  33.7 1.5 %collective-permute-start.6 = (bf16[4,128,256]{2,1,0:T(8,128)(2,1)S(1)}, bf16[4,128,256]{2,1,0:T(8,128)(2,1)S(1)}, u32[]{:S(2)}, u32[]{:S(2)}) collective-permute-start(bf16[4,128,256]{2,1,0:T(8,128)(2,1)S(1)} %get-tuple-element.48.refs_0_), channel_id=1, source_target_pairs={{0,2},{1,3},{2,0},{3,1},{4,6},{5,7},{6,4},{7,5},{8,10},{9,11},{10,... | collective-permute-start | bytes 786440 | tf_op jit(solution)/shard_map/ppermute | solution.py:27
  35.2 3.2 %collective-permute-start.4 = (bf16[4,128,256]{2,1,0:T(8,128)(2,1)S(1)}, bf16[4,128,256]{2,1,0:T(8,128)(2,1)S(1)}, u32[]{:S(2)}, u32[]{:S(2)}) collective-permute-start(bf16[4,128,256]{2,1,0:T(8,128)(2,1)S(1)} %get-tuple-element.48.refs_0_), channel_id=1, source_target_pairs={{0,1},{1,2},{2,3},{3,0},{4,5},{5,6},{6,7},{7,4},{8,9},{9,10},{10,1... | collective-permute-start | bytes 786440 | tf_op jit(solution)/shard_map/ppermute | solution.py:27
  38.5 3.6 %collective-permute-done.6.refs_3_ = bf16[4,128,256]{2,1,0:T(8,128)(2,1)S(1)} collective-permute-done((bf16[4,128,256]{2,1,0:T(8,128)(2,1)S(1)}, bf16[4,128,256]{2,1,0:T(8,128)(2,1)S(1)}, u32[]{:S(2)}, u32[]{:S(2)}) %collective-permute-start.6) | collective-permute-done | bytes 262176 | tf_op jit(solution)/shard_map/ppermute | solution.py:27
  42.1 2.7 %collective-permute-done.5.refs_2_ = bf16[4,128,256]{2,1,0:T(8,128)(2,1)S(1)} collective-permute-done((bf16[4,128,256]{2,1,0:T(8,128)(2,1)S(1)}, bf16[4,128,256]{2,1,0:T(8,128)(2,1)S(1)}, u32[]{:S(2)}, u32[]{:S(2)}) %collective-permute-start.5) | collective-permute-done | bytes 262176 | tf_op jit(solution)/shard_map/ppermute | solution.py:27
  47.7 1.9 %shard_map.102 = (bf16[272,768]{1,0:T(8,128)(2,1)S(1)}, bf16[256,2048]{1,0:T(8,128)(2,1)S(1)}) custom-call(s32[5]{0:T(128)S(1)} %stack.44.ids, bf16[4,128,256]{2,1,0:T(8,128)(2,1)S(1)} %get-tuple-element.48.refs_0_, bf16[4,128,256]{2,1,0:T(8,128)(2,1)S(1)} %collective-permute-done.4.refs_1_, bf16[4,128,256]{2,1,0:T(8,128)(2,1)S(1)} %collective-permute-done.5.refs_2_, ...), custom_call_target="tpu_custom_call" | custom-call | bytes 7249920 | tf_op jit(solution)/shard_map/pallas_call | solution.py:52
  49.6 5.5 %collective-permute-start.17 = (bf16[272,768]{1,0:T(8,128)(2,1)S(1)}, bf16[272,768]{1,0:T(8,128)(2,1)S(1)}, u32[]{:S(2)}, u32[]{:S(2)}) collective-permute-start(bf16[272,768]{1,0:T(8,128)(2,1)S(1)} %get-tuple-element.57.mine), channel_id=1, source_target_pairs={{0,128},{128,0},{1,129},{129,1},{2,130},{130,2},{3,131},{131,3},{4... | collective-permute-start | bytes 1253384 | tf_op jit(solution)/shard_map/ppermute | solution.py:31
  56.6 3.1 %collective-permute-start.14 = (bf16[4,128,256]{2,1,0:T(8,128)(2,1)S(1)}, bf16[4,128,256]{2,1,0:T(8,128)(2,1)S(1)}, u32[]{:S(2)}, u32[]{:S(2)}) collective-permute-start(bf16[4,128,256]{2,1,0:T(8,128)(2,1)S(1)} %get-tuple-element.55.refs_0_), channel_id=1, source_target_pairs={{0,1},{1,2},{2,3},{3,0},{4,5},{5,6},{6,7},{7,4},{8,9},{9,10},{10,1... | collective-permute-start | bytes 786440 | tf_op jit(solution)/shard_map/ppermute | solution.py:27
  59.7 6.1 %collective-permute-done.16.refs_3_ = bf16[4,128,256]{2,1,0:T(8,128)(2,1)S(1)} collective-permute-done((bf16[4,128,256]{2,1,0:T(8,128)(2,1)S(1)}, bf16[4,128,256]{2,1,0:T(8,128)(2,1)S(1)}, u32[]{:S(2)}, u32[]{:S(2)}) %collective-permute-start.16) | collective-permute-done | bytes 262176 | tf_op jit(solution)/shard_map/ppermute | solution.py:27
  65.8 4.4 %collective-permute-done.15.refs_2_ = bf16[4,128,256]{2,1,0:T(8,128)(2,1)S(1)} collective-permute-done((bf16[4,128,256]{2,1,0:T(8,128)(2,1)S(1)}, bf16[4,128,256]{2,1,0:T(8,128)(2,1)S(1)}, u32[]{:S(2)}, u32[]{:S(2)}) %collective-permute-start.15) | collective-permute-done | bytes 262176 | tf_op jit(solution)/shard_map/ppermute | solution.py:27
  72.2 2.1 %collective-permute-done.17.recv = bf16[272,768]{1,0:T(8,128)(2,1)S(1)} collective-permute-done((bf16[272,768]{1,0:T(8,128)(2,1)S(1)}, bf16[272,768]{1,0:T(8,128)(2,1)S(1)}, u32[]{:S(2)}, u32[]{:S(2)}) %collective-permute-start.17) | collective-permute-done | bytes 417824 | tf_op jit(solution)/shard_map/ppermute | solution.py:31
  74.3 1.7 %shard_map.104 = (bf16[256,384]{1,0:T(8,128)(2,1)S(1)}, bf16[4,128,256]{2,1,0:T(8,128)(2,1)S(1)}, bf16[4,128,256]{2,1,0:T(8,128)(2,1)S(1)}, bf16[4,128,256]{2,1,0:T(8,128)(2,1)S(1)}, bf16[4,128,256]{2,1,0:T(8,128)(2,1)S(1)}) custom-call(s32[5]{0:T(128)S(1)} %stack.44.ids, bf16[272,768]{1,0:T(8,128)(2,1)S(1)} %get-tuple-element.57.mine, ...), custom_call_target="tpu_custom_call" | custom-call | flops 536870912 | bytes 6799360 | tf_op jit(solution)/shard_map/pallas_call | solution.py:52
  75.9 1.5 %collective-permute-start.18 = (bf16[4,128,256]{2,1,0:T(8,128)(2,1)S(1)}, bf16[4,128,256]{2,1,0:T(8,128)(2,1)S(1)}, u32[]{:S(2)}, u32[]{:S(2)}) collective-permute-start(bf16[4,128,256]{2,1,0:T(8,128)(2,1)S(1)} %get-tuple-element.59), channel_id=1, source_target_pairs={{0,2},{1,3},{2,0},{3,1},{4,6},{5,7},{6,4},{7,5},{8,10},{9,11},{10,... | collective-permute-start | bytes 786440 | tf_op jit(solution)/shard_map/ppermute | solution.py:27
  77.4 3.4 %collective-permute-start.19 = (bf16[4,128,256]{2,1,0:T(8,128)(2,1)S(1)}, bf16[4,128,256]{2,1,0:T(8,128)(2,1)S(1)}, u32[]{:S(2)}, u32[]{:S(2)}) collective-permute-start(bf16[4,128,256]{2,1,0:T(8,128)(2,1)S(1)} %get-tuple-element.60), channel_id=1, source_target_pairs={{0,3},{1,0},{2,1},{3,2},{4,7},{5,4},{6,5},{7,6},{8,11},{9,8},{10,9... | collective-permute-start | bytes 786440 | tf_op jit(solution)/shard_map/ppermute | solution.py:27
  80.9 5.7 %collective-permute-done.21.d_recv = bf16[256,384]{1,0:T(8,128)(2,1)S(1)} collective-permute-done((bf16[256,384]{1,0:T(8,128)(2,1)S(1)}, bf16[256,384]{1,0:T(8,128)(2,1)S(1)}, u32[]{:S(2)}, u32[]{:S(2)}) %collective-permute-start.21) | collective-permute-done | bytes 196640 | tf_op jit(solution)/shard_map/ppermute | solution.py:31
  87.8 1.9 %shard_map.106 = (bf16[4,144,256]{2,1,0:T(8,128)(2,1)S(1)}, bf16[4,144,256]{2,1,0:T(8,128)(2,1)S(1)}, bf16[4,144,256]{2,1,0:T(8,128)(2,1)S(1)}, bf16[4,144,256]{2,1,0:T(8,128)(2,1)S(1)}) custom-call(s32[5]{0:T(128)S(1)} %stack.44.ids, bf16[256,768]{1,0:T(8,128)(2,1)S(1)} %get-tuple-element.62.acts, bf16[2,16,256]{2,1,0:T(8,128)(2,1)S(1)} %get-tuple-element.63.tail, ...), custom_call_target="tpu_custom_call" | custom-call | flops 1073741824 | bytes 6307840 | tf_op jit(solution)/shard_map/pallas_call | solution.py:52
  90.9 2.4 %shard_map.109 = (bf16[3,4,256,384]{3,2,1,0:T(8,128)(2,1)S(1)}, bf16[3,4,256,384]{3,2,1,0:T(8,128)(2,1)S(1)}) custom-call(s32[5]{0:T(128)S(1)} %stack.44.ids, bf16[256,768]{1,0:T(8,128)(2,1)S(1)} %get-tuple-element.62.acts, bf16[256,384]{1,0:T(8,128)(2,1)S(1)} %get-tuple-element.73.inner, bf16[256,2048]{1,0:T(8,128)(2,1)S(1)} %get-tuple-element.74.tokens, ...), custom_call_target="tpu_custom_call" | custom-call | flops 2147483648 | bytes 7405568 | tf_op jit(solution)/shard_map/pallas_call | solution.py:52
  93.4 1.5 %collective-permute-start.22 = (bf16[4,144,256]{2,1,0:T(8,128)(2,1)S(1)}, bf16[4,144,256]{2,1,0:T(8,128)(2,1)S(1)}, u32[]{:S(2)}, u32[]{:S(2)}) collective-permute-start(bf16[4,144,256]{2,1,0:T(8,128)(2,1)S(1)} %get-tuple-element.65), channel_id=1, source_target_pairs={{0,2},{1,3},{2,0},{3,1},{4,6},{5,7},{6,4},{7,5},{8,10},{9,11},{10,... | collective-permute-start | bytes 884744 | tf_op jit(solution)/shard_map/ppermute | solution.py:27
  95.3 2.8 %collective-permute-start.24 = (bf16[4,144,256]{2,1,0:T(8,128)(2,1)S(1)}, bf16[4,144,256]{2,1,0:T(8,128)(2,1)S(1)}, u32[]{:S(2)}, u32[]{:S(2)}) collective-permute-start(bf16[4,144,256]{2,1,0:T(8,128)(2,1)S(1)} %get-tuple-element.67), channel_id=1, source_target_pairs={{0,1},{1,2},{2,3},{3,0},{4,5},{5,6},{6,7},{7,4},{8,9},{9,10},{10,1... | collective-permute-start | bytes 884744 | tf_op jit(solution)/shard_map/ppermute | solution.py:27
  101.5 3.3 %collective-permute-done.22.refs_5_ = bf16[4,144,256]{2,1,0:T(8,128)(2,1)S(1)} collective-permute-done((bf16[4,144,256]{2,1,0:T(8,128)(2,1)S(1)}, bf16[4,144,256]{2,1,0:T(8,128)(2,1)S(1)}, u32[]{:S(2)}, u32[]{:S(2)}) %collective-permute-start.22) | collective-permute-done | bytes 294944 | tf_op jit(solution)/shard_map/ppermute | solution.py:27
  104.9 5.8 %collective-permute-done.23.refs_6_ = bf16[4,144,256]{2,1,0:T(8,128)(2,1)S(1)} collective-permute-done((bf16[4,144,256]{2,1,0:T(8,128)(2,1)S(1)}, bf16[4,144,256]{2,1,0:T(8,128)(2,1)S(1)}, u32[]{:S(2)}, u32[]{:S(2)}) %collective-permute-start.23) | collective-permute-done | bytes 294944 | tf_op jit(solution)/shard_map/ppermute | solution.py:27
  111.4 1.7 %collective-permute-start.32 = (bf16[3,256,384]{2,1,0:T(8,128)(2,1)S(1)}, bf16[3,256,384]{2,1,0:T(8,128)(2,1)S(1)}, u32[]{:S(2)}, u32[]{:S(2)}) collective-permute-start(bf16[3,256,384]{2,1,0:T(8,128)(2,1)S(1)} %get-tuple-element.84), channel_id=1, source_target_pairs={{0,64},{32,96},{64,0},{96,32},{1,65},{33,97},{65,1},{97,33},{2,66}... | collective-permute-start | bytes 1769480 | tf_op jit(solution)/shard_map/ppermute | solution.py:27
  113.1 4.0 %collective-permute-start.27 = (bf16[272,256]{1,0:T(8,128)(2,1)S(1)}, bf16[272,256]{1,0:T(8,128)(2,1)S(1)}, u32[]{:S(2)}, u32[]{:S(2)}) collective-permute-start(bf16[272,256]{1,0:T(8,128)(2,1)S(1)} %get-tuple-element.70), channel_id=1, source_target_pairs={{8,0},{12,4},{136,8},{140,12},{0,128},{4,132},{128,136},{132,140},... | collective-permute-start | bytes 417800 | tf_op jit(solution)/shard_map/ppermute | solution.py:322
  118.6 10.8 %collective-permute-done.30.p3 = bf16[3,256,384]{2,1,0:T(8,128)(2,1)S(1)} collective-permute-done((bf16[3,256,384]{2,1,0:T(8,128)(2,1)S(1)}, bf16[3,256,384]{2,1,0:T(8,128)(2,1)S(1)}, u32[]{:S(2)}, u32[]{:S(2)}) %collective-permute-start.30) | collective-permute-done | bytes 589856 | tf_op jit(solution)/shard_map/ppermute | solution.py:27
  129.4 2.2 %collective-permute-start.31 = (bf16[272,256]{1,0:T(8,128)(2,1)S(1)}, bf16[272,256]{1,0:T(8,128)(2,1)S(1)}, u32[]{:S(2)}, u32[]{:S(2)}) collective-permute-start(bf16[272,256]{1,0:T(8,128)(2,1)S(1)} %get-tuple-element.80), channel_id=1, source_target_pairs={{12,0},{8,4},{140,8},{136,12},{4,128},{0,132},{132,136},{128,140},... | collective-permute-start | bytes 417800 | tf_op jit(solution)/shard_map/ppermute | solution.py:322
  131.6 1.8 %shard_map.111 = (f32[256,384]{1,0:T(8,128)}, f32[256,384]{1,0:T(8,128)}, f32[384,256]{1,0:T(8,128)}) custom-call(s32[5]{0:T(128)S(1)} %stack.44.ids, bf16[3,256,384]{2,1,0:T(8,128)(2,1)S(1)} %get-tuple-element.82.p0, bf16[3,256,384]{2,1,0:T(8,128)(2,1)S(1)} %collective-permute-done.29.p1, bf16[3,256,384]{2,1,0:T(8,128)(2,1)S(1)} %collective-permute-done.32.p2, ...), custom_call_target="tpu_custom_call" | custom-call | bytes 2949120 | tf_op jit(solution)/shard_map/pallas_call | solution.py:52
  133.4 2.8 %collective-permute-done.31.p3 = bf16[272,256]{1,0:T(8,128)(2,1)S(1)} collective-permute-done((bf16[272,256]{1,0:T(8,128)(2,1)S(1)}, bf16[272,256]{1,0:T(8,128)(2,1)S(1)}, u32[]{:S(2)}, u32[]{:S(2)}) %collective-permute-start.31) | collective-permute-done | bytes 139296 | tf_op jit(solution)/shard_map/ppermute | solution.py:322
  (56 shorter events, 22.1 us)
Async XLA Ops:
  2.8 28.2 %collective-permute-start.8 = (bf16[3,256,384]{2,1,0:T(8,128)(2,1)S(1)}, bf16[3,256,384]{2,1,0:T(8,128)(2,1)S(1)}, u32[]{:S(2)}, u32[]{:S(2)}) collective-permute-start(bf16[3,256,384]{2,1,0:T(8,128)(2,1)S(1)} %pad_maximum_fusion.refs_4_.refs_0_), channel_id=1, source_target_pairs={{0,96},{32,0},{64,32},{96,64},{1,97},{33,1},{65,33},{97,65},{2,98}... | collective-permute-start | bytes 1769480 | tf_op jit(solution)/shard_map/ppermute | solution.py:27
  5.9 25.1 %collective-permute-start.7 = (bf16[3,256,384]{2,1,0:T(8,128)(2,1)S(1)}, bf16[3,256,384]{2,1,0:T(8,128)(2,1)S(1)}, u32[]{:S(2)}, u32[]{:S(2)}) collective-permute-start(bf16[3,256,384]{2,1,0:T(8,128)(2,1)S(1)} %pad_maximum_fusion.refs_4_.refs_0_), channel_id=1, source_target_pairs={{0,32},{32,64},{64,96},{96,0},{1,33},{33,65},{65,97},{97,1},{2,34}... | collective-permute-start | bytes 1769480 | tf_op jit(solution)/shard_map/ppermute | solution.py:27
  6.8 9.3 %collective-permute-start.3 = (bf16[2,128,256]{2,1,0:T(8,128)(2,1)S(1)}, bf16[2,128,256]{2,1,0:T(8,128)(2,1)S(1)}, u32[]{:S(2)}, u32[]{:S(2)}) collective-permute-start(bf16[2,128,256]{2,1,0:T(8,128)(2,1)S(1)} %pad_maximum_fusion.1), channel_id=1, source_target_pairs={{0,4},{4,0},{8,132},{12,128},{128,12},{132,8},{136,140},{140,136},... | collective-permute-start | bytes 393224 | tf_op jit(solution)/shard_map/ppermute | solution.py:240
  8.8 9.5 %collective-permute-start.2 = (bf16[2,128,256]{2,1,0:T(8,128)(2,1)S(1)}, bf16[2,128,256]{2,1,0:T(8,128)(2,1)S(1)}, u32[]{:S(2)}, u32[]{:S(2)}) collective-permute-start(bf16[2,128,256]{2,1,0:T(8,128)(2,1)S(1)} %pad_maximum_fusion.1), channel_id=1, source_target_pairs={{0,12},{4,8},{8,140},{12,136},{128,4},{132,0},{136,132},{140,128},... | collective-permute-start | bytes 393224 | tf_op jit(solution)/shard_map/ppermute | solution.py:240
  14.7 16.4 %collective-permute-start.1 = (bf16[2,128,256]{2,1,0:T(8,128)(2,1)S(1)}, bf16[2,128,256]{2,1,0:T(8,128)(2,1)S(1)}, u32[]{:S(2)}, u32[]{:S(2)}) collective-permute-start(bf16[2,128,256]{2,1,0:T(8,128)(2,1)S(1)} %pad_maximum_fusion.1), channel_id=1, source_target_pairs={{0,8},{4,12},{8,136},{12,140},{128,0},{132,4},{136,128},{140,132},... | collective-permute-start | bytes 393224 | tf_op jit(solution)/shard_map/ppermute | solution.py:240
  16.1 14.9 %collective-permute-start = (bf16[2,128,256]{2,1,0:T(8,128)(2,1)S(1)}, bf16[2,128,256]{2,1,0:T(8,128)(2,1)S(1)}, u32[]{:S(2)}, u32[]{:S(2)}) collective-permute-start(bf16[2,128,256]{2,1,0:T(8,128)(2,1)S(1)} %pad_maximum_fusion.1), channel_id=1, source_target_pairs={{0,0},{4,4},{8,128},{12,132},{128,8},{132,12},{136,136},{140,140},... | collective-permute-start | bytes 393224 | tf_op jit(solution)/shard_map/ppermute | solution.py:240
  31.1 13.8 %collective-permute-start.9 = (bf16[3,256,384]{2,1,0:T(8,128)(2,1)S(1)}, bf16[3,256,384]{2,1,0:T(8,128)(2,1)S(1)}, u32[]{:S(2)}, u32[]{:S(2)}) collective-permute-start(bf16[3,256,384]{2,1,0:T(8,128)(2,1)S(1)} %pad_maximum_fusion.refs_4_.refs_0_), channel_id=1, source_target_pairs={{0,64},{32,96},{64,0},{96,32},{1,65},{33,97},{65,1},{97,33},{2,66}... | collective-permute-start | bytes 1769480 | tf_op jit(solution)/shard_map/ppermute | solution.py:27
  33.7 8.4 %collective-permute-start.6 = (bf16[4,128,256]{2,1,0:T(8,128)(2,1)S(1)}, bf16[4,128,256]{2,1,0:T(8,128)(2,1)S(1)}, u32[]{:S(2)}, u32[]{:S(2)}) collective-permute-start(bf16[4,128,256]{2,1,0:T(8,128)(2,1)S(1)} %get-tuple-element.48.refs_0_), channel_id=1, source_target_pairs={{0,2},{1,3},{2,0},{3,1},{4,6},{5,7},{6,4},{7,5},{8,10},{9,11},{10,... | collective-permute-start | bytes 786440 | tf_op jit(solution)/shard_map/ppermute | solution.py:27
  35.2 9.6 %collective-permute-start.5 = (bf16[4,128,256]{2,1,0:T(8,128)(2,1)S(1)}, bf16[4,128,256]{2,1,0:T(8,128)(2,1)S(1)}, u32[]{:S(2)}, u32[]{:S(2)}) collective-permute-start(bf16[4,128,256]{2,1,0:T(8,128)(2,1)S(1)} %get-tuple-element.48.refs_0_), channel_id=1, source_target_pairs={{0,3},{1,0},{2,1},{3,2},{4,7},{5,4},{6,5},{7,6},{8,11},{9,8},{10,9... | collective-permute-start | bytes 786440 | tf_op jit(solution)/shard_map/ppermute | solution.py:27
  35.2 9.6 %collective-permute-start.4 = (bf16[4,128,256]{2,1,0:T(8,128)(2,1)S(1)}, bf16[4,128,256]{2,1,0:T(8,128)(2,1)S(1)}, u32[]{:S(2)}, u32[]{:S(2)}) collective-permute-start(bf16[4,128,256]{2,1,0:T(8,128)(2,1)S(1)} %get-tuple-element.48.refs_0_), channel_id=1, source_target_pairs={{0,1},{1,2},{2,3},{3,0},{4,5},{5,6},{6,7},{7,4},{8,9},{9,10},{10,1... | collective-permute-start | bytes 786440 | tf_op jit(solution)/shard_map/ppermute | solution.py:27
  38.4 6.9 %collective-permute-start.10 = (bf16[3,256,384]{2,1,0:T(8,128)(2,1)S(1)}, bf16[3,256,384]{2,1,0:T(8,128)(2,1)S(1)}, u32[]{:S(2)}, u32[]{:S(2)}) collective-permute-start(bf16[3,256,384]{2,1,0:T(8,128)(2,1)S(1)} %pad_maximum_fusion.refs_4_.refs_0_), channel_id=1, source_target_pairs={{0,16},{16,0},{1,17},{17,1},{2,18},{18,2},{3,19},{19,3},{4,20},{20... | collective-permute-start | bytes 1769480 | tf_op jit(solution)/shard_map/ppermute | solution.py:31
  42.1 3.2 %collective-permute-start.11 = (bf16[3,256,384]{2,1,0:T(8,128)(2,1)S(1)}, bf16[3,256,384]{2,1,0:T(8,128)(2,1)S(1)}, u32[]{:S(2)}, u32[]{:S(2)}) collective-permute-start(bf16[3,256,384]{2,1,0:T(8,128)(2,1)S(1)} %collective-permute-done.7.refs_5_.refs_1_), channel_id=1, source_target_pairs={{0,16},{16,0},{1,17},{17,1},{2,18},{18,2},{3,19},{19,3},{4,20},{20... | collective-permute-start | bytes 1769480 | tf_op jit(solution)/shard_map/ppermute | solution.py:31
  44.8 2.8 %collective-permute-start.12 = (bf16[3,256,384]{2,1,0:T(8,128)(2,1)S(1)}, bf16[3,256,384]{2,1,0:T(8,128)(2,1)S(1)}, u32[]{:S(2)}, u32[]{:S(2)}) collective-permute-start(bf16[3,256,384]{2,1,0:T(8,128)(2,1)S(1)} %collective-permute-done.9.refs_6_.refs_2_), channel_id=1, source_target_pairs={{0,16},{16,0},{1,17},{17,1},{2,18},{18,2},{3,19},{19,3},{4,20},{20... | collective-permute-start | bytes 1769480 | tf_op jit(solution)/shard_map/ppermute | solution.py:31
  49.6 24.7 %collective-permute-start.17 = (bf16[272,768]{1,0:T(8,128)(2,1)S(1)}, bf16[272,768]{1,0:T(8,128)(2,1)S(1)}, u32[]{:S(2)}, u32[]{:S(2)}) collective-permute-start(bf16[272,768]{1,0:T(8,128)(2,1)S(1)} %get-tuple-element.57.mine), channel_id=1, source_target_pairs={{0,128},{128,0},{1,129},{129,1},{2,130},{130,2},{3,131},{131,3},{4... | collective-permute-start | bytes 1253384 | tf_op jit(solution)/shard_map/ppermute | solution.py:31
  55.0 10.7 %collective-permute-start.16 = (bf16[4,128,256]{2,1,0:T(8,128)(2,1)S(1)}, bf16[4,128,256]{2,1,0:T(8,128)(2,1)S(1)}, u32[]{:S(2)}, u32[]{:S(2)}) collective-permute-start(bf16[4,128,256]{2,1,0:T(8,128)(2,1)S(1)} %get-tuple-element.55.refs_0_), channel_id=1, source_target_pairs={{0,2},{1,3},{2,0},{3,1},{4,6},{5,7},{6,4},{7,5},{8,10},{9,11},{10,... | collective-permute-start | bytes 786440 | tf_op jit(solution)/shard_map/ppermute | solution.py:27
  56.4 13.8 %collective-permute-start.15 = (bf16[4,128,256]{2,1,0:T(8,128)(2,1)S(1)}, bf16[4,128,256]{2,1,0:T(8,128)(2,1)S(1)}, u32[]{:S(2)}, u32[]{:S(2)}) collective-permute-start(bf16[4,128,256]{2,1,0:T(8,128)(2,1)S(1)} %get-tuple-element.55.refs_0_), channel_id=1, source_target_pairs={{0,3},{1,0},{2,1},{3,2},{4,7},{5,4},{6,5},{7,6},{8,11},{9,8},{10,9... | collective-permute-start | bytes 786440 | tf_op jit(solution)/shard_map/ppermute | solution.py:27
  56.6 13.6 %collective-permute-start.14 = (bf16[4,128,256]{2,1,0:T(8,128)(2,1)S(1)}, bf16[4,128,256]{2,1,0:T(8,128)(2,1)S(1)}, u32[]{:S(2)}, u32[]{:S(2)}) collective-permute-start(bf16[4,128,256]{2,1,0:T(8,128)(2,1)S(1)} %get-tuple-element.55.refs_0_), channel_id=1, source_target_pairs={{0,1},{1,2},{2,3},{3,0},{4,5},{5,6},{6,7},{7,4},{8,9},{9,10},{10,1... | collective-permute-start | bytes 786440 | tf_op jit(solution)/shard_map/ppermute | solution.py:27
  71.5 15.0 %collective-permute-start.21 = (bf16[256,384]{1,0:T(8,128)(2,1)S(1)}, bf16[256,384]{1,0:T(8,128)(2,1)S(1)}, u32[]{:S(2)}, u32[]{:S(2)}) collective-permute-start(bf16[256,384]{1,0:T(8,128)(2,1)S(1)} %get-tuple-element.56.d_mine), channel_id=1, source_target_pairs={{0,128},{128,0},{1,129},{129,1},{2,130},{130,2},{3,131},{131,3},{4... | collective-permute-start | bytes 589832 | tf_op jit(solution)/shard_map/ppermute | solution.py:31
  75.9 13.8 %collective-permute-start.18 = (bf16[4,128,256]{2,1,0:T(8,128)(2,1)S(1)}, bf16[4,128,256]{2,1,0:T(8,128)(2,1)S(1)}, u32[]{:S(2)}, u32[]{:S(2)}) collective-permute-start(bf16[4,128,256]{2,1,0:T(8,128)(2,1)S(1)} %get-tuple-element.59), channel_id=1, source_target_pairs={{0,2},{1,3},{2,0},{3,1},{4,6},{5,7},{6,4},{7,5},{8,10},{9,11},{10,... | collective-permute-start | bytes 786440 | tf_op jit(solution)/shard_map/ppermute | solution.py:27
  77.4 13.5 %collective-permute-start.19 = (bf16[4,128,256]{2,1,0:T(8,128)(2,1)S(1)}, bf16[4,128,256]{2,1,0:T(8,128)(2,1)S(1)}, u32[]{:S(2)}, u32[]{:S(2)}) collective-permute-start(bf16[4,128,256]{2,1,0:T(8,128)(2,1)S(1)} %get-tuple-element.60), channel_id=1, source_target_pairs={{0,3},{1,0},{2,1},{3,2},{4,7},{5,4},{6,5},{7,6},{8,11},{9,8},{10,9... | collective-permute-start | bytes 786440 | tf_op jit(solution)/shard_map/ppermute | solution.py:27
  80.9 10.1 %collective-permute-start.20 = (bf16[4,128,256]{2,1,0:T(8,128)(2,1)S(1)}, bf16[4,128,256]{2,1,0:T(8,128)(2,1)S(1)}, u32[]{:S(2)}, u32[]{:S(2)}) collective-permute-start(bf16[4,128,256]{2,1,0:T(8,128)(2,1)S(1)} %get-tuple-element.61), channel_id=1, source_target_pairs={{0,1},{1,2},{2,3},{3,0},{4,5},{5,6},{6,7},{7,4},{8,9},{9,10},{10,1... | collective-permute-start | bytes 786440 | tf_op jit(solution)/shard_map/ppermute | solution.py:27
  93.3 4.8 %collective-permute-start.28 = (bf16[3,4,256,384]{3,2,1,0:T(8,128)(2,1)S(1)}, bf16[3,4,256,384]{3,2,1,0:T(8,128)(2,1)S(1)}, u32[]{:S(2)}, u32[]{:S(2)}) collective-permute-start(bf16[3,4,256,384]{3,2,1,0:T(8,128)(2,1)S(1)} %get-tuple-element.77), channel_id=1, source_target_pairs={{0,16},{16,0},{1,17},{17,1},{2,18},{18,2},{3,19},{19,3},{4,20},{20... | collective-permute-start | bytes 7077896 | tf_op jit(solution)/shard_map/ppermute | solution.py:31
  93.4 11.4 %collective-permute-start.22 = (bf16[4,144,256]{2,1,0:T(8,128)(2,1)S(1)}, bf16[4,144,256]{2,1,0:T(8,128)(2,1)S(1)}, u32[]{:S(2)}, u32[]{:S(2)}) collective-permute-start(bf16[4,144,256]{2,1,0:T(8,128)(2,1)S(1)} %get-tuple-element.65), channel_id=1, source_target_pairs={{0,2},{1,3},{2,0},{3,1},{4,6},{5,7},{6,4},{7,5},{8,10},{9,11},{10,... | collective-permute-start | bytes 884744 | tf_op jit(solution)/shard_map/ppermute | solution.py:27
  94.9 15.8 %collective-permute-start.23 = (bf16[4,144,256]{2,1,0:T(8,128)(2,1)S(1)}, bf16[4,144,256]{2,1,0:T(8,128)(2,1)S(1)}, u32[]{:S(2)}, u32[]{:S(2)}) collective-permute-start(bf16[4,144,256]{2,1,0:T(8,128)(2,1)S(1)} %get-tuple-element.66), channel_id=1, source_target_pairs={{0,3},{1,0},{2,1},{3,2},{4,7},{5,4},{6,5},{7,6},{8,11},{9,8},{10,9... | collective-permute-start | bytes 884744 | tf_op jit(solution)/shard_map/ppermute | solution.py:27
  95.3 15.3 %collective-permute-start.24 = (bf16[4,144,256]{2,1,0:T(8,128)(2,1)S(1)}, bf16[4,144,256]{2,1,0:T(8,128)(2,1)S(1)}, u32[]{:S(2)}, u32[]{:S(2)}) collective-permute-start(bf16[4,144,256]{2,1,0:T(8,128)(2,1)S(1)} %get-tuple-element.67), channel_id=1, source_target_pairs={{0,1},{1,2},{2,3},{3,0},{4,5},{5,6},{6,7},{7,4},{8,9},{9,10},{10,1... | collective-permute-start | bytes 884744 | tf_op jit(solution)/shard_map/ppermute | solution.py:27
  99.3 19.2 %collective-permute-start.29 = (bf16[3,256,384]{2,1,0:T(8,128)(2,1)S(1)}, bf16[3,256,384]{2,1,0:T(8,128)(2,1)S(1)}, u32[]{:S(2)}, u32[]{:S(2)}) collective-permute-start(bf16[3,256,384]{2,1,0:T(8,128)(2,1)S(1)} %get-tuple-element.78), channel_id=1, source_target_pairs={{0,96},{32,0},{64,32},{96,64},{1,97},{33,1},{65,33},{97,65},{2,98}... | collective-permute-start | bytes 1769480 | tf_op jit(solution)/shard_map/ppermute | solution.py:27
  100.6 28.8 %collective-permute-start.30 = (bf16[3,256,384]{2,1,0:T(8,128)(2,1)S(1)}, bf16[3,256,384]{2,1,0:T(8,128)(2,1)S(1)}, u32[]{:S(2)}, u32[]{:S(2)}) collective-permute-start(bf16[3,256,384]{2,1,0:T(8,128)(2,1)S(1)} %get-tuple-element.79), channel_id=1, source_target_pairs={{0,32},{32,64},{64,96},{96,0},{1,33},{33,65},{65,97},{97,1},{2,34}... | collective-permute-start | bytes 1769480 | tf_op jit(solution)/shard_map/ppermute | solution.py:27
  111.4 20.2 %collective-permute-start.32 = (bf16[3,256,384]{2,1,0:T(8,128)(2,1)S(1)}, bf16[3,256,384]{2,1,0:T(8,128)(2,1)S(1)}, u32[]{:S(2)}, u32[]{:S(2)}) collective-permute-start(bf16[3,256,384]{2,1,0:T(8,128)(2,1)S(1)} %get-tuple-element.84), channel_id=1, source_target_pairs={{0,64},{32,96},{64,0},{96,32},{1,65},{33,97},{65,1},{97,33},{2,66}... | collective-permute-start | bytes 1769480 | tf_op jit(solution)/shard_map/ppermute | solution.py:27
  113.1 20.3 %collective-permute-start.27 = (bf16[272,256]{1,0:T(8,128)(2,1)S(1)}, bf16[272,256]{1,0:T(8,128)(2,1)S(1)}, u32[]{:S(2)}, u32[]{:S(2)}) collective-permute-start(bf16[272,256]{1,0:T(8,128)(2,1)S(1)} %get-tuple-element.70), channel_id=1, source_target_pairs={{8,0},{12,4},{136,8},{140,12},{0,128},{4,132},{128,136},{132,140},... | collective-permute-start | bytes 417800 | tf_op jit(solution)/shard_map/ppermute | solution.py:322
  117.8 15.6 %collective-permute-start.25 = (bf16[272,256]{1,0:T(8,128)(2,1)S(1)}, bf16[272,256]{1,0:T(8,128)(2,1)S(1)}, u32[]{:S(2)}, u32[]{:S(2)}) collective-permute-start(bf16[272,256]{1,0:T(8,128)(2,1)S(1)} %get-tuple-element.68), channel_id=1, source_target_pairs={{0,0},{4,4},{128,8},{132,12},{8,128},{12,132},{136,136},{140,140},... | collective-permute-start | bytes 417800 | tf_op jit(solution)/shard_map/ppermute | solution.py:322
  118.5 14.9 %collective-permute-start.26 = (bf16[272,256]{1,0:T(8,128)(2,1)S(1)}, bf16[272,256]{1,0:T(8,128)(2,1)S(1)}, u32[]{:S(2)}, u32[]{:S(2)}) collective-permute-start(bf16[272,256]{1,0:T(8,128)(2,1)S(1)} %get-tuple-element.69), channel_id=1, source_target_pairs={{4,0},{0,4},{132,8},{128,12},{12,128},{8,132},{140,136},{136,140},... | collective-permute-start | bytes 417800 | tf_op jit(solution)/shard_map/ppermute | solution.py:322
  129.4 6.9 %collective-permute-start.31 = (bf16[272,256]{1,0:T(8,128)(2,1)S(1)}, bf16[272,256]{1,0:T(8,128)(2,1)S(1)}, u32[]{:S(2)}, u32[]{:S(2)}) collective-permute-start(bf16[272,256]{1,0:T(8,128)(2,1)S(1)} %get-tuple-element.80), channel_id=1, source_target_pairs={{12,0},{8,4},{140,8},{136,12},{4,128},{0,132},{132,136},{128,140},... | collective-permute-start | bytes 417800 | tf_op jit(solution)/shard_map/ppermute | solution.py:322
  (4 other events, 98.8 us)

commit v6 on v5

--- a/solution.py
+++ b/solution.py
@@ -193,15 +193,15 @@
     return total
 
 
-def x_sum_kernel(first, ids, *refs):
+def x_sum_kernel(chosen, ids, *refs):
     forward, backward, outs = refs[:4], refs[4:8], refs[8:]
-    for k in range(2):
-        outs[k][:128] = sum_refs(forward, first + k).astype(BF16)
-        outs[k][128:256] = sum_refs(backward, (first + k, slice(0, 128))).astype(BF16)
-        tail = sum_refs(backward, (first + k, slice(128, 144)))
+    for j, k in enumerate(chosen):
+        outs[j][:128] = sum_refs(forward, k).astype(BF16)
+        outs[j][128:256] = sum_refs(backward, (k, slice(0, 128))).astype(BF16)
+        tail = sum_refs(backward, (k, slice(128, 144)))
         head, rest = split_float(tail[:, :128] + tail[:, 128:])
-        outs[k][256:, :128] = head.astype(BF16)
-        outs[k][256:, 128:] = rest.astype(BF16)
+        outs[j][256:, :128] = head.astype(BF16)
+        outs[j][256:, 128:] = rest.astype(BF16)
 
 
 def scatter_x(parts):
@@ -312,14 +312,15 @@
     )
     near = [shift(sums[1], "y", -1), shift(sums[3], "y", 1)]
     blocks = []
-    for k in (0, 2):
-        body = functools.partial(x_sum_kernel, k)
+    for chosen in ((1, 3), (2, 0)):
+        body = functools.partial(x_sum_kernel, chosen)
         parts = [*forward, *backward]
         blocks += call(body, ids, parts, [VMEM] * 8, [((272, 256), BF16)] * 2)
     blocks[3] = after(blocks[3], *near)
     far = shift(after(sums[2], blocks[2]), "y", 2)
     blocks = [
-        lax.ppermute(blocks[k], ("zh", "zl"), [(t, s) for s, t in z_pairs(k)]) for k in range(4)
+        lax.ppermute(block, ("zh", "zl"), [(t, s) for s, t in z_pairs(k)])
+        for block, k in zip(blocks, (1, 3, 2, 0))
     ]
     grad_gate, grad_up, grad_down = call(
         grads_sum_kernel,

time: 138 us -> 136 us (0.986)
  the two profiles are of different devices: /device:TPU:6 before, /device:TPU:124 now
where the time goes in v6:
time: 136 us
  waiting for transfers between devices  62.5 us (46%)
  starting transfers between devices  52.8 us (39%)
  Pallas kernels  16.7 us (12%)
  other arithmetic  1.99 us (1%)
    ppermute x18, waiting for transfers between devices, shift(): return lax.ppermute(array, axis, [(i, (i + by) % 4) for i in range(4)])  43.4 us
    ppermute x18, starting transfers between devices, shift(): return lax.ppermute(array, axis, [(i, (i + by) % 4) for i in range(4)])  21.6 us
    pallas_call x12, Pallas kernels, call(): pl.pallas_call(body, out_shape=[jax.ShapeDtypeStruct(s, d) for s, d in ou...  16.7 us
    ppermute x4, starting transfers between devices, on_device(): by_z = [lax.ppermute(pair, ('zh', 'zl'), z_pairs(k)) for k in range(4)]  14 us
    ppermute x4, starting transfers between devices, on_device(): lax.ppermute(block, ('zh', 'zl'), [(t, s) for s, t in z_pairs(k)])  11.3 us
    ppermute x7, waiting for transfers between devices, swap(): return lax.ppermute(array, axis, [(0, 1), (1, 0)])  7.36 us
    ppermute x4, waiting for transfers between devices, on_device(): by_z = [lax.ppermute(pair, ('zh', 'zl'), z_pairs(k)) for k in range(4)]  6.41 us
    ppermute x7, starting transfers between devices, swap(): return lax.ppermute(array, axis, [(0, 1), (1, 0)])  5.83 us
  transfers between devices with their start and end apart: 33, of which 23 were waited for; matrix products, arithmetic and copies ran while one was open for 1% of the time, Pallas kernels for 8%

profile of v6, /device:TPU:124, one launch (start us, length us, event | category | flops | bytes accessed | tf_op | source)
XLA Modules:
  0.0 136.0 jit_solution(15954635239140441203)
XLA Ops:
  3.7 2.5 %collective-permute-start.7 = (bf16[3,256,384]{2,1,0:T(8,128)(2,1)S(1)}, bf16[3,256,384]{2,1,0:T(8,128)(2,1)S(1)}, u32[]{:S(2)}, u32[]{:S(2)}) collective-permute-start(bf16[3,256,384]{2,1,0:T(8,128)(2,1)S(1)} %pad_maximum_fusion.refs_4_.refs_0_), channel_id=1, source_target_pairs={{0,32},{32,64},{64,96},{96,0},{1,33},{33,65},{65,97},{97,1},{2,34}... | collective-permute-start | bytes 1769480 | tf_op jit(solution)/shard_map/ppermute | solution.py:27
  7.0 3.2 %collective-permute-start.3 = (bf16[2,128,256]{2,1,0:T(8,128)(2,1)S(1)}, bf16[2,128,256]{2,1,0:T(8,128)(2,1)S(1)}, u32[]{:S(2)}, u32[]{:S(2)}) collective-permute-start(bf16[2,128,256]{2,1,0:T(8,128)(2,1)S(1)} %pad_maximum_fusion.1), channel_id=1, source_target_pairs={{0,4},{4,0},{8,132},{12,128},{128,12},{132,8},{136,140},{140,136},... | collective-permute-start | bytes 393224 | tf_op jit(solution)/shard_map/ppermute | solution.py:240
  10.3 1.9 %collective-permute-start.2 = (bf16[2,128,256]{2,1,0:T(8,128)(2,1)S(1)}, bf16[2,128,256]{2,1,0:T(8,128)(2,1)S(1)}, u32[]{:S(2)}, u32[]{:S(2)}) collective-permute-start(bf16[2,128,256]{2,1,0:T(8,128)(2,1)S(1)} %pad_maximum_fusion.1), channel_id=1, source_target_pairs={{0,12},{4,8},{8,140},{12,136},{128,4},{132,0},{136,132},{140,128},... | collective-permute-start | bytes 393224 | tf_op jit(solution)/shard_map/ppermute | solution.py:240
  13.6 3.5 %collective-permute-done.3.p1 = bf16[2,128,256]{2,1,0:T(8,128)(2,1)S(1)} collective-permute-done((bf16[2,128,256]{2,1,0:T(8,128)(2,1)S(1)}, bf16[2,128,256]{2,1,0:T(8,128)(2,1)S(1)}, u32[]{:S(2)}, u32[]{:S(2)}) %collective-permute-start.3) | collective-permute-done | bytes 131104 | tf_op jit(solution)/shard_map/ppermute | solution.py:240
  17.1 7.5 %collective-permute-start = (bf16[2,128,256]{2,1,0:T(8,128)(2,1)S(1)}, bf16[2,128,256]{2,1,0:T(8,128)(2,1)S(1)}, u32[]{:S(2)}, u32[]{:S(2)}) collective-permute-start(bf16[2,128,256]{2,1,0:T(8,128)(2,1)S(1)} %pad_maximum_fusion.1), channel_id=1, source_target_pairs={{0,0},{4,4},{8,128},{12,132},{128,8},{132,12},{136,136},{140,140},... | collective-permute-start | bytes 393224 | tf_op jit(solution)/shard_map/ppermute | solution.py:240
  24.6 2.9 %collective-permute-done.p0 = bf16[2,128,256]{2,1,0:T(8,128)(2,1)S(1)} collective-permute-done((bf16[2,128,256]{2,1,0:T(8,128)(2,1)S(1)}, bf16[2,128,256]{2,1,0:T(8,128)(2,1)S(1)}, u32[]{:S(2)}, u32[]{:S(2)}) %collective-permute-start) | collective-permute-done | bytes 131104 | tf_op jit(solution)/shard_map/ppermute | solution.py:240
  28.8 2.2 %collective-permute-start.5 = (bf16[4,128,256]{2,1,0:T(8,128)(2,1)S(1)}, bf16[4,128,256]{2,1,0:T(8,128)(2,1)S(1)}, u32[]{:S(2)}, u32[]{:S(2)}) collective-permute-start(bf16[4,128,256]{2,1,0:T(8,128)(2,1)S(1)} %get-tuple-element.48.refs_0_), channel_id=1, source_target_pairs={{0,3},{1,0},{2,1},{3,2},{4,7},{5,4},{6,5},{7,6},{8,11},{9,8},{10,9... | collective-permute-start | bytes 786440 | tf_op jit(solution)/shard_map/ppermute | solution.py:27
  31.0 7.0 %collective-permute-done.6.refs_3_ = bf16[4,128,256]{2,1,0:T(8,128)(2,1)S(1)} collective-permute-done((bf16[4,128,256]{2,1,0:T(8,128)(2,1)S(1)}, bf16[4,128,256]{2,1,0:T(8,128)(2,1)S(1)}, u32[]{:S(2)}, u32[]{:S(2)}) %collective-permute-start.6) | collective-permute-done | bytes 262176 | tf_op jit(solution)/shard_map/ppermute | solution.py:27
  38.0 1.8 %collective-permute-done.5.refs_2_ = bf16[4,128,256]{2,1,0:T(8,128)(2,1)S(1)} collective-permute-done((bf16[4,128,256]{2,1,0:T(8,128)(2,1)S(1)}, bf16[4,128,256]{2,1,0:T(8,128)(2,1)S(1)}, u32[]{:S(2)}, u32[]{:S(2)}) %collective-permute-start.5) | collective-permute-done | bytes 262176 | tf_op jit(solution)/shard_map/ppermute | solution.py:27
  43.3 1.9 %shard_map.102 = (bf16[272,768]{1,0:T(8,128)(2,1)S(1)}, bf16[256,2048]{1,0:T(8,128)(2,1)S(1)}) custom-call(s32[5]{0:T(128)S(1)} %stack.44.ids, bf16[4,128,256]{2,1,0:T(8,128)(2,1)S(1)} %get-tuple-element.48.refs_0_, bf16[4,128,256]{2,1,0:T(8,128)(2,1)S(1)} %collective-permute-done.4.refs_1_, bf16[4,128,256]{2,1,0:T(8,128)(2,1)S(1)} %collective-permute-done.5.refs_2_, ...), custom_call_target="tpu_custom_call" | custom-call | bytes 7249920 | tf_op jit(solution)/shard_map/pallas_call | solution.py:52
  46.5 1.9 %collective-permute-start.15 = (bf16[4,128,256]{2,1,0:T(8,128)(2,1)S(1)}, bf16[4,128,256]{2,1,0:T(8,128)(2,1)S(1)}, u32[]{:S(2)}, u32[]{:S(2)}) collective-permute-start(bf16[4,128,256]{2,1,0:T(8,128)(2,1)S(1)} %get-tuple-element.55.refs_0_), channel_id=1, source_target_pairs={{0,3},{1,0},{2,1},{3,2},{4,7},{5,4},{6,5},{7,6},{8,11},{9,8},{10,9... | collective-permute-start | bytes 786440 | tf_op jit(solution)/shard_map/ppermute | solution.py:27
  48.5 7.6 %collective-permute-done.16.refs_3_ = bf16[4,128,256]{2,1,0:T(8,128)(2,1)S(1)} collective-permute-done((bf16[4,128,256]{2,1,0:T(8,128)(2,1)S(1)}, bf16[4,128,256]{2,1,0:T(8,128)(2,1)S(1)}, u32[]{:S(2)}, u32[]{:S(2)}) %collective-permute-start.16) | collective-permute-done | bytes 262176 | tf_op jit(solution)/shard_map/ppermute | solution.py:27
  56.1 4.1 %collective-permute-done.15.refs_2_ = bf16[4,128,256]{2,1,0:T(8,128)(2,1)S(1)} collective-permute-done((bf16[4,128,256]{2,1,0:T(8,128)(2,1)S(1)}, bf16[4,128,256]{2,1,0:T(8,128)(2,1)S(1)}, u32[]{:S(2)}, u32[]{:S(2)}) %collective-permute-start.15) | collective-permute-done | bytes 262176 | tf_op jit(solution)/shard_map/ppermute | solution.py:27
  62.2 5.6 %collective-permute-start.21 = (bf16[256,384]{1,0:T(8,128)(2,1)S(1)}, bf16[256,384]{1,0:T(8,128)(2,1)S(1)}, u32[]{:S(2)}, u32[]{:S(2)}) collective-permute-start(bf16[256,384]{1,0:T(8,128)(2,1)S(1)} %get-tuple-element.56.d_mine), channel_id=1, source_target_pairs={{0,128},{128,0},{1,129},{129,1},{2,130},{130,2},{3,131},{131,3},{4... | collective-permute-start | bytes 589832 | tf_op jit(solution)/shard_map/ppermute | solution.py:31
  67.9 2.3 %collective-permute-done.17.recv = bf16[272,768]{1,0:T(8,128)(2,1)S(1)} collective-permute-done((bf16[272,768]{1,0:T(8,128)(2,1)S(1)}, bf16[272,768]{1,0:T(8,128)(2,1)S(1)}, u32[]{:S(2)}, u32[]{:S(2)}) %collective-permute-start.17) | collective-permute-done | bytes 417824 | tf_op jit(solution)/shard_map/ppermute | solution.py:31
  72.8 2.0 %collective-permute-start.19 = (bf16[4,128,256]{2,1,0:T(8,128)(2,1)S(1)}, bf16[4,128,256]{2,1,0:T(8,128)(2,1)S(1)}, u32[]{:S(2)}, u32[]{:S(2)}) collective-permute-start(bf16[4,128,256]{2,1,0:T(8,128)(2,1)S(1)} %get-tuple-element.60), channel_id=1, source_target_pairs={{0,3},{1,0},{2,1},{3,2},{4,7},{5,4},{6,5},{7,6},{8,11},{9,8},{10,9... | collective-permute-start | bytes 786440 | tf_op jit(solution)/shard_map/ppermute | solution.py:27
  74.8 1.9 %collective-permute-done.21.d_recv = bf16[256,384]{1,0:T(8,128)(2,1)S(1)} collective-permute-done((bf16[256,384]{1,0:T(8,128)(2,1)S(1)}, bf16[256,384]{1,0:T(8,128)(2,1)S(1)}, u32[]{:S(2)}, u32[]{:S(2)}) %collective-permute-start.21) | collective-permute-done | bytes 196640 | tf_op jit(solution)/shard_map/ppermute | solution.py:31
  78.0 1.9 %shard_map.106 = (bf16[4,144,256]{2,1,0:T(8,128)(2,1)S(1)}, bf16[4,144,256]{2,1,0:T(8,128)(2,1)S(1)}, bf16[4,144,256]{2,1,0:T(8,128)(2,1)S(1)}, bf16[4,144,256]{2,1,0:T(8,128)(2,1)S(1)}) custom-call(s32[5]{0:T(128)S(1)} %stack.44.ids, bf16[256,768]{1,0:T(8,128)(2,1)S(1)} %get-tuple-element.62.acts, bf16[2,16,256]{2,1,0:T(8,128)(2,1)S(1)} %get-tuple-element.63.tail, ...), custom_call_target="tpu_custom_call" | custom-call | flops 1073741824 | bytes 6307840 | tf_op jit(solution)/shard_map/pallas_call | solution.py:52
  80.0 2.1 %collective-permute-done.18.refs_1_ = bf16[4,128,256]{2,1,0:T(8,128)(2,1)S(1)} collective-permute-done((bf16[4,128,256]{2,1,0:T(8,128)(2,1)S(1)}, bf16[4,128,256]{2,1,0:T(8,128)(2,1)S(1)}, u32[]{:S(2)}, u32[]{:S(2)}) %collective-permute-start.18) | collective-permute-done | bytes 262176 | tf_op jit(solution)/shard_map/ppermute | solution.py:27
  82.0 2.0 %collective-permute-done.19.refs_2_ = bf16[4,128,256]{2,1,0:T(8,128)(2,1)S(1)} collective-permute-done((bf16[4,128,256]{2,1,0:T(8,128)(2,1)S(1)}, bf16[4,128,256]{2,1,0:T(8,128)(2,1)S(1)}, u32[]{:S(2)}, u32[]{:S(2)}) %collective-permute-start.19) | collective-permute-done | bytes 262176 | tf_op jit(solution)/shard_map/ppermute | solution.py:27
  84.7 2.4 %shard_map.109 = (bf16[3,4,256,384]{3,2,1,0:T(8,128)(2,1)S(1)}, bf16[3,4,256,384]{3,2,1,0:T(8,128)(2,1)S(1)}) custom-call(s32[5]{0:T(128)S(1)} %stack.44.ids, bf16[256,768]{1,0:T(8,128)(2,1)S(1)} %get-tuple-element.62.acts, bf16[256,384]{1,0:T(8,128)(2,1)S(1)} %get-tuple-element.73.inner, bf16[256,2048]{1,0:T(8,128)(2,1)S(1)} %get-tuple-element.74.tokens, ...), custom_call_target="tpu_custom_call" | custom-call | flops 2147483648 | bytes 7405568 | tf_op jit(solution)/shard_map/pallas_call | solution.py:52
  93.1 3.0 %collective-permute-start.30 = (bf16[3,256,384]{2,1,0:T(8,128)(2,1)S(1)}, bf16[3,256,384]{2,1,0:T(8,128)(2,1)S(1)}, u32[]{:S(2)}, u32[]{:S(2)}) collective-permute-start(bf16[3,256,384]{2,1,0:T(8,128)(2,1)S(1)} %get-tuple-element.79), channel_id=1, source_target_pairs={{0,32},{32,64},{64,96},{96,0},{1,33},{33,65},{65,97},{97,1},{2,34}... | collective-permute-start | bytes 1769480 | tf_op jit(solution)/shard_map/ppermute | solution.py:27
  96.1 2.5 %collective-permute-done.22.refs_5_ = bf16[4,144,256]{2,1,0:T(8,128)(2,1)S(1)} collective-permute-done((bf16[4,144,256]{2,1,0:T(8,128)(2,1)S(1)}, bf16[4,144,256]{2,1,0:T(8,128)(2,1)S(1)}, u32[]{:S(2)}, u32[]{:S(2)}) %collective-permute-start.22) | collective-permute-done | bytes 294944 | tf_op jit(solution)/shard_map/ppermute | solution.py:27
  98.6 5.1 %collective-permute-done.23.refs_6_ = bf16[4,144,256]{2,1,0:T(8,128)(2,1)S(1)} collective-permute-done((bf16[4,144,256]{2,1,0:T(8,128)(2,1)S(1)}, bf16[4,144,256]{2,1,0:T(8,128)(2,1)S(1)}, u32[]{:S(2)}, u32[]{:S(2)}) %collective-permute-start.23) | collective-permute-done | bytes 294944 | tf_op jit(solution)/shard_map/ppermute | solution.py:27
  105.1 2.7 %collective-permute-start.32 = (bf16[3,256,384]{2,1,0:T(8,128)(2,1)S(1)}, bf16[3,256,384]{2,1,0:T(8,128)(2,1)S(1)}, u32[]{:S(2)}, u32[]{:S(2)}) collective-permute-start(bf16[3,256,384]{2,1,0:T(8,128)(2,1)S(1)} %get-tuple-element.84), channel_id=1, source_target_pairs={{0,64},{32,96},{64,0},{96,32},{1,65},{33,97},{65,1},{97,33},{2,66}... | collective-permute-start | bytes 1769480 | tf_op jit(solution)/shard_map/ppermute | solution.py:27
  107.8 1.9 %collective-permute-start.27 = (bf16[272,256]{1,0:T(8,128)(2,1)S(1)}, bf16[272,256]{1,0:T(8,128)(2,1)S(1)}, u32[]{:S(2)}, u32[]{:S(2)}) collective-permute-start(bf16[272,256]{1,0:T(8,128)(2,1)S(1)} %get-tuple-element.70), channel_id=1, source_target_pairs={{8,0},{12,4},{136,8},{140,12},{0,128},{4,132},{128,136},{132,140},... | collective-permute-start | bytes 417800 | tf_op jit(solution)/shard_map/ppermute | solution.py:322
  110.4 4.0 %collective-permute-start.25 = (bf16[272,256]{1,0:T(8,128)(2,1)S(1)}, bf16[272,256]{1,0:T(8,128)(2,1)S(1)}, u32[]{:S(2)}, u32[]{:S(2)}) collective-permute-start(bf16[272,256]{1,0:T(8,128)(2,1)S(1)} %get-tuple-element.68), channel_id=1, source_target_pairs={{4,0},{0,4},{132,8},{128,12},{12,128},{8,132},{140,136},{136,140},... | collective-permute-start | bytes 417800 | tf_op jit(solution)/shard_map/ppermute | solution.py:322
  114.4 7.7 %collective-permute-done.29.p1 = bf16[3,256,384]{2,1,0:T(8,128)(2,1)S(1)} collective-permute-done((bf16[3,256,384]{2,1,0:T(8,128)(2,1)S(1)}, bf16[3,256,384]{2,1,0:T(8,128)(2,1)S(1)}, u32[]{:S(2)}, u32[]{:S(2)}) %collective-permute-start.29) | collective-permute-done | bytes 589856 | tf_op jit(solution)/shard_map/ppermute | solution.py:27
  122.1 3.4 %collective-permute-start.26 = (bf16[272,256]{1,0:T(8,128)(2,1)S(1)}, bf16[272,256]{1,0:T(8,128)(2,1)S(1)}, u32[]{:S(2)}, u32[]{:S(2)}) collective-permute-start(bf16[272,256]{1,0:T(8,128)(2,1)S(1)} %get-tuple-element.69), channel_id=1, source_target_pairs={{12,0},{8,4},{140,8},{136,12},{4,128},{0,132},{132,136},{128,140},... | collective-permute-start | bytes 417800 | tf_op jit(solution)/shard_map/ppermute | solution.py:322
  125.6 1.9 %collective-permute-start.31 = (bf16[272,256]{1,0:T(8,128)(2,1)S(1)}, bf16[272,256]{1,0:T(8,128)(2,1)S(1)}, u32[]{:S(2)}, u32[]{:S(2)}) collective-permute-start(bf16[272,256]{1,0:T(8,128)(2,1)S(1)} %get-tuple-element.80), channel_id=1, source_target_pairs={{0,0},{4,4},{128,8},{132,12},{8,128},{12,132},{136,136},{140,140},... | collective-permute-start | bytes 417800 | tf_op jit(solution)/shard_map/ppermute | solution.py:322
  127.5 1.8 %shard_map.111 = (f32[256,384]{1,0:T(8,128)}, f32[256,384]{1,0:T(8,128)}, f32[384,256]{1,0:T(8,128)}) custom-call(s32[5]{0:T(128)S(1)} %stack.44.ids, bf16[3,256,384]{2,1,0:T(8,128)(2,1)S(1)} %get-tuple-element.82.p0, bf16[3,256,384]{2,1,0:T(8,128)(2,1)S(1)} %collective-permute-done.29.p1, bf16[3,256,384]{2,1,0:T(8,128)(2,1)S(1)} %collective-permute-done.32.p2, ...), custom_call_target="tpu_custom_call" | custom-call | bytes 2949120 | tf_op jit(solution)/shard_map/pallas_call | solution.py:52
  130.2 4.4 %collective-permute-done.31.p3 = bf16[272,256]{1,0:T(8,128)(2,1)S(1)} collective-permute-done((bf16[272,256]{1,0:T(8,128)(2,1)S(1)}, bf16[272,256]{1,0:T(8,128)(2,1)S(1)}, u32[]{:S(2)}, u32[]{:S(2)}) %collective-permute-start.31) | collective-permute-done | bytes 139296 | tf_op jit(solution)/shard_map/ppermute | solution.py:322
  (56 shorter events, 28.4 us)
Async XLA Ops:
  2.8 24.7 %collective-permute-start.8 = (bf16[3,256,384]{2,1,0:T(8,128)(2,1)S(1)}, bf16[3,256,384]{2,1,0:T(8,128)(2,1)S(1)}, u32[]{:S(2)}, u32[]{:S(2)}) collective-permute-start(bf16[3,256,384]{2,1,0:T(8,128)(2,1)S(1)} %pad_maximum_fusion.refs_4_.refs_0_), channel_id=1, source_target_pairs={{0,96},{32,0},{64,32},{96,64},{1,97},{33,1},{65,33},{97,65},{2,98}... | collective-permute-start | bytes 1769480 | tf_op jit(solution)/shard_map/ppermute | solution.py:27
  3.7 23.9 %collective-permute-start.7 = (bf16[3,256,384]{2,1,0:T(8,128)(2,1)S(1)}, bf16[3,256,384]{2,1,0:T(8,128)(2,1)S(1)}, u32[]{:S(2)}, u32[]{:S(2)}) collective-permute-start(bf16[3,256,384]{2,1,0:T(8,128)(2,1)S(1)} %pad_maximum_fusion.refs_4_.refs_0_), channel_id=1, source_target_pairs={{0,32},{32,64},{64,96},{96,0},{1,33},{33,65},{65,97},{97,1},{2,34}... | collective-permute-start | bytes 1769480 | tf_op jit(solution)/shard_map/ppermute | solution.py:27
  7.0 10.0 %collective-permute-start.3 = (bf16[2,128,256]{2,1,0:T(8,128)(2,1)S(1)}, bf16[2,128,256]{2,1,0:T(8,128)(2,1)S(1)}, u32[]{:S(2)}, u32[]{:S(2)}) collective-permute-start(bf16[2,128,256]{2,1,0:T(8,128)(2,1)S(1)} %pad_maximum_fusion.1), channel_id=1, source_target_pairs={{0,4},{4,0},{8,132},{12,128},{128,12},{132,8},{136,140},{140,136},... | collective-permute-start | bytes 393224 | tf_op jit(solution)/shard_map/ppermute | solution.py:240
  10.3 14.3 %collective-permute-start.2 = (bf16[2,128,256]{2,1,0:T(8,128)(2,1)S(1)}, bf16[2,128,256]{2,1,0:T(8,128)(2,1)S(1)}, u32[]{:S(2)}, u32[]{:S(2)}) collective-permute-start(bf16[2,128,256]{2,1,0:T(8,128)(2,1)S(1)} %pad_maximum_fusion.1), channel_id=1, source_target_pairs={{0,12},{4,8},{8,140},{12,136},{128,4},{132,0},{136,132},{140,128},... | collective-permute-start | bytes 393224 | tf_op jit(solution)/shard_map/ppermute | solution.py:240
  12.2 12.4 %collective-permute-start.1 = (bf16[2,128,256]{2,1,0:T(8,128)(2,1)S(1)}, bf16[2,128,256]{2,1,0:T(8,128)(2,1)S(1)}, u32[]{:S(2)}, u32[]{:S(2)}) collective-permute-start(bf16[2,128,256]{2,1,0:T(8,128)(2,1)S(1)} %pad_maximum_fusion.1), channel_id=1, source_target_pairs={{0,8},{4,12},{8,136},{12,140},{128,0},{132,4},{136,128},{140,132},... | collective-permute-start | bytes 393224 | tf_op jit(solution)/shard_map/ppermute | solution.py:240
  17.1 10.4 %collective-permute-start = (bf16[2,128,256]{2,1,0:T(8,128)(2,1)S(1)}, bf16[2,128,256]{2,1,0:T(8,128)(2,1)S(1)}, u32[]{:S(2)}, u32[]{:S(2)}) collective-permute-start(bf16[2,128,256]{2,1,0:T(8,128)(2,1)S(1)} %pad_maximum_fusion.1), channel_id=1, source_target_pairs={{0,0},{4,4},{8,128},{12,132},{128,8},{132,12},{136,136},{140,140},... | collective-permute-start | bytes 393224 | tf_op jit(solution)/shard_map/ppermute | solution.py:240
  27.5 13.8 %collective-permute-start.9 = (bf16[3,256,384]{2,1,0:T(8,128)(2,1)S(1)}, bf16[3,256,384]{2,1,0:T(8,128)(2,1)S(1)}, u32[]{:S(2)}, u32[]{:S(2)}) collective-permute-start(bf16[3,256,384]{2,1,0:T(8,128)(2,1)S(1)} %pad_maximum_fusion.refs_4_.refs_0_), channel_id=1, source_target_pairs={{0,64},{32,96},{64,0},{96,32},{1,65},{33,97},{65,1},{97,33},{2,66}... | collective-permute-start | bytes 1769480 | tf_op jit(solution)/shard_map/ppermute | solution.py:27
  28.2 9.8 %collective-permute-start.6 = (bf16[4,128,256]{2,1,0:T(8,128)(2,1)S(1)}, bf16[4,128,256]{2,1,0:T(8,128)(2,1)S(1)}, u32[]{:S(2)}, u32[]{:S(2)}) collective-permute-start(bf16[4,128,256]{2,1,0:T(8,128)(2,1)S(1)} %get-tuple-element.48.refs_0_), channel_id=1, source_target_pairs={{0,2},{1,3},{2,0},{3,1},{4,6},{5,7},{6,4},{7,5},{8,10},{9,11},{10,... | collective-permute-start | bytes 786440 | tf_op jit(solution)/shard_map/ppermute | solution.py:27
  28.8 11.0 %collective-permute-start.5 = (bf16[4,128,256]{2,1,0:T(8,128)(2,1)S(1)}, bf16[4,128,256]{2,1,0:T(8,128)(2,1)S(1)}, u32[]{:S(2)}, u32[]{:S(2)}) collective-permute-start(bf16[4,128,256]{2,1,0:T(8,128)(2,1)S(1)} %get-tuple-element.48.refs_0_), channel_id=1, source_target_pairs={{0,3},{1,0},{2,1},{3,2},{4,7},{5,4},{6,5},{7,6},{8,11},{9,8},{10,9... | collective-permute-start | bytes 786440 | tf_op jit(solution)/shard_map/ppermute | solution.py:27
  31.0 9.7 %collective-permute-start.4 = (bf16[4,128,256]{2,1,0:T(8,128)(2,1)S(1)}, bf16[4,128,256]{2,1,0:T(8,128)(2,1)S(1)}, u32[]{:S(2)}, u32[]{:S(2)}) collective-permute-start(bf16[4,128,256]{2,1,0:T(8,128)(2,1)S(1)} %get-tuple-element.48.refs_0_), channel_id=1, source_target_pairs={{0,1},{1,2},{2,3},{3,0},{4,5},{5,6},{6,7},{7,4},{8,9},{9,10},{10,1... | collective-permute-start | bytes 786440 | tf_op jit(solution)/shard_map/ppermute | solution.py:27
  31.0 10.3 %collective-permute-start.10 = (bf16[3,256,384]{2,1,0:T(8,128)(2,1)S(1)}, bf16[3,256,384]{2,1,0:T(8,128)(2,1)S(1)}, u32[]{:S(2)}, u32[]{:S(2)}) collective-permute-start(bf16[3,256,384]{2,1,0:T(8,128)(2,1)S(1)} %pad_maximum_fusion.refs_4_.refs_0_), channel_id=1, source_target_pairs={{0,16},{16,0},{1,17},{17,1},{2,18},{18,2},{3,19},{19,3},{4,20},{20... | collective-permute-start | bytes 1769480 | tf_op jit(solution)/shard_map/ppermute | solution.py:31
  38.0 3.3 %collective-permute-start.11 = (bf16[3,256,384]{2,1,0:T(8,128)(2,1)S(1)}, bf16[3,256,384]{2,1,0:T(8,128)(2,1)S(1)}, u32[]{:S(2)}, u32[]{:S(2)}) collective-permute-start(bf16[3,256,384]{2,1,0:T(8,128)(2,1)S(1)} %collective-permute-done.7.refs_5_.refs_1_), channel_id=1, source_target_pairs={{0,16},{16,0},{1,17},{17,1},{2,18},{18,2},{3,19},{19,3},{4,20},{20... | collective-permute-start | bytes 1769480 | tf_op jit(solution)/shard_map/ppermute | solution.py:31
  39.8 2.0 %collective-permute-start.13 = (bf16[3,256,384]{2,1,0:T(8,128)(2,1)S(1)}, bf16[3,256,384]{2,1,0:T(8,128)(2,1)S(1)}, u32[]{:S(2)}, u32[]{:S(2)}) collective-permute-start(bf16[3,256,384]{2,1,0:T(8,128)(2,1)S(1)} %collective-permute-done.8.refs_7_.refs_3_), channel_id=1, source_target_pairs={{0,16},{16,0},{1,17},{17,1},{2,18},{18,2},{3,19},{19,3},{4,20},{20... | collective-permute-start | bytes 1769480 | tf_op jit(solution)/shard_map/ppermute | solution.py:31
  45.3 24.9 %collective-permute-start.17 = (bf16[272,768]{1,0:T(8,128)(2,1)S(1)}, bf16[272,768]{1,0:T(8,128)(2,1)S(1)}, u32[]{:S(2)}, u32[]{:S(2)}) collective-permute-start(bf16[272,768]{1,0:T(8,128)(2,1)S(1)} %get-tuple-element.57.mine), channel_id=1, source_target_pairs={{0,128},{128,0},{1,129},{129,1},{2,130},{130,2},{3,131},{131,3},{4... | collective-permute-start | bytes 1253384 | tf_op jit(solution)/shard_map/ppermute | solution.py:31
  45.4 10.8 %collective-permute-start.16 = (bf16[4,128,256]{2,1,0:T(8,128)(2,1)S(1)}, bf16[4,128,256]{2,1,0:T(8,128)(2,1)S(1)}, u32[]{:S(2)}, u32[]{:S(2)}) collective-permute-start(bf16[4,128,256]{2,1,0:T(8,128)(2,1)S(1)} %get-tuple-element.55.refs_0_), channel_id=1, source_target_pairs={{0,2},{1,3},{2,0},{3,1},{4,6},{5,7},{6,4},{7,5},{8,10},{9,11},{10,... | collective-permute-start | bytes 786440 | tf_op jit(solution)/shard_map/ppermute | solution.py:27
  46.5 13.7 %collective-permute-start.15 = (bf16[4,128,256]{2,1,0:T(8,128)(2,1)S(1)}, bf16[4,128,256]{2,1,0:T(8,128)(2,1)S(1)}, u32[]{:S(2)}, u32[]{:S(2)}) collective-permute-start(bf16[4,128,256]{2,1,0:T(8,128)(2,1)S(1)} %get-tuple-element.55.refs_0_), channel_id=1, source_target_pairs={{0,3},{1,0},{2,1},{3,2},{4,7},{5,4},{6,5},{7,6},{8,11},{9,8},{10,9... | collective-permute-start | bytes 786440 | tf_op jit(solution)/shard_map/ppermute | solution.py:27
  48.4 12.5 %collective-permute-start.14 = (bf16[4,128,256]{2,1,0:T(8,128)(2,1)S(1)}, bf16[4,128,256]{2,1,0:T(8,128)(2,1)S(1)}, u32[]{:S(2)}, u32[]{:S(2)}) collective-permute-start(bf16[4,128,256]{2,1,0:T(8,128)(2,1)S(1)} %get-tuple-element.55.refs_0_), channel_id=1, source_target_pairs={{0,1},{1,2},{2,3},{3,0},{4,5},{5,6},{6,7},{7,4},{8,9},{9,10},{10,1... | collective-permute-start | bytes 786440 | tf_op jit(solution)/shard_map/ppermute | solution.py:27
  62.2 14.5 %collective-permute-start.21 = (bf16[256,384]{1,0:T(8,128)(2,1)S(1)}, bf16[256,384]{1,0:T(8,128)(2,1)S(1)}, u32[]{:S(2)}, u32[]{:S(2)}) collective-permute-start(bf16[256,384]{1,0:T(8,128)(2,1)S(1)} %get-tuple-element.56.d_mine), channel_id=1, source_target_pairs={{0,128},{128,0},{1,129},{129,1},{2,130},{130,2},{3,131},{131,3},{4... | collective-permute-start | bytes 589832 | tf_op jit(solution)/shard_map/ppermute | solution.py:31
  71.8 10.2 %collective-permute-start.18 = (bf16[4,128,256]{2,1,0:T(8,128)(2,1)S(1)}, bf16[4,128,256]{2,1,0:T(8,128)(2,1)S(1)}, u32[]{:S(2)}, u32[]{:S(2)}) collective-permute-start(bf16[4,128,256]{2,1,0:T(8,128)(2,1)S(1)} %get-tuple-element.59), channel_id=1, source_target_pairs={{0,2},{1,3},{2,0},{3,1},{4,6},{5,7},{6,4},{7,5},{8,10},{9,11},{10,... | collective-permute-start | bytes 786440 | tf_op jit(solution)/shard_map/ppermute | solution.py:27
  72.8 11.2 %collective-permute-start.19 = (bf16[4,128,256]{2,1,0:T(8,128)(2,1)S(1)}, bf16[4,128,256]{2,1,0:T(8,128)(2,1)S(1)}, u32[]{:S(2)}, u32[]{:S(2)}) collective-permute-start(bf16[4,128,256]{2,1,0:T(8,128)(2,1)S(1)} %get-tuple-element.60), channel_id=1, source_target_pairs={{0,3},{1,0},{2,1},{3,2},{4,7},{5,4},{6,5},{7,6},{8,11},{9,8},{10,9... | collective-permute-start | bytes 786440 | tf_op jit(solution)/shard_map/ppermute | solution.py:27
  74.8 9.9 %collective-permute-start.20 = (bf16[4,128,256]{2,1,0:T(8,128)(2,1)S(1)}, bf16[4,128,256]{2,1,0:T(8,128)(2,1)S(1)}, u32[]{:S(2)}, u32[]{:S(2)}) collective-permute-start(bf16[4,128,256]{2,1,0:T(8,128)(2,1)S(1)} %get-tuple-element.61), channel_id=1, source_target_pairs={{0,1},{1,2},{2,3},{3,0},{4,5},{5,6},{6,7},{7,4},{8,9},{9,10},{10,1... | collective-permute-start | bytes 786440 | tf_op jit(solution)/shard_map/ppermute | solution.py:27
  87.1 4.6 %collective-permute-start.28 = (bf16[3,4,256,384]{3,2,1,0:T(8,128)(2,1)S(1)}, bf16[3,4,256,384]{3,2,1,0:T(8,128)(2,1)S(1)}, u32[]{:S(2)}, u32[]{:S(2)}) collective-permute-start(bf16[3,4,256,384]{3,2,1,0:T(8,128)(2,1)S(1)} %get-tuple-element.77), channel_id=1, source_target_pairs={{0,16},{16,0},{1,17},{17,1},{2,18},{18,2},{3,19},{19,3},{4,20},{20... | collective-permute-start | bytes 7077896 | tf_op jit(solution)/shard_map/ppermute | solution.py:31
  87.2 11.4 %collective-permute-start.22 = (bf16[4,144,256]{2,1,0:T(8,128)(2,1)S(1)}, bf16[4,144,256]{2,1,0:T(8,128)(2,1)S(1)}, u32[]{:S(2)}, u32[]{:S(2)}) collective-permute-start(bf16[4,144,256]{2,1,0:T(8,128)(2,1)S(1)} %get-tuple-element.65), channel_id=1, source_target_pairs={{0,2},{1,3},{2,0},{3,1},{4,6},{5,7},{6,4},{7,5},{8,10},{9,11},{10,... | collective-permute-start | bytes 884744 | tf_op jit(solution)/shard_map/ppermute | solution.py:27
  88.5 15.3 %collective-permute-start.23 = (bf16[4,144,256]{2,1,0:T(8,128)(2,1)S(1)}, bf16[4,144,256]{2,1,0:T(8,128)(2,1)S(1)}, u32[]{:S(2)}, u32[]{:S(2)}) collective-permute-start(bf16[4,144,256]{2,1,0:T(8,128)(2,1)S(1)} %get-tuple-element.66), channel_id=1, source_target_pairs={{0,3},{1,0},{2,1},{3,2},{4,7},{5,4},{6,5},{7,6},{8,11},{9,8},{10,9... | collective-permute-start | bytes 884744 | tf_op jit(solution)/shard_map/ppermute | solution.py:27
  90.1 14.3 %collective-permute-start.24 = (bf16[4,144,256]{2,1,0:T(8,128)(2,1)S(1)}, bf16[4,144,256]{2,1,0:T(8,128)(2,1)S(1)}, u32[]{:S(2)}, u32[]{:S(2)}) collective-permute-start(bf16[4,144,256]{2,1,0:T(8,128)(2,1)S(1)} %get-tuple-element.67), channel_id=1, source_target_pairs={{0,1},{1,2},{2,3},{3,0},{4,5},{5,6},{6,7},{7,4},{8,9},{9,10},{10,1... | collective-permute-start | bytes 884744 | tf_op jit(solution)/shard_map/ppermute | solution.py:27
  92.8 29.3 %collective-permute-start.29 = (bf16[3,256,384]{2,1,0:T(8,128)(2,1)S(1)}, bf16[3,256,384]{2,1,0:T(8,128)(2,1)S(1)}, u32[]{:S(2)}, u32[]{:S(2)}) collective-permute-start(bf16[3,256,384]{2,1,0:T(8,128)(2,1)S(1)} %get-tuple-element.78), channel_id=1, source_target_pairs={{0,96},{32,0},{64,32},{96,64},{1,97},{33,1},{65,33},{97,65},{2,98}... | collective-permute-start | bytes 1769480 | tf_op jit(solution)/shard_map/ppermute | solution.py:27
  93.1 32.5 %collective-permute-start.30 = (bf16[3,256,384]{2,1,0:T(8,128)(2,1)S(1)}, bf16[3,256,384]{2,1,0:T(8,128)(2,1)S(1)}, u32[]{:S(2)}, u32[]{:S(2)}) collective-permute-start(bf16[3,256,384]{2,1,0:T(8,128)(2,1)S(1)} %get-tuple-element.79), channel_id=1, source_target_pairs={{0,32},{32,64},{64,96},{96,0},{1,33},{33,65},{65,97},{97,1},{2,34}... | collective-permute-start | bytes 1769480 | tf_op jit(solution)/shard_map/ppermute | solution.py:27
  105.1 22.3 %collective-permute-start.32 = (bf16[3,256,384]{2,1,0:T(8,128)(2,1)S(1)}, bf16[3,256,384]{2,1,0:T(8,128)(2,1)S(1)}, u32[]{:S(2)}, u32[]{:S(2)}) collective-permute-start(bf16[3,256,384]{2,1,0:T(8,128)(2,1)S(1)} %get-tuple-element.84), channel_id=1, source_target_pairs={{0,64},{32,96},{64,0},{96,32},{1,65},{33,97},{65,1},{97,33},{2,66}... | collective-permute-start | bytes 1769480 | tf_op jit(solution)/shard_map/ppermute | solution.py:27
  107.8 22.3 %collective-permute-start.27 = (bf16[272,256]{1,0:T(8,128)(2,1)S(1)}, bf16[272,256]{1,0:T(8,128)(2,1)S(1)}, u32[]{:S(2)}, u32[]{:S(2)}) collective-permute-start(bf16[272,256]{1,0:T(8,128)(2,1)S(1)} %get-tuple-element.70), channel_id=1, source_target_pairs={{8,0},{12,4},{136,8},{140,12},{0,128},{4,132},{128,136},{132,140},... | collective-permute-start | bytes 417800 | tf_op jit(solution)/shard_map/ppermute | solution.py:322
  110.4 18.8 %collective-permute-start.25 = (bf16[272,256]{1,0:T(8,128)(2,1)S(1)}, bf16[272,256]{1,0:T(8,128)(2,1)S(1)}, u32[]{:S(2)}, u32[]{:S(2)}) collective-permute-start(bf16[272,256]{1,0:T(8,128)(2,1)S(1)} %get-tuple-element.68), channel_id=1, source_target_pairs={{4,0},{0,4},{132,8},{128,12},{12,128},{8,132},{140,136},{136,140},... | collective-permute-start | bytes 417800 | tf_op jit(solution)/shard_map/ppermute | solution.py:322
  122.1 8.1 %collective-permute-start.26 = (bf16[272,256]{1,0:T(8,128)(2,1)S(1)}, bf16[272,256]{1,0:T(8,128)(2,1)S(1)}, u32[]{:S(2)}, u32[]{:S(2)}) collective-permute-start(bf16[272,256]{1,0:T(8,128)(2,1)S(1)} %get-tuple-element.69), channel_id=1, source_target_pairs={{12,0},{8,4},{140,8},{136,12},{4,128},{0,132},{132,136},{128,140},... | collective-permute-start | bytes 417800 | tf_op jit(solution)/shard_map/ppermute | solution.py:322
  125.6 9.0 %collective-permute-start.31 = (bf16[272,256]{1,0:T(8,128)(2,1)S(1)}, bf16[272,256]{1,0:T(8,128)(2,1)S(1)}, u32[]{:S(2)}, u32[]{:S(2)}) collective-permute-start(bf16[272,256]{1,0:T(8,128)(2,1)S(1)} %get-tuple-element.80), channel_id=1, source_target_pairs={{0,0},{4,4},{128,8},{132,12},{8,128},{12,132},{136,136},{140,140},... | collective-permute-start | bytes 417800 | tf_op jit(solution)/shard_map/ppermute | solution.py:322
  (4 other events, 103.7 us)
